TPU v7x, 256 devices: a whole 4x4x8 slice. The times are simulated.
256 devices in a mesh: dp: 2 (over x_lo), row: 8 (over y, x_hi), col: 16 (over z, core).
Axes of the slice: x: 4 (x_hi: 2, x_lo: 2; x = x_hi * 2 + x_lo), y: 4, z: 8, core: 2. Of those that a mesh axis runs over, the one named last changes fastest.
Arguments:
- small_w: bfloat16 [4096, 4096], P('col', 'row'), may hold values from -0.09375 to 0.09375
- grow_a: bfloat16 [8192, 4096], P('row', 'col'), may hold values from -0.09375 to 0.09375
- grow_b: bfloat16 [8192, 4096], P('col', 'row'), may hold values from -0.09375 to 0.09375
- inputs: bfloat16 [1024, 8192], P('dp', 'col'), may hold values from -6 to 6
- cotangent: bfloat16 [1024, 8192], P('dp', 'row'), may hold values from -0.1875 to 0.1875
Outputs:
- outputs: bfloat16 [1024, 8192], P(('dp', 'col'), 'row')
- big_weight: bfloat16 [8192, 8192], P('row', 'col')
- grad_weight: bfloat16 [8192, 8192], P('row', 'col')
- grad_a: float32 [8192, 4096], P('row', ('dp', 'col'))
- grad_b: float32 [8192, 4096], P('col', ('dp', 'row'))
All inputs are finite; a program needn't handle non-finite values.
Results may differ from a plain program's by a relative error of at most 0.035.
Values may be sent and summed in bfloat16 or wider, within the bound.
No kernel may reach another device: no remote copies, remote signals or barrier semaphores. Data moves between devices by JAX's collectives and lax.ppermute only.
A program may use at most 64 MiB of HBM per device.

v0:
```python
import jax
import jax.numpy as jnp
from jax import lax
from jax.sharding import PartitionSpec as P


def contract(first_op, second_op, first_dim, second_dim):
    return lax.dot_general(
        first_op,
        second_op,
        (((first_dim,), (second_dim,)), ((), ())),
        preferred_element_type=jnp.float32,
    )


def body(small_w, grow_a, grow_b, inputs, cotangent):
    col_count = lax.axis_size("col")
    portion = small_w.shape[0] * col_count // lax.axis_size("dp")
    offset = lax.axis_index("dp") * portion
    w_by_rows = lax.all_gather(small_w, "row", axis=1, tiled=True)
    w_by_cols = lax.all_gather(small_w, "col", axis=0, tiled=True)
    rows_half = lax.dynamic_slice_in_dim(w_by_rows, offset, portion, 1)
    cols_half = lax.dynamic_slice_in_dim(w_by_cols, offset, portion, 0)
    picked = rows_half
    proj_piece = lax.psum_scatter(
        contract(picked, grow_a, 0, 1).astype(jnp.bfloat16), "col", scatter_dimension=0, tiled=True
    )
    proj_half = lax.all_gather(proj_piece, "col", axis=0, tiled=True)
    picked = cols_half
    map_piece = lax.psum_scatter(
        contract(picked, grow_b, 1, 1).astype(jnp.bfloat16), "row", scatter_dimension=0, tiled=True
    )
    map_half = lax.all_gather(map_piece, "row", axis=0, tiled=True)
    b_full = lax.all_gather(grow_b, "row", axis=1, tiled=True)
    b_half = lax.dynamic_slice_in_dim(b_full, offset, portion, 1)
    weight_term = contract(proj_half, b_half, 0, 1)
    grad_term = contract(cotangent, inputs, 0, 0)
    weight_sum, grad_sum = (
        lax.psum(weight_term.astype(jnp.bfloat16), "dp").astype(jnp.float32),
        lax.psum(grad_term.astype(jnp.bfloat16), "dp").astype(jnp.float32),
    )
    big_weight = weight_sum.astype(jnp.bfloat16)
    grad_weight = grad_sum.astype(jnp.bfloat16)
    picked = inputs
    outputs = lax.psum_scatter(
        contract(picked, big_weight, 1, 1).astype(jnp.bfloat16),
        "col",
        scatter_dimension=0,
        tiled=True,
    )
    picked = map_half
    grad_a = lax.psum_scatter(
        contract(picked, grad_weight, 1, 1).astype(jnp.bfloat16),
        "col",
        scatter_dimension=0,
        tiled=True,
    ).astype(jnp.float32)
    picked = proj_half
    grad_b = lax.psum_scatter(
        contract(picked, grad_weight, 1, 0).astype(jnp.bfloat16),
        "row",
        scatter_dimension=0,
        tiled=True,
    ).astype(jnp.float32)
    return (outputs, big_weight, grad_weight, grad_a.T, grad_b.T)


def solution(mesh):
    return jax.shard_map(
        body,
        mesh=mesh,
        in_specs=(
            P("col", "row"),
            P("row", "col"),
            P("col", "row"),
            P("dp", "col"),
            P("dp", "row"),
        ),
        out_specs=(
            P(("dp", "col"), "row"),
            P("row", "col"),
            P("row", "col"),
            P("row", ("dp", "col")),
            P("col", ("dp", "row")),
        ),
        check_vma=False,
    )
```

profile of v0, /device:TPU:1, one launch (start us, length us, event | category | flops | bytes accessed | tf_op | source)
XLA Modules:
  0.0 738.1 jit_solution(2826842288235354585)
XLA Ops:
  7.2 0.0 all-gather.6.cloned.1.call-start
  7.2 0.7 all-gather.6.cloned.1.call-update
  7.9 0.0 reduce-scatter.8.cloned.1.call-start
  8.0 65.4 %all-gather.6.cloned.1.call-done = bf16[256,4096]{1,0:T(8,128)(2,1)} async-done(((bf16[256,512]{1,0:T(8,128)(2,1)}), bf16[256,4096]{1,0:T(8,128)(2,1)}) %all-gather.6.cloned.1.call-update) | async-done | bytes 2097168 | tf_op jit(solution)/shard_map/all_gather | solution.py:20
  73.4 4.6 convolution_convert_fusion.1
  78.0 0.0 reduce-scatter.8.cloned.1.call-update
  78.0 0.0 all-gather.12.cloned.1.call-start
  78.1 0.7 all-gather.12.cloned.1.call-update
  78.7 0.0 all-gather.10.cloned.1.call-start
  78.8 0.5 all-gather.10.cloned.1.call-update
  79.3 0.0 all-gather.8.cloned.1.call-start
  79.4 56.9 %reduce-scatter.8.cloned.1.call-done = bf16[128,1024]{1,0:T(8,128)(2,1)} async-done(((bf16[2048,1024]{1,0:T(8,128)(2,1)}), bf16[128,1024]{1,0:T(8,128)(2,1)}) %reduce-scatter.8.cloned.1.call-update) | async-done | bytes 262160 | tf_op jit(solution)/shard_map/reduce_scatter | solution.py:25
  136.3 0.0 all-gather.8.cloned.1.call-update
  136.3 0.0 reduce-scatter.10.cloned.1.call-start
  136.3 45.7 %all-gather.12.cloned.1.call-done = bf16[4096,512]{1,0:T(8,128)(2,1)} async-done(((bf16[256,512]{1,0:T(8,128)(2,1)}), bf16[4096,512]{1,0:T(8,128)(2,1)}) %all-gather.12.cloned.1.call-update) | async-done | bytes 4194320 | tf_op jit(solution)/shard_map/all_gather | solution.py:21
  182.1 4.2 convolution_convert_fusion.3
  186.3 0.0 reduce-scatter.10.cloned.1.call-update
  186.3 0.0 all-reduce.3.cloned.1.call-start
  186.4 1.7 convolution_convert_fusion.4
  188.1 72.8 %all-gather.10.cloned.1.call-done = bf16[512,4096]{1,0:T(8,128)(2,1)} async-done(((bf16[512,512]{1,0:T(8,128)(2,1)}), bf16[512,4096]{1,0:T(8,128)(2,1)}) %all-gather.10.cloned.1.call-update) | async-done | bytes 4194320 | tf_op jit(solution)/shard_map/all_gather | solution.py:34
  260.9 42.6 %all-gather.8.cloned.1.call-done = bf16[2048,1024]{1,0:T(8,128)(2,1)} async-done(((bf16[128,1024]{1,0:T(8,128)(2,1)}), bf16[2048,1024]{1,0:T(8,128)(2,1)}) %all-gather.8.cloned.1.call-update) | async-done | bytes 4194320 | tf_op jit(solution)/shard_map/all_gather | solution.py:28
  303.5 6.2 fusion.3
  309.7 0.0 all-reduce.3.cloned.1.call-update
  309.7 0.0 all-gather.14.cloned.1.call-start
  309.8 74.3 %reduce-scatter.10.cloned.1.call-done = bf16[256,512]{1,0:T(8,128)(2,1)} async-done(((bf16[2048,512]{1,0:T(8,128)(2,1)}), bf16[256,512]{1,0:T(8,128)(2,1)}) %reduce-scatter.10.cloned.1.call-update) | async-done | bytes 262160 | tf_op jit(solution)/shard_map/reduce_scatter | solution.py:30
  384.1 0.0 all-gather.14.cloned.1.call-update
  384.1 0.0 reduce-scatter.14.cloned.1.call-start
  384.2 78.3 %all-reduce.3.cloned.1.call-done = (bf16[1024,512]{1,0:T(8,128)(2,1)}, bf16[1024,512]{1,0:T(8,128)(2,1)}) async-done(((bf16[1024,512]{1,0:T(8,128)(2,1)}, bf16[1024,512]{1,0:T(8,128)(2,1)}), (bf16[1024,512]{1,0:T(8,128)(2,1)}, bf16[1024,512]{1,0:T(8,128)(2,1)})) %all-reduce.3.cloned.1.call-update) | async-done | bytes 2097168 | tf_op jit(solution)/shard_map/psum | solution.py:39
  462.5 6.3 convolution_convert_fusion.2
  468.7 0.0 reduce-scatter.14.cloned.1.call-update
  468.8 0.0 reduce-scatter.12.cloned.1.call-start
  468.8 56.3 %all-gather.14.cloned.1.call-done = bf16[2048,512]{1,0:T(8,128)(2,1)} async-done(((bf16[256,512]{1,0:T(8,128)(2,1)}), bf16[2048,512]{1,0:T(8,128)(2,1)}) %all-gather.14.cloned.1.call-update) | async-done | bytes 2097168 | tf_op jit(solution)/shard_map/all_gather | solution.py:33
  525.1 5.9 convolution_convert_fusion
  531.0 0.0 reduce-scatter.12.cloned.1.call-update
  531.0 0.0 reduce-scatter.16.cloned.1.call-start
  531.1 1.1 copy-done.2
  532.2 2.7 fusion.6
  535.0 2.3 copy.16
  537.3 0.0 reduce-scatter.16.cloned.1.call-update
  537.3 69.3 %reduce-scatter.14.cloned.1.call-done = bf16[256,512]{1,0:T(8,128)(2,1)} async-done(((bf16[2048,512]{1,0:T(8,128)(2,1)}), bf16[256,512]{1,0:T(8,128)(2,1)}) %reduce-scatter.14.cloned.1.call-update) | async-done | bytes 262160 | tf_op jit(solution)/shard_map/reduce_scatter | solution.py:59
  606.6 1.0 convert_bitcast_fusion
  607.6 1.0 copy.15
  608.6 60.6 %reduce-scatter.12.cloned.1.call-done = bf16[128,1024]{1,0:T(8,128)(2,1)} async-done(((bf16[2048,1024]{1,0:T(8,128)(2,1)}), bf16[128,1024]{1,0:T(8,128)(2,1)}) %reduce-scatter.12.cloned.1.call-update) | async-done | bytes 262160 | tf_op jit(solution)/shard_map/reduce_scatter | solution.py:52
  669.2 1.0 convert_bitcast_fusion.1
  670.2 1.0 copy.14
  671.2 57.2 %reduce-scatter.16.cloned.1.call-done = bf16[32,1024]{1,0:T(8,128)(2,1)} async-done(((bf16[512,1024]{1,0:T(8,128)(2,1)}), bf16[32,1024]{1,0:T(8,128)(2,1)}) %reduce-scatter.16.cloned.1.call-update) | async-done | bytes 65552
  728.4 2.3 copy.20
  730.6 1.0 copy.21
  (9 shorter events, 0.0 us)
Async XLA Ops:
  7.2 179.2 %copy-start = (bf16[512,1024]{1,0:T(8,128)(2,1)S(1)}, bf16[512,1024]{1,0:T(8,128)(2,1)}, u32[]{:S(2)}) copy-start(bf16[512,1024]{1,0:T(8,128)(2,1)} %param.9) | copy-start | bytes 3145732
  7.2 66.2 %all-gather.6.cloned.1.call-start = ((), (), s32[]{:S(2)}) async-start(), calls=%async_computation.5 | async-start | bytes 2359296 | tf_op jit(solution)/shard_map/all_gather | solution.py:20
  7.9 128.3 %reduce-scatter.8.cloned.1.call-start = ((), (), s32[]{:S(2)}) async-start(), calls=%async_computation.6 | async-start | bytes 4456448 | tf_op jit(solution)/shard_map/reduce_scatter | solution.py:25
  78.0 104.1 %copy-start.3 = (bf16[512,512]{1,0:T(8,128)(2,1)S(1)}, bf16[512,512]{1,0:T(8,128)(2,1)}, u32[]{:S(2)}) copy-start(bf16[512,512]{1,0:T(8,128)(2,1)} %param.7) | copy-start | bytes 1572868
  78.0 104.1 %all-gather.12.cloned.1.call-start = ((), (), s32[]{:S(2)}) async-start(), calls=%async_computation.9 | async-start | bytes 4456448 | tf_op jit(solution)/shard_map/all_gather | solution.py:21
  78.7 182.1 %all-gather.10.cloned.1.call-start = ((), (), s32[]{:S(2)}) async-start(), calls=%async_computation.8 | async-start | bytes 4718592 | tf_op jit(solution)/shard_map/all_gather | solution.py:34
  79.3 224.2 %all-gather.8.cloned.1.call-start = ((), (), s32[]{:S(2)}) async-start(), calls=%async_computation.7 | async-start | bytes 4456448 | tf_op jit(solution)/shard_map/all_gather | solution.py:28
  136.3 50.1 %copy-start.4 = (bf16[512,512]{1,0:T(8,128)(2,1)S(1)}, bf16[512,512]{1,0:T(8,128)(2,1)}, u32[]{:S(2)}) copy-start(bf16[512,512]{1,0:T(8,128)(2,1)} %param.8) | copy-start | bytes 1572868
  136.3 247.8 %reduce-scatter.10.cloned.1.call-start = ((), (), s32[]{:S(2)}) async-start(), calls=%async_computation.10 | async-start | bytes 2359296 | tf_op jit(solution)/shard_map/reduce_scatter | solution.py:30
  186.3 276.2 %all-reduce.3.cloned.1.call-start = ((), (), s32[]{:S(2)}) async-start(), calls=%async_computation.15 | async-start | bytes 4194304 | tf_op jit(solution)/shard_map/psum | solution.py:39
  309.7 215.4 %all-gather.14.cloned.1.call-start = ((), (), s32[]{:S(2)}) async-start(), calls=%async_computation.11 | async-start | bytes 2359296 | tf_op jit(solution)/shard_map/all_gather | solution.py:33
  384.1 222.4 %reduce-scatter.14.cloned.1.call-start = ((), (), s32[]{:S(2)}) async-start(), calls=%async_computation.13 | async-start | bytes 2359296 | tf_op jit(solution)/shard_map/reduce_scatter | solution.py:59
  462.5 62.6 %copy-start.1 = (bf16[1024,512]{1,0:T(8,128)(2,1)S(1)}, bf16[1024,512]{1,0:T(8,128)(2,1)}, u32[]{:S(2)}) copy-start(bf16[1024,512]{1,0:T(8,128)(2,1)} %get-tuple-element.19) | copy-start | bytes 3145732
  468.8 200.4 %reduce-scatter.12.cloned.1.call-start = ((), (), s32[]{:S(2)}) async-start(), calls=%async_computation.12 | async-start | bytes 4456448 | tf_op jit(solution)/shard_map/reduce_scatter | solution.py:52
  531.0 1.2 copy-start.2
  531.0 197.3 %reduce-scatter.16.cloned.1.call-start = ((), (), s32[]{:S(2)}) async-start(), calls=%async_computation.14 | async-start | bytes 1114112
Sparse Core Ops, SparseCore 0:
  10.5 62.8 all-gather.5
  78.1 58.0 reduce-scatter.7
  138.1 43.9 all-gather.11
  184.4 76.4 all-gather.9
  262.6 40.8 all-gather.7
  307.4 76.6 reduce-scatter.9
  387.3 75.1 all-reduce.2
  465.5 59.5 all-gather.13
  529.6 76.8 reduce-scatter.13
  609.1 60.0 reduce-scatter.11
  672.4 55.8 reduce-scatter.15
where the time goes:
time: 741 us; the launch traced here: 738 us
  waiting for transfers between devices  681 us (92%)
  matrix products  31.7 us (4%)
  between operations  13.9 us (2%)
  local copies, waits for them, and re-layouts  8.66 us (1%)
    psum x1, waiting for transfers between devices, body(): lax.psum(weight_term.astype(jnp.bfloat16), 'dp').astype(jnp.float32)  78.3 us
    reduce_scatter x1, waiting for transfers between devices, body(): lax.psum_scatter(contract(picked, grow_b, 1, 1).astype(jnp.bfloat16), 'ro...  74.3 us
    all_gather x1, waiting for transfers between devices, body(): b_full = lax.all_gather(grow_b, 'row', axis=1, tiled=True)  72.8 us
    reduce_scatter x1, waiting for transfers between devices, body(): lax.psum_scatter(contract(picked, grad_weight, 1, 0).astype(jnp.bfloat16)...  69.3 us
    all_gather x1, waiting for transfers between devices, body(): w_by_rows = lax.all_gather(small_w, 'row', axis=1, tiled=True)  65.4 us
    reduce_scatter x1, waiting for transfers between devices, body(): lax.psum_scatter(contract(picked, grad_weight, 1, 1).astype(jnp.bfloat16)...  60.6 us
    unnamed x12, waiting for transfers between devices  59.2 us
    reduce_scatter x1, waiting for transfers between devices, body(): lax.psum_scatter(contract(picked, grow_a, 0, 1).astype(jnp.bfloat16), 'co...  56.9 us
  transfers between devices with their start and end apart: 11, of which 11 were waited for; matrix products, arithmetic and copies ran while one was open for 5% of the time, Pallas kernels for 0%

commit v1 on v0

v1 whole, which is shorter than its diff:
```python
import jax
import jax.numpy as jnp
from jax import lax
from jax.sharding import PartitionSpec as P

BF = jnp.bfloat16
F32 = jnp.float32


def dot(a, b, da, db):
    return lax.dot_general(
        a, b, (((da,), (db,)), ((), ())), preferred_element_type=F32
    )


def rows(x, start, size):
    return lax.dynamic_slice_in_dim(x, start, size, 0)


def total(a, b):
    return (a.astype(F32) + b.astype(F32)).astype(BF)


def body(small_w, grow_a, grow_b, inputs, cotangent):
    n_dp, n_row, n_col = (lax.axis_size(a) for a in ("dp", "row", "col"))
    d, c = lax.axis_index("dp"), lax.axis_index("col")
    core_id = c % 2
    n_z = n_col // 2
    z_rings = [[2 * z + i for z in range(n_z)] for i in range(2)]

    def permute(x, axis, size, target):
        return lax.ppermute(x, axis, [(i, target(i)) for i in range(size)])

    def core(x):
        return permute(x, "col", n_col, lambda i: i ^ 1)

    def other_dp(x):
        return permute(x, "dp", n_dp, lambda i: i ^ 1)

    def exchange(x, axis):
        return lax.all_to_all(x, axis, 0, 0, tiled=True)

    def z_gather(x):
        return lax.all_gather(x, "col", axis=0, tiled=True, axis_index_groups=z_rings)

    def by_dp(own, other, axis):
        first = jnp.where(d == 0, own, other)
        second = jnp.where(d == 0, other, own)
        return jnp.stack([first, second], axis)

    n_w = small_w.shape[0] // 2
    w_own = z_gather(rows(small_w, d * n_w, n_w))
    w_other = core(w_own)

    tok = inputs.shape[0] // n_col
    x_other, c_other = other_dp(inputs), other_dp(cotangent)
    x_all = by_dp(
        inputs.reshape(n_col, tok, -1), x_other.reshape(n_col, tok, -1), 1
    ).reshape(n_dp * n_col * tok, -1)
    c_all = by_dp(
        cotangent.reshape(n_col, tok, -1), c_other.reshape(n_col, tok, -1), 1
    ).reshape(n_dp * n_col * tok, -1)

    u_part = dot(inputs, grow_b, 1, 0).astype(BF)
    q_part = dot(cotangent, grow_a, 1, 0).astype(BF)
    n_u = u_part.shape[1]
    got = exchange(jnp.concatenate([u_part, q_part], 1), "col").reshape(n_col, tok, -1)
    u_mine = got[:, :, :n_u].astype(F32).sum(0).astype(BF)
    q_got = got[:, :, n_u:]
    q_low, q_high = q_got[:, :, :n_w], q_got[:, :, n_w:]
    q_keep = jnp.where(d == 0, q_low, q_high)
    q_send = jnp.where(d == 0, q_high, q_low)
    u = by_dp(u_mine, other_dp(u_mine), 0).reshape(n_dp * tok, n_u)
    q = by_dp(q_keep, other_dp(q_send), 0)
    q = q.reshape(n_dp, n_z, 2, tok, n_w)
    q = jnp.where(core_id == 0, q, q[:, :, ::-1])
    q = q.transpose(0, 3, 2, 1, 4).reshape(n_dp * tok, n_col * n_w)

    w_all = jnp.concatenate([w_own, w_other], 0)
    width = w_all.shape[0]
    n_m = grow_b.shape[0] // n_row
    n_t = n_dp * tok // n_row
    left = jnp.concatenate(
        [grow_b.reshape(n_row, n_m, -1), u.reshape(n_row, n_t, -1)], 1
    ).reshape(n_row * (n_m + n_t), -1)
    part = dot(left, w_all, 1, 1).astype(BF).reshape(n_row, n_m + n_t, width)
    part = jnp.concatenate([part, q.reshape(n_row, n_t, width)], 1)
    got = exchange(part.reshape(-1, width), "row").reshape(n_row, -1, width)
    got = got.astype(F32).sum(0).astype(BF)

    m_all = lax.all_gather(got[:n_m], "row", axis=0, tiled=True)
    vq = jnp.broadcast_to(got[n_m:], (n_dp * n_row, 2 * n_t, width))
    vq = exchange(vq.reshape(-1, width), ("dp", "row"))
    vq = vq.reshape(n_dp, n_row, 2, n_t, width)
    v_both = vq[:, :, 0].reshape(n_dp, n_dp * tok, width)
    q_both = vq[:, :, 1].reshape(n_dp, n_dp * tok, width)
    v = lax.dynamic_index_in_dim(v_both, d, 0, keepdims=False)
    q = lax.dynamic_index_in_dim(q_both, d, 0, keepdims=False)

    r_part = dot(q, w_all, 1, 0).astype(BF)
    n_k = r_part.shape[1] // 2

    def move(x, parity):
        def target(i):
            a, b = divmod(i, n_row)
            return 2 * b + (a ^ parity)

        return permute(x, ("dp", "row"), n_dp * n_row, target)

    low, high = r_part[:, :n_k], r_part[:, n_k:]
    r_piece = total(
        move(jnp.where(d == 0, low, high), 0), move(jnp.where(d == 0, high, low), 1)
    )

    v_cols = v_both.reshape(n_dp, n_dp * tok, 2, n_z, n_w)
    v_cols = jnp.where(core_id == 0, v_cols, v_cols[:, :, ::-1])
    v_cols = lax.dynamic_slice_in_dim(v_cols, d * (n_z // 2), n_z // 2, 3)
    v_cols = v_cols.transpose(3, 2, 0, 1, 4).reshape(n_col, n_dp * tok, n_w)
    r_rep = jnp.broadcast_to(r_piece, (n_col,) + r_piece.shape)
    sent = jnp.concatenate([r_rep, v_cols], 2).reshape(-1, n_k + n_w)
    got = exchange(sent, "col")
    grad_b = dot(x_all, got[:, :n_k], 0, 0)
    grad_a = dot(c_all, got[:, n_k:], 0, 0)

    a_half = jnp.where(d == 0, grow_a[:, :n_w], grow_a[:, n_w:]).T
    a_half, _ = lax.optimization_barrier((a_half, w_own))
    a_own = z_gather(a_half)
    a_all = jnp.concatenate([a_own, core(a_own)], 0)

    y_part = dot(v, a_all, 1, 0).astype(BF)
    outputs = total(
        rows(y_part, d * tok, tok), other_dp(rows(y_part, (1 - d) * tok, tok))
    )

    def weight_rows(i, n):
        piece = dot(a_all[:, i * n : (i + 1) * n], m_all, 0, 1).astype(BF)
        return total(piece, other_dp(piece))

    n = grow_a.shape[0] // 2
    big_weight = jnp.concatenate([weight_rows(i, n) for i in range(2)], 0)
    grad_weight = dot(c_all, x_all, 0, 0).astype(BF)
    return outputs, big_weight, grad_weight, grad_a, grad_b


def solution(mesh):
    return jax.shard_map(
        body,
        mesh=mesh,
        in_specs=(
            P("col", "row"),
            P("row", "col"),
            P("col", "row"),
            P("dp", "col"),
            P("dp", "row"),
        ),
        out_specs=(
            P(("dp", "col"), "row"),
            P("row", "col"),
            P("row", "col"),
            P("row", ("dp", "col")),
            P("col", ("dp", "row")),
        ),
        check_vma=False,
    )
```

time: 741 us -> 246 us (0.33)
  waiting for transfers between devices: 681 us -> 135 us
  starting transfers between devices: 0.44 us -> 47.4 us
  matrix products: 31.7 us -> 19.9 us
  other arithmetic: 1.99 us -> 13 us
    reduce_scatter x4 -> x0, waiting for transfers between devices: 261 us -> none  [the longest x1 74.3 us: body(): lax.psum_scatter(contract(picked, grow_b, 1, 1).astype(jnp.bfloat16), 'ro...]
    all_gather x5 -> x3, waiting for transfers between devices: 283 us -> 23.1 us  [the longest x2 15.9 us: z_gather(): lax.all_gather(x, 'col', axis=0, tiled=True, axis_index_groups=z_rings)]
    psum x1 -> x0, waiting for transfers between devices: 78.3 us -> none  [body(): lax.psum(weight_term.astype(jnp.bfloat16), 'dp').astype(jnp.float32)]
    all_to_all x0 -> x4, waiting for transfers between devices: none -> 66.1 us  [exchange(): return lax.all_to_all(x, axis, 0, 0, tiled=True)]
    unnamed x12 -> x3, waiting for transfers between devices: 59.2 us -> 0.05 us
    ppermute x0 -> x11, waiting for transfers between devices: none -> 45.6 us  [permute(): return lax.ppermute(x, axis, [(i, target(i)) for i in range(size)])]
    all_to_all x0 -> x4, starting transfers between devices: none -> 27.5 us  [exchange(): return lax.all_to_all(x, axis, 0, 0, tiled=True)]
    ppermute x0 -> x11, starting transfers between devices: none -> 19.7 us  [permute(): return lax.ppermute(x, axis, [(i, target(i)) for i in range(size)])]
  transfers between devices with their start and end apart: 11 -> 18, of which waited for: 11 -> 12; matrix products, arithmetic and copies ran while one was open for 5% -> 15% of each run, Pallas kernels for 0% -> 0%
where the time goes in v1:
time: 246 us; the launch traced here: 245 us
  waiting for transfers between devices  135 us (55%)
  starting transfers between devices  47.4 us (19%)
  matrix products  19.9 us (8%)
  local copies, waits for them, and re-layouts  15.4 us (6%)
  between operations  14.2 us (6%)
  other arithmetic  13 us (5%)
    all_to_all x4, waiting for transfers between devices, exchange(): return lax.all_to_all(x, axis, 0, 0, tiled=True)  66.1 us
    ppermute x11, waiting for transfers between devices, permute(): return lax.ppermute(x, axis, [(i, target(i)) for i in range(size)])  45.6 us
    all_to_all x4, starting transfers between devices, exchange(): return lax.all_to_all(x, axis, 0, 0, tiled=True)  27.5 us
    dot_general x10, matrix products, dot(): lax.dot_general(a, b, (((da,), (db,)), ((), ())), preferred_element_type=...  19.9 us
    ppermute x11, starting transfers between devices, permute(): return lax.ppermute(x, axis, [(i, target(i)) for i in range(size)])  19.7 us
    all_gather x2, waiting for transfers between devices, z_gather(): lax.all_gather(x, 'col', axis=0, tiled=True, axis_index_groups=z_rings)  15.9 us
    all_gather x1, waiting for transfers between devices, body(): m_all = lax.all_gather(got[:n_m], 'row', axis=0, tiled=True)  7.2 us
  transfers between devices with their start and end apart: 18, of which 12 were waited for; matrix products, arithmetic and copies ran while one was open for 15% of the time, Pallas kernels for 0%

profile of v1, /device:TPU:1, one launch (start us, length us, event | category | flops | bytes accessed | tf_op | source)
XLA Modules:
  0.0 244.7 jit_solution(10534240242628971438)
XLA Ops:
  7.2 1.9 convolution_convert_fusion.2
  9.1 1.7 convolution_convert_fusion.1
  10.8 1.2 copy.16
  12.0 10.1 %all-to-all-start = ((bf16[16,32,768]{2,1,0:T(8,128)(2,1)}), bf16[16,32,768]{2,1,0:T(8,128)(2,1)S(1)}, u32[]{:S(2)}, u32[]{:S(2)}) async-start(bf16[16,32,768]{2,1,0:T(8,128)(2,1)} %bitcast.1), calls=%async_computation | async-start | bytes 1572864 | tf_op jit(solution)/shard_map/all_to_all | solution.py:41
  23.7 21.1 %all-to-all-done = bf16[16,32,768]{2,1,0:T(8,128)(2,1)S(1)} async-done(((bf16[16,32,768]{2,1,0:T(8,128)(2,1)}), bf16[16,32,768]{2,1,0:T(8,128)(2,1)S(1)}, u32[]{:S(2)}, u32[]{:S(2)}) %all-to-all-start) | async-done | bytes 786464 | tf_op jit(solution)/shard_map/all_to_all | solution.py:41
  44.8 1.3 collective-permute-start
  46.5 15.8 %all-gather.4.cloned.1.call-done = bf16[1024,512]{1,0:T(8,128)(2,1)} async-done(((bf16[128,512]{1,0:T(8,128)(2,1)}), bf16[1024,512]{1,0:T(8,128)(2,1)}) %all-gather.4.cloned.1.call-update) | async-done | bytes 1048592 | tf_op jit(solution)/shard_map/all_gather | solution.py:44
  62.3 4.5 %collective-permute-start.1 = (bf16[1024,512]{1,0:T(8,128)(2,1)}, bf16[1024,512]{1,0:T(8,128)(2,1)}, u32[]{:S(2)}, u32[]{:S(2)}) collective-permute-start(bf16[1024,512]{1,0:T(8,128)(2,1)} %all-gather.4.cloned.1.call-done), channel_id=1, source_target_pairs={{0,1},{1,0},{2,3},{3,2},{4,5},{5,4},{6,7},{7,6},{8,9},{9,8},{10,11... | collective-permute-start | bytes 3145736 | tf_op jit(solution)/shard_map/ppermute | solution.py:32
  66.8 0.9 pad_maximum_fusion.6
  68.3 1.1 collective-permute-done.1
  69.4 1.3 constant_dynamic-update-slice_fusion
  70.7 1.5 convolution_convert_fusion
  72.2 1.7 pad_maximum_fusion
  73.9 6.8 %all-to-all-start.1 = ((bf16[8,80,2048]{2,1,0:T(8,128)(2,1)}), bf16[8,80,2048]{2,1,0:T(8,128)(2,1)S(1)}, u32[]{:S(2)}, u32[]{:S(2)}) async-start(bf16[8,80,2048]{2,1,0:T(8,128)(2,1)} %pad_maximum_fusion), calls=%async_computation.1 | async-start | bytes 5242880 | tf_op jit(solution)/shard_map/all_to_all | solution.py:41
  80.7 1.4 collective-permute-start.8
  82.1 32.0 %all-to-all-done.1 = bf16[8,80,2048]{2,1,0:T(8,128)(2,1)S(1)} async-done(((bf16[8,80,2048]{2,1,0:T(8,128)(2,1)}), bf16[8,80,2048]{2,1,0:T(8,128)(2,1)S(1)}, u32[]{:S(2)}, u32[]{:S(2)}) %all-to-all-start.1) | async-done | bytes 2621472 | tf_op jit(solution)/shard_map/all_to_all | solution.py:41
  114.1 1.3 reduce_sum.25
  116.2 1.1 broadcast_in_dim.6
  117.3 3.7 %all-to-all-start.2 = ((bf16[16,16,2048]{2,1,0:T(8,128)(2,1)}), bf16[16,16,2048]{2,1,0:T(8,128)(2,1)S(1)}, u32[]{:S(2)}, u32[]{:S(2)}) async-start(bf16[16,16,2048]{2,1,0:T(8,128)(2,1)} %broadcast_in_dim.6), calls=%async_computation.2 | async-start | bytes 2097152 | tf_op jit(solution)/shard_map/all_to_all | solution.py:41
  121.1 22.4 %collective-permute-done.8 = bf16[512,512]{1,0:T(8,128)(2,1)} collective-permute-done((bf16[512,512]{1,0:T(8,128)(2,1)S(1)}, bf16[512,512]{1,0:T(8,128)(2,1)}, u32[]{:S(2)}, u32[]{:S(2)}) %collective-permute-start.8) | collective-permute-done | bytes 524320 | tf_op jit(solution)/shard_map/ppermute | solution.py:32
  143.5 1.1 broadcast_select_fusion.3
  144.6 1.2 pad_maximum_fusion.3
  145.8 2.4 broadcast_select_fusion.1
  149.0 2.1 collective-permute-start.3
  151.1 6.8 %all-to-all-done.2 = bf16[16,16,2048]{2,1,0:T(8,128)(2,1)S(1)} async-done(((bf16[16,16,2048]{2,1,0:T(8,128)(2,1)}), bf16[16,16,2048]{2,1,0:T(8,128)(2,1)S(1)}, u32[]{:S(2)}, u32[]{:S(2)}) %all-to-all-start.2) | async-done | bytes 1048608 | tf_op jit(solution)/shard_map/all_to_all | solution.py:41
  157.9 1.0 copy-done.8
  158.8 2.5 %slice_bitcast_fusion = (bf16[2,64,2048]{2,1,0:T(8,128)(2,1)}, bf16[2,64,2048]{2,1,0:T(8,128)(2,1)}, bf16[2,8,1,8,2048]{4,3,2,1,0:T(8,128)(2,1)S(1)}) fusion(bf16[2,8,2,8,2048]{4,3,2,1,0:T(8,128)(2,1)} %bitcast.64), kind=kLoop, calls=%fused_computation.25 | loop fusion | bytes 2621440 | tf_op jit(solution)/shard_map/reshape;squeeze | solution.py:96
  161.3 0.9 copy.20
  162.2 1.9 rev.7
  164.2 1.5 convolution_convert_fusion.4
  165.7 1.9 collective-permute-start.10
  169.0 1.0 pad_maximum_fusion.5
  170.0 7.0 %all-to-all-start.3 = ((bf16[16,64,384]{2,1,0:T(8,128)(2,1)}), bf16[16,64,384]{2,1,0:T(8,128)(2,1)}, u32[]{:S(2)}, u32[]{:S(2)}) async-start(bf16[16,64,384]{2,1,0:T(8,128)(2,1)} %pad_maximum_fusion.5), calls=%async_computation.3 | async-start | bytes 1572864 | tf_op jit(solution)/shard_map/all_to_all | solution.py:41
  177.1 2.3 bitcast_convert_fusion
  179.6 1.9 constant_dynamic-update-slice_fusion.2
  181.5 1.4 convolution_convert_fusion.3
  183.4 5.9 %collective-permute-start.4 = (bf16[32,1024]{1,0:T(8,128)(2,1)S(1)}, bf16[32,1024]{1,0:T(8,128)(2,1)S(1)}, u32[]{:S(2)}, u32[]{:S(2)}) collective-permute-start(bf16[32,1024]{1,0:T(8,128)(2,1)S(1)} %constant_dynamic-slice_fusion), channel_id=1, source_target_pairs={{0,128},{128,0},{1,129},{129,1},{2,130},{130,2},{3,131},{131,3},{4... | collective-permute-start | bytes 196616 | tf_op jit(solution)/shard_map/ppermute | solution.py:32
  189.5 3.4 %collective-permute-done.4 = bf16[32,1024]{1,0:T(8,128)(2,1)S(1)} collective-permute-done((bf16[32,1024]{1,0:T(8,128)(2,1)S(1)}, bf16[32,1024]{1,0:T(8,128)(2,1)S(1)}, u32[]{:S(2)}, u32[]{:S(2)}) %collective-permute-start.4) | collective-permute-done | bytes 65568 | tf_op jit(solution)/shard_map/ppermute | solution.py:32
  193.5 6.3 %all-to-all-done.3 = bf16[16,64,384]{2,1,0:T(8,128)(2,1)} async-done(((bf16[16,64,384]{2,1,0:T(8,128)(2,1)}), bf16[16,64,384]{2,1,0:T(8,128)(2,1)}, u32[]{:S(2)}, u32[]{:S(2)}) %all-to-all-start.3) | async-done | bytes 786464 | tf_op jit(solution)/shard_map/all_to_all | solution.py:41
  199.8 2.5 %fusion.13 = f32[1024,128]{1,0:T(8,128)} fusion(bf16[1024,1024]{1,0:T(8,128)(2,1)S(1)} %bitcast.59, bf16[1024,384]{1,0:T(8,128)(2,1)} %bitcast.25), kind=kOutput, calls=%fused_computation.31 | convolution fusion | flops 268435456 | bytes 2883584 | tf_op jit(solution)/shard_map/dot_general | solution.py:11
  202.3 7.2 %all-gather.8.cloned.1.call-done = bf16[512,2048]{1,0:T(8,128)(2,1)} async-done(((bf16[64,2048]{1,0:T(8,128)(2,1)}), bf16[512,2048]{1,0:T(8,128)(2,1)}) %all-gather.8.cloned.1.call-update) | async-done | bytes 2097168 | tf_op jit(solution)/shard_map/all_gather | solution.py:91
  209.5 3.7 %fusion.7 = bf16[512,512]{1,0:T(8,128)(2,1)S(1)} fusion(bf16[512,2048]{1,0:T(8,128)(2,1)} %all-gather.8.cloned.1.call-done, bf16[2048,1024]{0,1:T(8,128)(2,1)} %copy-done.1), kind=kOutput, calls=%fused_computation.9 | convolution fusion | flops 1074003968 | bytes 4718592 | tf_op jit(solution)/shard_map/dot_general | solution.py:11
  213.2 1.0 collective-permute-start.6
  214.1 1.3 fusion.4
  216.1 2.3 fusion.10
  218.4 7.4 %collective-permute-done.6 = bf16[512,512]{1,0:T(8,128)(2,1)S(1)} collective-permute-done((bf16[512,512]{1,0:T(8,128)(2,1)S(1)}, bf16[512,512]{1,0:T(8,128)(2,1)S(1)}, u32[]{:S(2)}, u32[]{:S(2)}) %collective-permute-start.6) | collective-permute-done | bytes 524320 | tf_op jit(solution)/shard_map/ppermute | solution.py:32
  225.9 11.1 %collective-permute-done.5 = bf16[512,512]{1,0:T(8,128)(2,1)S(1)} collective-permute-done((bf16[512,512]{1,0:T(8,128)(2,1)S(1)}, bf16[512,512]{1,0:T(8,128)(2,1)S(1)}, u32[]{:S(2)}, u32[]{:S(2)}) %collective-permute-start.5) | collective-permute-done | bytes 524320 | tf_op jit(solution)/shard_map/ppermute | solution.py:32
  237.2 1.0 pad_maximum_fusion.2
  (92 shorter events, 8.2 us)
Async XLA Ops:
  7.2 15.0 %copy-start = (bf16[256,512]{1,0:T(8,128)(2,1)S(1)}, bf16[256,512]{1,0:T(8,128)(2,1)}, u32[]{:S(2)}) copy-start(bf16[256,512]{1,0:T(8,128)(2,1)} %param.5) | copy-start | bytes 786436
  10.8 12.1 %copy-start.11 = (bf16[1024,256]{1,0:T(8,128)(2,1)S(1)}, bf16[1024,256]{1,0:T(8,128)(2,1)}, u32[]{:S(2)}) copy-start(bf16[1024,256]{1,0:T(8,128)(2,1)} %param.6) | copy-start | bytes 1572868
  12.0 54.8 %copy-start.12 = (bf16[512,512]{1,0:T(8,128)(2,1)S(1)}, bf16[512,512]{1,0:T(8,128)(2,1)}, u32[]{:S(2)}) copy-start(bf16[512,512]{1,0:T(8,128)(2,1)} %param.7) | copy-start | bytes 1572868
  12.0 32.7 %all-to-all-start = ((bf16[16,32,768]{2,1,0:T(8,128)(2,1)}), bf16[16,32,768]{2,1,0:T(8,128)(2,1)S(1)}, u32[]{:S(2)}, u32[]{:S(2)}) async-start(bf16[16,32,768]{2,1,0:T(8,128)(2,1)} %bitcast.1), calls=%async_computation | async-start | bytes 1572864 | tf_op jit(solution)/shard_map/all_to_all | solution.py:41
  22.1 40.2 %all-gather.4.cloned.1.call-start = ((), (), s32[]{:S(2)}) async-start(), calls=%async_computation.4 | async-start | bytes 1179648 | tf_op jit(solution)/shard_map/all_gather | solution.py:44
  22.9 126.1 %all-gather.6.cloned.1.call-start = ((), (), s32[]{:S(2)}) async-start(), calls=%async_computation.5 | async-start | bytes 2359296 | tf_op jit(solution)/shard_map/all_gather | solution.py:44
  44.8 22.0 %collective-permute-start = (bf16[32,512]{1,0:T(8,128)(2,1)S(1)}, bf16[32,512]{1,0:T(8,128)(2,1)S(1)}, u32[]{:S(2)}, u32[]{:S(2)}) collective-permute-start(bf16[32,512]{1,0:T(8,128)(2,1)S(1)} %slice_reduce_fusion), channel_id=1, source_target_pairs={{0,128},{128,0},{1,129},{129,1},{2,130},{130,2},{3,131},{131,3},{4... | collective-permute-start | bytes 98312 | tf_op jit(solution)/shard_map/ppermute | solution.py:32
  46.1 21.6 %collective-permute-start.2 = (bf16[16,32,128]{2,1,0:T(8,128)(2,1)S(1)}, bf16[16,32,128]{2,1,0:T(8,128)(2,1)S(1)}, u32[]{:S(2)}, u32[]{:S(2)}) collective-permute-start(bf16[16,32,128]{2,1,0:T(8,128)(2,1)S(1)} %broadcast_select_fusion.6), channel_id=1, source_target_pairs={{0,128},{128,0},{1,129},{129,1},{2,130},{130,2},{3,131},{131,3},{4... | collective-permute-start | bytes 393224 | tf_op jit(solution)/shard_map/ppermute | solution.py:32
  62.3 7.1 %collective-permute-start.1 = (bf16[1024,512]{1,0:T(8,128)(2,1)}, bf16[1024,512]{1,0:T(8,128)(2,1)}, u32[]{:S(2)}, u32[]{:S(2)}) collective-permute-start(bf16[1024,512]{1,0:T(8,128)(2,1)} %all-gather.4.cloned.1.call-done), channel_id=1, source_target_pairs={{0,1},{1,0},{2,3},{3,2},{4,5},{5,4},{6,7},{7,6},{8,9},{9,8},{10,11... | collective-permute-start | bytes 3145736 | tf_op jit(solution)/shard_map/ppermute | solution.py:32
  66.8 1.4 copy-start.22
  68.3 2.5 %copy-start.23 = (bf16[8,72,512]{2,1,0:T(8,128)(2,1)S(1)}, bf16[8,72,512]{2,1,0:T(8,128)(2,1)}, u32[]{:S(2)}) copy-start(bf16[8,72,512]{2,1,0:T(8,128)(2,1)} %pad_maximum_fusion.6) | copy-start | bytes 1769476
  70.7 1.5 copy-start.3
  73.9 6.8 %copy-start.10 = (bf16[512,512]{1,0:T(8,128)(2,1)S(1)}, bf16[512,512]{1,0:T(8,128)(2,1)}, u32[]{:S(2)}) copy-start(bf16[512,512]{1,0:T(8,128)(2,1)} %param.8) | copy-start | bytes 1572868
  73.9 40.3 %all-to-all-start.1 = ((bf16[8,80,2048]{2,1,0:T(8,128)(2,1)}), bf16[8,80,2048]{2,1,0:T(8,128)(2,1)S(1)}, u32[]{:S(2)}, u32[]{:S(2)}) async-start(bf16[8,80,2048]{2,1,0:T(8,128)(2,1)} %pad_maximum_fusion), calls=%async_computation.1 | async-start | bytes 5242880 | tf_op jit(solution)/shard_map/all_to_all | solution.py:41
  80.7 65.1 %collective-permute-start.7 = (bf16[512,1024]{1,0:T(8,128)(2,1)}, bf16[512,1024]{1,0:T(8,128)(2,1)}, u32[]{:S(2)}, u32[]{:S(2)}) collective-permute-start(bf16[512,1024]{1,0:T(8,128)(2,1)} %param.9), channel_id=1, source_target_pairs={{0,128},{128,0},{1,129},{129,1},{2,130},{130,2},{3,131},{131,3},{4... | collective-permute-start | bytes 3145736 | tf_op jit(solution)/shard_map/ppermute | solution.py:32
  80.7 62.8 %collective-permute-start.8 = (bf16[512,512]{1,0:T(8,128)(2,1)S(1)}, bf16[512,512]{1,0:T(8,128)(2,1)}, u32[]{:S(2)}, u32[]{:S(2)}) collective-permute-start(bf16[512,512]{1,0:T(8,128)(2,1)S(1)} %copy-done.10), channel_id=1, source_target_pairs={{0,128},{128,0},{1,129},{129,1},{2,130},{130,2},{3,131},{131,3},{4... | collective-permute-start | bytes 1572872 | tf_op jit(solution)/shard_map/ppermute | solution.py:32
  117.3 40.5 %all-to-all-start.2 = ((bf16[16,16,2048]{2,1,0:T(8,128)(2,1)}), bf16[16,16,2048]{2,1,0:T(8,128)(2,1)S(1)}, u32[]{:S(2)}, u32[]{:S(2)}) async-start(bf16[16,16,2048]{2,1,0:T(8,128)(2,1)} %broadcast_in_dim.6), calls=%async_computation.2 | async-start | bytes 2097152 | tf_op jit(solution)/shard_map/all_to_all | solution.py:41
  121.0 88.5 %all-gather.8.cloned.1.call-start = ((), (), s32[]{:S(2)}) async-start(), calls=%async_computation.6 | async-start | bytes 2359296 | tf_op jit(solution)/shard_map/all_gather | solution.py:91
  121.0 24.8 %copy-start.5 = (bf16[512,1024]{1,0:T(8,128)(2,1)S(1)}, bf16[512,1024]{1,0:T(8,128)(2,1)}, u32[]{:S(2)}) copy-start(bf16[512,1024]{1,0:T(8,128)(2,1)} %param.9) | copy-start | bytes 3145732
  144.6 1.2 copy-start.16
  144.6 3.6 %copy-start.14 = (bf16[512,512]{1,0:T(8,128)(2,1)}, bf16[512,512]{1,0:T(8,128)(2,1)S(1)}, u32[]{:S(2)}) copy-start(bf16[512,512]{1,0:T(8,128)(2,1)S(1)} %get-tuple-element.12) | copy-start | bytes 1572868
  145.8 2.4 copy-start.18
  149.0 30.6 %collective-permute-start.3 = (bf16[1024,1024]{0,1:T(8,128)(2,1)}, bf16[1024,1024]{0,1:T(8,128)(2,1)}, u32[]{:S(2)}, u32[]{:S(2)}) collective-permute-start(bf16[1024,1024]{0,1:T(8,128)(2,1)} %all-gather.6.cloned.1.call-done), channel_id=1, source_target_pairs={{0,1},{1,0},{2,3},{3,2},{4,5},{5,4},{6,7},{7,6},{8,9},{9,8},{10,11... | collective-permute-start | bytes 6291464 | tf_op jit(solution)/shard_map/ppermute | solution.py:32
  157.9 1.0 copy-start.8
  158.8 5.4 %copy-start.4 = (bf16[2048,512]{1,0:T(8,128)(2,1)S(1)}, bf16[2048,512]{1,0:T(8,128)(2,1)}, u32[]{:S(2)}) copy-start(bf16[2048,512]{1,0:T(8,128)(2,1)} %copy-done.3) | copy-start | bytes 6291460
  164.2 4.1 %copy-start.9 = (bf16[16,8,16,128]{3,2,1,0:T(8,128)(2,1)S(1)}, bf16[16,8,16,128]{3,2,1,0:T(8,128)(2,1)}, u32[]{:S(2)}) copy-start(bf16[16,8,16,128]{3,2,1,0:T(8,128)(2,1)} %copy.20) | copy-start | bytes 1572868
  164.2 4.2 %copy-start.20 = (bf16[2,64,2,8,128]{4,3,2,1,0:T(8,128)(2,1)S(1)}, bf16[2,64,2,8,128]{4,3,2,1,0:T(8,128)(2,1)}, u32[]{:S(2)}) copy-start(bf16[2,64,2,8,128]{4,3,2,1,0:T(8,128)(2,1)} %rev.7) | copy-start | bytes 1572868
  165.7 3.2 %collective-permute-start.10 = (bf16[64,256]{1,0:T(8,128)(2,1)S(1)}, bf16[64,256]{1,0:T(8,128)(2,1)S(1)}, u32[]{:S(2)}, u32[]{:S(2)}) collective-permute-start(bf16[64,256]{1,0:T(8,128)(2,1)S(1)} %get-tuple-element.17), channel_id=1, source_target_pairs={{0,16},{16,48},{32,80},{48,112},{64,144},{80,176},{96,208},{112,24... | collective-permute-start | bytes 98312 | tf_op jit(solution)/shard_map/ppermute | solution.py:32
  167.7 1.3 collective-permute-start.9
  168.6 8.4 %copy-start.6 = (bf16[512,1024]{1,0:T(8,128)(2,1)S(1)}, bf16[512,1024]{1,0:T(8,128)(2,1)}, u32[]{:S(2)}) copy-start(bf16[512,1024]{1,0:T(8,128)(2,1)} %get-tuple-element.8) | copy-start | bytes 3145732
  168.6 8.4 %copy-start.15 = (bf16[512,512]{1,0:T(8,128)(2,1)S(1)}, bf16[512,512]{1,0:T(8,128)(2,1)}, u32[]{:S(2)}) copy-start(bf16[512,512]{1,0:T(8,128)(2,1)} %copy-done.14) | copy-start | bytes 1572868
  168.6 8.4 %copy-start.17 = (bf16[512,512]{1,0:T(8,128)(2,1)S(1)}, bf16[512,512]{1,0:T(8,128)(2,1)}, u32[]{:S(2)}) copy-start(bf16[512,512]{1,0:T(8,128)(2,1)} %copy-done.16) | copy-start | bytes 1572868
  170.0 29.7 %all-to-all-start.3 = ((bf16[16,64,384]{2,1,0:T(8,128)(2,1)}), bf16[16,64,384]{2,1,0:T(8,128)(2,1)}, u32[]{:S(2)}, u32[]{:S(2)}) async-start(bf16[16,64,384]{2,1,0:T(8,128)(2,1)} %pad_maximum_fusion.5), calls=%async_computation.3 | async-start | bytes 1572864 | tf_op jit(solution)/shard_map/all_to_all | solution.py:41
  177.1 2.3 copy-start.13
  179.6 1.9 copy-start.19
  181.5 2.0 copy-start.1
  181.5 7.8 %copy-start.7 = (bf16[512,1024]{1,0:T(8,128)(2,1)S(1)}, bf16[512,1024]{1,0:T(8,128)(2,1)}, u32[]{:S(2)}) copy-start(bf16[512,1024]{1,0:T(8,128)(2,1)} %get-tuple-element.8) | copy-start | bytes 3145732
  183.4 9.4 %collective-permute-start.4 = (bf16[32,1024]{1,0:T(8,128)(2,1)S(1)}, bf16[32,1024]{1,0:T(8,128)(2,1)S(1)}, u32[]{:S(2)}, u32[]{:S(2)}) collective-permute-start(bf16[32,1024]{1,0:T(8,128)(2,1)S(1)} %constant_dynamic-slice_fusion), channel_id=1, source_target_pairs={{0,128},{128,0},{1,129},{129,1},{2,130},{130,2},{3,131},{131,3},{4... | collective-permute-start | bytes 196616 | tf_op jit(solution)/shard_map/ppermute | solution.py:32
  209.5 4.6 %copy-start.2 = (bf16[2048,1024]{0,1:T(8,128)(2,1)S(1)}, bf16[2048,1024]{0,1:T(8,128)(2,1)}, u32[]{:S(2)}) copy-start(bf16[2048,1024]{0,1:T(8,128)(2,1)} %copy-done.1) | copy-start | bytes 12582916
  209.5 4.6 %copy-start.24 = (bf16[512,2048]{1,0:T(8,128)(2,1)S(1)}, bf16[512,2048]{1,0:T(8,128)(2,1)}, u32[]{:S(2)}) copy-start(bf16[512,2048]{1,0:T(8,128)(2,1)} %all-gather.8.cloned.1.call-done) | copy-start | bytes 6291460
  213.1 2.9 %copy-start.21 = (bf16[16,2,32,512]{3,2,1,0:T(8,128)(2,1)S(1)}, bf16[16,2,32,512]{3,2,1,0:T(8,128)(2,1)}, u32[]{:S(2)}) copy-start(bf16[16,2,32,512]{3,2,1,0:T(8,128)(2,1)} %pad_maximum_fusion.3) | copy-start | bytes 3145732
  213.2 12.6 %collective-permute-start.6 = (bf16[512,512]{1,0:T(8,128)(2,1)S(1)}, bf16[512,512]{1,0:T(8,128)(2,1)S(1)}, u32[]{:S(2)}, u32[]{:S(2)}) collective-permute-start(bf16[512,512]{1,0:T(8,128)(2,1)S(1)} %fusion.7), channel_id=1, source_target_pairs={{0,128},{128,0},{1,129},{129,1},{2,130},{130,2},{3,131},{131,3},{4... | collective-permute-start | bytes 1572872 | tf_op jit(solution)/shard_map/ppermute | solution.py:32
  215.4 21.6 %collective-permute-start.5 = (bf16[512,512]{1,0:T(8,128)(2,1)S(1)}, bf16[512,512]{1,0:T(8,128)(2,1)S(1)}, u32[]{:S(2)}, u32[]{:S(2)}) collective-permute-start(bf16[512,512]{1,0:T(8,128)(2,1)S(1)} %fusion.4), channel_id=1, source_target_pairs={{0,128},{128,0},{1,129},{129,1},{2,130},{130,2},{3,131},{131,3},{4... | collective-permute-start | bytes 1572872 | tf_op jit(solution)/shard_map/ppermute | solution.py:32
Sparse Core Ops, SparseCore 0:
  25.3 36.9 all-gather.3
  68.3 41.8 all-gather.5
  149.1 60.3 all-gather.7

commit v2 on v1

v2 whole, which is shorter than its diff:
```python
import jax
import jax.numpy as jnp
from jax import lax
from jax.sharding import PartitionSpec as P

BF = jnp.bfloat16
F32 = jnp.float32


def dot(a, b, da, db):
    return lax.dot_general(
        a, b, (((da,), (db,)), ((), ())), preferred_element_type=F32
    )


def rows(x, start, size):
    return lax.dynamic_slice_in_dim(x, start, size, 0)


def total(a, b):
    return (a.astype(F32) + b.astype(F32)).astype(BF)


def body(small_w, grow_a, grow_b, inputs, cotangent):
    n_dp, n_row, n_col = (lax.axis_size(a) for a in ("dp", "row", "col"))
    d, c = lax.axis_index("dp"), lax.axis_index("col")
    core_id = c % 2
    n_z = n_col // 2
    z_rings = [[2 * z + i for z in range(n_z)] for i in range(2)]

    def permute(x, axis, size, target):
        return lax.ppermute(x, axis, [(i, target(i)) for i in range(size)])

    def core(x):
        return permute(x, "col", n_col, lambda i: i ^ 1)

    def other_dp(x):
        return permute(x, "dp", n_dp, lambda i: i ^ 1)

    def from_y(x, k):
        return permute(x, "row", n_row, lambda i: (i - 2 * k) % n_row)

    def x_far(x):
        return permute(x, "row", n_row, lambda i: i ^ 1)

    def from_z(x, k):
        return permute(x, "col", n_col, lambda i: (i - 2 * k) % n_col) if k else x

    def exchange(x, axis, groups=None):
        return lax.all_to_all(x, axis, 0, 0, tiled=True, axis_index_groups=groups)

    def scatter_sum(x, axis, size):
        got = exchange(x, axis).reshape(size, -1, x.shape[1])
        return got.astype(F32).sum(0).astype(BF)

    def gather(x, axis, size):
        return exchange(jnp.broadcast_to(x, (size,) + x.shape).reshape(-1, x.shape[1]), axis)

    def assemble(pieces, first):
        n = pieces[0].shape[0]
        out = jnp.zeros((n * len(pieces), pieces[0].shape[1]), BF)
        for k, piece in enumerate(pieces):
            at = (first + k) % len(pieces) * n
            out = lax.dynamic_update_slice_in_dim(out, piece, at, 0)
        return out

    def z_assemble(x):
        return assemble([from_z(x, k) for k in range(n_z)], c // 2)

    def z_gather(x):
        return lax.all_gather(x, "col", axis=0, tiled=True, axis_index_groups=z_rings)

    def both_cores(own):
        other = core(own)
        low = jnp.where(core_id == 0, own, other)
        high = jnp.where(core_id == 0, other, own)
        return jnp.concatenate([low, high], 0)

    def x_pair(x):
        return permute(x, ("dp", "row"), n_dp * n_row, lambda i: (i ^ n_row) ^ 1)

    def by_dp(own, other):
        n = own.shape[0] // n_col
        own = own.reshape(n_col, n, -1)
        other = other.reshape(n_col, n, -1)
        first = jnp.where(d == 0, own, other)
        second = jnp.where(d == 0, other, own)
        return jnp.stack([first, second], 1).reshape(n_dp * n_col * n, -1)

    n_w = small_w.shape[0] // 2
    w_half = rows(small_w, d * n_w, n_w)
    w_own = z_gather(w_half)
    q_mine = scatter_sum(dot(cotangent, grow_a, 1, 0).astype(BF), "row", n_row)
    q = gather(q_mine, "row", n_row)
    x_other, c_other = x_pair(inputs), other_dp(cotangent)
    w_own, q, x_other, c_other = lax.optimization_barrier(
        (w_own, q, x_other, c_other)
    )
    w_all = both_cores(w_own)

    tok = inputs.shape[0] // n_col
    x_all = by_dp(inputs, x_other)

    part = dot(w_all, grow_b, 1, 1).astype(BF)
    n_m, n_n = part.shape[0] // n_row, part.shape[1]
    a_half = jnp.where(d == 0, grow_a[:, :n_w], grow_a[:, n_w:]).T
    a_half, _ = lax.optimization_barrier((a_half, w_own))
    a_own = z_gather(a_half)
    m_slice = scatter_sum(part, "row", n_row)
    x_hi = lax.axis_index("row") % 2
    m_other = x_far(m_slice)
    m_pair = jnp.concatenate(
        [jnp.where(x_hi == 0, m_slice, m_other), jnp.where(x_hi == 0, m_other, m_slice)], 0
    )
    m_pieces = [m_pair] + [from_y(m_pair, k) for k in range(1, n_row // 2)]
    m_all = assemble(m_pieces, lax.axis_index("row") // 2)

    r_part = dot(q, small_w, 1, 0).astype(BF)
    n_k = r_part.shape[1] // 2
    v_part = dot(x_all, m_slice, 1, 1).astype(BF)
    n_s = v_part.shape[1]
    both = jnp.concatenate(
        [
            r_part[:, :n_k].reshape(n_z, 2, tok, n_k),
            r_part[:, n_k:].reshape(n_z, 2, tok, n_k),
            v_part.reshape(n_z, 2, n_dp * tok, n_s),
        ],
        2,
    )
    keep = jnp.where(core_id == 0, both[:, 0], both[:, 1])
    send = jnp.where(core_id == 0, both[:, 1], both[:, 0])
    both = total(keep, core(send)).reshape(-1, n_s)
    both = exchange(both, "col", z_rings).reshape(n_z, -1, n_s)
    both = both.astype(F32).sum(0).astype(BF)
    low, high, v_mine = both[:tok], both[tok : 2 * tok], both[2 * tok :]

    def move(x, parity):
        def target(i):
            a, b = divmod(i, n_row)
            return 2 * b + (a ^ parity)

        return permute(x, ("dp", "row"), n_dp * n_row, target)

    same = move(jnp.where(d == 0, low, high), 0)
    swap = move(jnp.where(d == 0, high, low), 1)
    r_piece = jnp.concatenate(
        [jnp.where(x_hi == 0, same, swap), jnp.where(x_hi == 0, swap, same)], 0
    )
    v_both = gather(v_mine, ("dp", "row"), n_dp * n_row)
    v_both, m_all, a_own = lax.optimization_barrier((v_both, m_all, a_own))
    c_all = by_dp(cotangent, c_other)
    v_both = v_both.reshape(n_dp, n_row, n_dp * tok, n_s)
    v = lax.dynamic_index_in_dim(v_both, d, 0, keepdims=False)
    v = v.transpose(1, 0, 2).reshape(n_dp * tok, n_row * n_s)

    v_cols = v_both.reshape(n_dp, 2, n_z // 2, n_dp * tok, 2, n_w)
    v_cols = lax.dynamic_slice_in_dim(v_cols, d * (n_z // 4), n_z // 4, 2)
    v_cols = v_cols.transpose(2, 4, 1, 0, 3, 5).reshape(n_col, n_dp * tok, n_w)
    r_rep = jnp.broadcast_to(r_piece, (n_col,) + r_piece.shape)
    sent = jnp.concatenate([r_rep, v_cols], 2).reshape(-1, n_k + n_w)
    got = exchange(sent, "col")
    a_all = both_cores(a_own)
    n = grow_a.shape[0] // 2
    parts = [
        dot(a_all[:, i * n : (i + 1) * n], m_all, 0, 0).astype(BF) for i in range(2)
    ]
    big_weight = jnp.concatenate([total(p, other_dp(p)) for p in parts], 0)
    got, big_weight = lax.optimization_barrier((got, big_weight))
    grad_b = dot(x_all, got[:, :n_k], 0, 0)
    grad_a = dot(c_all, got[:, n_k:], 0, 0)

    y_part = dot(v, a_all, 1, 0).astype(BF)
    outputs = total(
        rows(y_part, d * tok, tok), other_dp(rows(y_part, (1 - d) * tok, tok))
    )

    grad_weight = dot(c_all, x_all, 0, 0).astype(BF)
    return outputs, big_weight, grad_weight, grad_a, grad_b


def solution(mesh):
    return jax.shard_map(
        body,
        mesh=mesh,
        in_specs=(
            P("col", "row"),
            P("row", "col"),
            P("col", "row"),
            P("dp", "col"),
            P("dp", "row"),
        ),
        out_specs=(
            P(("dp", "col"), "row"),
            P("row", "col"),
            P("row", "col"),
            P("row", ("dp", "col")),
            P("col", ("dp", "row")),
        ),
        check_vma=False,
    )
```

time: 246 us -> 209 us (0.85)
  waiting for transfers between devices: 135 us -> 69.6 us
  blocking collectives: 0 us -> 36.8 us
  local copies, waits for them, and re-layouts: 15.4 us -> 8.89 us
  starting transfers between devices: 47.4 us -> 44.4 us
  other arithmetic: 13 us -> 15.7 us
    all_to_all x0 -> x2, blocking collectives: none -> 36.8 us  [exchange(): return lax.all_to_all(x, axis, 0, 0, tiled=True, axis_index_groups=groups)]
    all_to_all x4, waiting for transfers between devices: 66.1 us -> 43.6 us  [exchange(): return lax.all_to_all(x, axis, 0, 0, tiled=True, axis_index_groups=groups)]
    ppermute x11 -> x14, waiting for transfers between devices: 45.6 us -> 25.9 us  [permute(): return lax.ppermute(x, axis, [(i, target(i)) for i in range(size)])]
    all_gather x2, waiting for transfers between devices: 15.9 us -> 0.04 us  [z_gather(): lax.all_gather(x, 'col', axis=0, tiled=True, axis_index_groups=z_rings)]
    all_gather x1 -> x0, waiting for transfers between devices: 7.2 us -> none  [body(): m_all = lax.all_gather(got[:n_m], 'row', axis=0, tiled=True)]
    all_to_all x4, starting transfers between devices: 27.5 us -> 22.5 us  [exchange(): return lax.all_to_all(x, axis, 0, 0, tiled=True, axis_index_groups=groups)]
    concatenate x3 -> x0, local copies, waits for them, and re-layouts: 4.3 us -> none  [the longest x1 1.86 us: body(): a_all = jnp.concatenate([a_own, core(a_own)], 0)]
    select_n x2 -> x6, other arithmetic: 0.03 us -> 3.98 us  [the longest x2 3.86 us: both_cores(): low = jnp.where(core_id == 0, own, other)]
  transfers between devices with their start and end apart: 18 -> 20, of which waited for: 12 -> 7; matrix products, arithmetic and copies ran while one was open for 15% -> 15% of each run, Pallas kernels for 0% -> 0%
where the time goes in v2:
time: 209 us; the launch traced here: 208 us
  waiting for transfers between devices  69.6 us (33%)
  starting transfers between devices  44.4 us (21%)
  blocking collectives  36.8 us (18%)
  matrix products  17.7 us (8%)
  other arithmetic  15.7 us (8%)
  between operations  14.5 us (7%)
  local copies, waits for them, and re-layouts  8.89 us (4%)
    all_to_all x4, waiting for transfers between devices, exchange(): return lax.all_to_all(x, axis, 0, 0, tiled=True, axis_index_groups=groups)  43.6 us
    all_to_all x2, blocking collectives, exchange(): return lax.all_to_all(x, axis, 0, 0, tiled=True, axis_index_groups=groups)  36.8 us
    ppermute x14, waiting for transfers between devices, permute(): return lax.ppermute(x, axis, [(i, target(i)) for i in range(size)])  25.9 us
    all_to_all x4, starting transfers between devices, exchange(): return lax.all_to_all(x, axis, 0, 0, tiled=True, axis_index_groups=groups)  22.5 us
    ppermute x14, starting transfers between devices, permute(): return lax.ppermute(x, axis, [(i, target(i)) for i in range(size)])  21.9 us
    dot_general x10, matrix products, dot(): lax.dot_general(a, b, (((da,), (db,)), ((), ())), preferred_element_type=...  17.7 us
  transfers between devices with their start and end apart: 20, of which 7 were waited for; matrix products, arithmetic and copies ran while one was open for 15% of the time, Pallas kernels for 0%

profile of v2, /device:TPU:1, one launch (start us, length us, event | category | flops | bytes accessed | tf_op | source)
XLA Modules:
  0.0 207.6 jit_solution(16814270901426347406)
XLA Ops:
  7.2 1.6 constant_dynamic-slice_fusion.1
  8.9 2.1 %collective-permute-start.1 = (bf16[512,1024]{1,0:T(8,128)(2,1)}, bf16[512,1024]{1,0:T(8,128)(2,1)S(1)}, u32[]{:S(2)}, u32[]{:S(2)}) collective-permute-start(bf16[512,1024]{1,0:T(8,128)(2,1)} %param.9), channel_id=1, source_target_pairs={{0,128},{128,0},{1,129},{129,1},{2,130},{130,2},{3,131},{131,3},{4... | collective-permute-start | bytes 3145736 | tf_op jit(solution)/shard_map/ppermute | solution.py:32
  11.0 1.8 collective-permute-start
  12.8 1.8 convolution_convert_fusion.3
  14.6 26.6 %all_to_all.51 = bf16[8,64,256]{2,1,0:T(8,128)(2,1)S(1)} all-to-all(bf16[8,64,256]{2,1,0:T(8,128)(2,1)S(1)} %bitcast.83), channel_id=1, replica_groups=mesh['dp'=2,'row'=8,'col'=16] {'row'}, dimensions={0} | all-to-all | bytes 524288 | tf_op jit(solution)/shard_map/all_to_all | solution.py:50
  41.3 10.2 %all_to_all.52 = bf16[8,64,256]{2,1,0:T(8,128)(2,1)S(1)} all-to-all(bf16[8,64,256]{2,1,0:T(8,128)(2,1)S(1)} %broadcast_in_dim.12), channel_id=1, replica_groups=mesh['dp'=2,'row'=8,'col'=16] {'row'}, dimensions={0} | all-to-all | bytes 524288 | tf_op jit(solution)/shard_map/all_to_all | solution.py:50
  52.3 2.8 %collective-permute-start.2 = (bf16[1024,512]{1,0:T(8,128)(2,1)}, bf16[1024,512]{1,0:T(8,128)(2,1)S(1)}, u32[]{:S(2)}, u32[]{:S(2)}) collective-permute-start(bf16[1024,512]{1,0:T(8,128)(2,1)} %all-gather.3.cloned.1.call-done), channel_id=1, source_target_pairs={{0,1},{1,0},{2,3},{3,2},{4,5},{5,4},{6,7},{7,6},{8,9},{9,8},{10,11... | collective-permute-start | bytes 3145736 | tf_op jit(solution)/shard_map/ppermute | solution.py:32
  55.1 2.5 %collective-permute-done.2 = bf16[1024,512]{1,0:T(8,128)(2,1)S(1)} collective-permute-done((bf16[1024,512]{1,0:T(8,128)(2,1)}, bf16[1024,512]{1,0:T(8,128)(2,1)S(1)}, u32[]{:S(2)}, u32[]{:S(2)}) %collective-permute-start.2) | collective-permute-done | bytes 1048608 | tf_op jit(solution)/shard_map/ppermute | solution.py:32
  57.6 1.4 broadcast_select_fusion.5
  59.0 2.7 %convolution_convert_fusion = bf16[2048,512]{1,0:T(8,128)(2,1)} fusion(bf16[512,512]{1,0:T(8,128)(2,1)S(1)} %copy-done, bf16[1024,512]{1,0:T(8,128)(2,1)S(1)} %get-tuple-element.30, bf16[1024,512]{1,0:T(8,128)(2,1)S(1)} %get-tuple-element.29), kind=kOutput, calls=%fused_computation.6 | convolution fusion | flops 1078984704 | bytes 4718592 | tf_op jit(solution)/shard_map/dot_general | solution.py:11
  61.7 4.8 %all-to-all-start.2 = ((bf16[8,256,512]{2,1,0:T(8,128)(2,1)}), bf16[8,256,512]{2,1,0:T(8,128)(2,1)S(1)}, u32[]{:S(2)}, u32[]{:S(2)}) async-start(bf16[8,256,512]{2,1,0:T(8,128)(2,1)} %bitcast.72), calls=%async_computation.2 | async-start | bytes 4194304 | tf_op jit(solution)/shard_map/all_to_all | solution.py:50
  66.5 1.8 select_bitcast_fusion
  68.3 1.3 broadcast_select_fusion.7
  69.7 1.2 pad_maximum_fusion.5
  71.2 23.1 %all-to-all-done.2 = bf16[8,256,512]{2,1,0:T(8,128)(2,1)S(1)} async-done(((bf16[8,256,512]{2,1,0:T(8,128)(2,1)}), bf16[8,256,512]{2,1,0:T(8,128)(2,1)S(1)}, u32[]{:S(2)}, u32[]{:S(2)}) %all-to-all-start.2) | async-done | bytes 2097184 | tf_op jit(solution)/shard_map/all_to_all | solution.py:50
  94.7 1.7 convolution_convert_fusion.1
  96.6 1.7 collective-permute-start.3
  98.8 1.0 collective-permute-done.3
  99.8 1.0 fusion.17
  100.8 6.9 %all-to-all-start.3 = ((bf16[8,128,256]{2,1,0:T(8,128)(2,1)}), bf16[8,128,256]{2,1,0:T(8,128)(2,1)S(1)}, u32[]{:S(2)}, u32[]{:S(2)}) async-start(bf16[8,128,256]{2,1,0:T(8,128)(2,1)} %fusion.17), calls=%async_computation.3 | async-start | bytes 1048576 | tf_op jit(solution)/shard_map/all_to_all | solution.py:50
  107.9 0.9 pad_maximum_fusion.9
  108.8 1.2 collective-permute-start.5
  110.6 15.8 %all-to-all-done.3 = bf16[8,128,256]{2,1,0:T(8,128)(2,1)S(1)} async-done(((bf16[8,128,256]{2,1,0:T(8,128)(2,1)}), bf16[8,128,256]{2,1,0:T(8,128)(2,1)S(1)}, u32[]{:S(2)}, u32[]{:S(2)}) %all-to-all-start.3) | async-done | bytes 524320 | tf_op jit(solution)/shard_map/all_to_all | solution.py:50
  126.5 0.8 broadcast_in_dim.13
  127.3 6.2 %all-to-all-start.4 = ((bf16[16,64,256]{2,1,0:T(8,128)(2,1)}), bf16[16,64,256]{2,1,0:T(8,128)(2,1)S(1)}, u32[]{:S(2)}, u32[]{:S(2)}) async-start(bf16[16,64,256]{2,1,0:T(8,128)(2,1)} %broadcast_in_dim.13), calls=%async_computation.4 | async-start | bytes 1048576 | tf_op jit(solution)/shard_map/all_to_all | solution.py:50
  133.6 1.1 constant_dynamic-update-slice_fusion.2
  134.7 1.1 constant_dynamic-update-slice_fusion.1
  135.8 1.1 collective-permute-done.7
  136.9 1.1 constant_dynamic-update-slice_fusion
  138.0 4.6 %all-to-all-done.4 = bf16[16,64,256]{2,1,0:T(8,128)(2,1)S(1)} async-done(((bf16[16,64,256]{2,1,0:T(8,128)(2,1)}), bf16[16,64,256]{2,1,0:T(8,128)(2,1)S(1)}, u32[]{:S(2)}, u32[]{:S(2)}) %all-to-all-start.4) | async-done | bytes 524320 | tf_op jit(solution)/shard_map/all_to_all | solution.py:50
  142.6 2.9 %collective-permute-start.8 = (bf16[1024,1024]{0,1:T(8,128)(2,1)}, bf16[1024,1024]{0,1:T(8,128)(2,1)}, u32[]{:S(2)}, u32[]{:S(2)}) collective-permute-start(bf16[1024,1024]{0,1:T(8,128)(2,1)} %all-gather.5.cloned.1.call-done), channel_id=1, source_target_pairs={{0,1},{1,0},{2,3},{3,2},{4,5},{5,4},{6,7},{7,6},{8,9},{9,8},{10,11... | collective-permute-start | bytes 6291464 | tf_op jit(solution)/shard_map/ppermute | solution.py:32
  145.6 1.8 broadcast_select_fusion.3
  148.0 4.5 %collective-permute-start.11 = (bf16[32,256]{1,0:T(8,128)(2,1)S(1)}, bf16[32,256]{1,0:T(8,128)(2,1)S(1)}, u32[]{:S(2)}, u32[]{:S(2)}) collective-permute-start(bf16[32,256]{1,0:T(8,128)(2,1)S(1)} %get-tuple-element.40), channel_id=1, source_target_pairs={{0,16},{16,48},{32,80},{48,112},{64,144},{80,176},{96,208},{112,24... | collective-permute-start | bytes 49160 | tf_op jit(solution)/shard_map/ppermute | solution.py:32
  152.6 2.3 %bitcast_convert_fusion = bf16[1024,512]{1,0:T(8,128)(2,1)} fusion(bf16[16,1,32,512]{3,2,1,0:T(8,128)(2,1)S(1)} %bitcast.76, bf16[16,1,32,512]{3,2,1,0:T(8,128)(2,1)S(1)} %bitcast.74, bf16[16,1,32,1024]{3,2,1,0:T(8,128)(2,1)S(1)} %bitcast.68, bf16[16,1,32,1024]{3,2,1,0:T(8,128)(2,1)S(1)} %bitcast.66), kind=kOutput, calls=%fused_computation.15 | convolution fusion | flops 1075838976 | bytes 4194304 | tf_op jit(solution)/shard_map/dot_general | solution.py:11
  154.9 0.9 reshape_reshape.3
  155.8 1.1 dynamic-slice_bitcast_fusion
  157.0 1.0 pad_maximum_fusion.8
  158.0 4.6 %all-to-all-start.5 = ((bf16[16,64,384]{2,1,0:T(8,128)(2,1)}), bf16[16,64,384]{2,1,0:T(8,128)(2,1)}, u32[]{:S(2)}, u32[]{:S(2)}) async-start(bf16[16,64,384]{2,1,0:T(8,128)(2,1)} %pad_maximum_fusion.8), calls=%async_computation.5 | async-start | bytes 1572864 | tf_op jit(solution)/shard_map/all_to_all | solution.py:50
  162.7 2.5 %broadcast_select_fusion.1 = (bf16[1024,1024]{0,1:T(8,128)(2,1)S(1)}, bf16[1024,1024]{0,1:T(8,128)(2,1)S(1)}) fusion(bf16[1024,1024]{0,1:T(8,128)(2,1)} %all-gather.5.cloned.1.call-done, bf16[1024,1024]{0,1:T(8,128)(2,1)} %collective-permute-done.8, pred[]{:T(512)S(6)} %eq.13), kind=kLoop, calls=%fused_computation.17 | loop fusion | flops 2097152 | bytes 8388609 | tf_op jit(solution)/shard_map/jit(_where)/select_n | solution.py:75
  165.2 1.3 fusion.13
  166.5 1.3 fusion.10
  167.7 1.5 collective-permute-start.12
  169.3 1.4 fusion.16
  170.7 1.5 collective-permute-start.9
  172.4 21.3 %collective-permute-done.9 = bf16[32,1024]{1,0:T(8,128)(2,1)S(1)} collective-permute-done((bf16[32,1024]{1,0:T(8,128)(2,1)S(1)}, bf16[32,1024]{1,0:T(8,128)(2,1)S(1)}, u32[]{:S(2)}, u32[]{:S(2)}) %collective-permute-start.9) | collective-permute-done | bytes 65568 | tf_op jit(solution)/shard_map/ppermute | solution.py:32
  194.6 1.0 pad_maximum_fusion.7
  195.7 2.6 %fusion.20 = f32[512,256]{1,0:T(8,128)} fusion(bf16[1024,512]{1,0:T(8,128)(2,1)} %bitcast.65, bf16[1024,384]{1,0:T(8,128)(2,1)} %bitcast.21), kind=kOutput, calls=%fused_computation.41 | convolution fusion | flops 268435456 | bytes 2097152 | tf_op jit(solution)/shard_map/dot_general | solution.py:11
  198.3 2.5 %fusion.22 = f32[1024,128]{1,0:T(8,128)} fusion(bf16[1024,1024]{1,0:T(8,128)(2,1)S(1)} %bitcast.63, bf16[1024,384]{1,0:T(8,128)(2,1)} %bitcast.21), kind=kOutput, calls=%fused_computation.45 | convolution fusion | flops 268435456 | bytes 2883584 | tf_op jit(solution)/shard_map/dot_general | solution.py:11
  (69 shorter events, 5.3 us)
Async XLA Ops:
  7.2 51.8 %copy-start = (bf16[512,512]{1,0:T(8,128)(2,1)S(1)}, bf16[512,512]{1,0:T(8,128)(2,1)}, u32[]{:S(2)}) copy-start(bf16[512,512]{1,0:T(8,128)(2,1)} %param.7) | copy-start | bytes 1572868
  7.2 44.4 %all-gather.3.cloned.1.call-start = ((), (), s32[]{:S(2)}) async-start(), calls=%async_computation.6 | async-start | bytes 1179648 | tf_op jit(solution)/shard_map/all_gather | solution.py:71
  8.9 42.6 %collective-permute-start.1 = (bf16[512,1024]{1,0:T(8,128)(2,1)}, bf16[512,1024]{1,0:T(8,128)(2,1)S(1)}, u32[]{:S(2)}, u32[]{:S(2)}) collective-permute-start(bf16[512,1024]{1,0:T(8,128)(2,1)} %param.9), channel_id=1, source_target_pairs={{0,128},{128,0},{1,129},{129,1},{2,130},{130,2},{3,131},{131,3},{4... | collective-permute-start | bytes 3145736 | tf_op jit(solution)/shard_map/ppermute | solution.py:32
  11.0 40.5 %collective-permute-start = (bf16[512,512]{1,0:T(8,128)(2,1)}, bf16[512,512]{1,0:T(8,128)(2,1)S(1)}, u32[]{:S(2)}, u32[]{:S(2)}) collective-permute-start(bf16[512,512]{1,0:T(8,128)(2,1)} %param.8), channel_id=1, source_target_pairs={{0,144},{16,128},{32,176},{48,160},{64,208},{80,192},{96,240},{112... | collective-permute-start | bytes 1572872 | tf_op jit(solution)/shard_map/ppermute | solution.py:32
  51.5 0.8 copy-start.11
  51.5 7.5 %copy-start.9 = (bf16[512,1024]{1,0:T(8,128)(2,1)}, bf16[512,1024]{1,0:T(8,128)(2,1)S(1)}, u32[]{:S(2)}) copy-start(bf16[512,1024]{1,0:T(8,128)(2,1)S(1)} %collective-permute-done.1) | copy-start | bytes 3145732
  52.3 5.3 %collective-permute-start.2 = (bf16[1024,512]{1,0:T(8,128)(2,1)}, bf16[1024,512]{1,0:T(8,128)(2,1)S(1)}, u32[]{:S(2)}, u32[]{:S(2)}) collective-permute-start(bf16[1024,512]{1,0:T(8,128)(2,1)} %all-gather.3.cloned.1.call-done), channel_id=1, source_target_pairs={{0,1},{1,0},{2,3},{3,2},{4,5},{5,4},{6,7},{7,6},{8,9},{9,8},{10,11... | collective-permute-start | bytes 3145736 | tf_op jit(solution)/shard_map/ppermute | solution.py:32
  61.7 32.7 %all-to-all-start.2 = ((bf16[8,256,512]{2,1,0:T(8,128)(2,1)}), bf16[8,256,512]{2,1,0:T(8,128)(2,1)S(1)}, u32[]{:S(2)}, u32[]{:S(2)}) async-start(bf16[8,256,512]{2,1,0:T(8,128)(2,1)} %bitcast.72), calls=%async_computation.2 | async-start | bytes 4194304 | tf_op jit(solution)/shard_map/all_to_all | solution.py:50
  66.5 71.5 %all-gather.5.cloned.1.call-start = ((), (), s32[]{:S(2)}) async-start(), calls=%async_computation.7 | async-start | bytes 2359296 | tf_op jit(solution)/shard_map/all_gather | solution.py:71
  68.3 2.6 %copy-start.10 = (bf16[256,512]{1,0:T(8,128)(2,1)S(1)}, bf16[256,512]{1,0:T(8,128)(2,1)}, u32[]{:S(2)}) copy-start(bf16[256,512]{1,0:T(8,128)(2,1)} %param.5) | copy-start | bytes 786436
  69.6 1.5 copy-start.5
  69.6 1.5 copy-start.7
  96.6 3.2 %collective-permute-start.3 = (bf16[8,128,256]{2,1,0:T(8,128)(2,1)S(1)}, bf16[8,128,256]{2,1,0:T(8,128)(2,1)S(1)}, u32[]{:S(2)}, u32[]{:S(2)}) collective-permute-start(bf16[8,128,256]{2,1,0:T(8,128)(2,1)S(1)} %fusion.18), channel_id=1, source_target_pairs={{0,1},{1,0},{2,3},{3,2},{4,5},{5,4},{6,7},{7,6},{8,9},{9,8},{10,11... | collective-permute-start | bytes 1572872 | tf_op jit(solution)/shard_map/ppermute | solution.py:32
  98.2 9.5 %collective-permute-start.4 = (bf16[256,512]{1,0:T(8,128)(2,1)S(1)}, bf16[256,512]{1,0:T(8,128)(2,1)S(1)}, u32[]{:S(2)}, u32[]{:S(2)}) collective-permute-start(bf16[256,512]{1,0:T(8,128)(2,1)S(1)} %reduce_sum.37), channel_id=1, source_target_pairs={{0,16},{16,0},{32,48},{48,32},{64,80},{80,64},{96,112},{112,96},{1... | collective-permute-start | bytes 786440 | tf_op jit(solution)/shard_map/ppermute | solution.py:32
  100.8 25.6 %all-to-all-start.3 = ((bf16[8,128,256]{2,1,0:T(8,128)(2,1)}), bf16[8,128,256]{2,1,0:T(8,128)(2,1)S(1)}, u32[]{:S(2)}, u32[]{:S(2)}) async-start(bf16[8,128,256]{2,1,0:T(8,128)(2,1)} %fusion.17), calls=%async_computation.3 | async-start | bytes 1048576 | tf_op jit(solution)/shard_map/all_to_all | solution.py:50
  108.8 24.8 %collective-permute-start.5 = (bf16[512,512]{1,0:T(8,128)(2,1)}, bf16[512,512]{1,0:T(8,128)(2,1)}, u32[]{:S(2)}, u32[]{:S(2)}) collective-permute-start(bf16[512,512]{1,0:T(8,128)(2,1)} %get-tuple-element.33), channel_id=1, source_target_pairs={{0,96},{16,112},{32,0},{48,16},{64,32},{80,48},{96,64},{112,80},{1... | collective-permute-start | bytes 1572872 | tf_op jit(solution)/shard_map/ppermute | solution.py:32
  110.0 24.7 %collective-permute-start.6 = (bf16[512,512]{1,0:T(8,128)(2,1)}, bf16[512,512]{1,0:T(8,128)(2,1)}, u32[]{:S(2)}, u32[]{:S(2)}) collective-permute-start(bf16[512,512]{1,0:T(8,128)(2,1)} %get-tuple-element.33), channel_id=1, source_target_pairs={{0,64},{16,80},{32,96},{48,112},{64,0},{80,16},{96,32},{112,48},{1... | collective-permute-start | bytes 1572872 | tf_op jit(solution)/shard_map/ppermute | solution.py:32
  110.5 26.4 %collective-permute-start.7 = (bf16[512,512]{1,0:T(8,128)(2,1)}, bf16[512,512]{1,0:T(8,128)(2,1)}, u32[]{:S(2)}, u32[]{:S(2)}) collective-permute-start(bf16[512,512]{1,0:T(8,128)(2,1)} %get-tuple-element.33), channel_id=1, source_target_pairs={{0,32},{16,48},{32,64},{48,80},{64,96},{80,112},{96,0},{112,16},{1... | collective-permute-start | bytes 1572872 | tf_op jit(solution)/shard_map/ppermute | solution.py:32
  127.3 15.3 %all-to-all-start.4 = ((bf16[16,64,256]{2,1,0:T(8,128)(2,1)}), bf16[16,64,256]{2,1,0:T(8,128)(2,1)S(1)}, u32[]{:S(2)}, u32[]{:S(2)}) async-start(bf16[16,64,256]{2,1,0:T(8,128)(2,1)} %broadcast_in_dim.13), calls=%async_computation.4 | async-start | bytes 1048576 | tf_op jit(solution)/shard_map/all_to_all | solution.py:50
  142.6 20.1 %collective-permute-start.8 = (bf16[1024,1024]{0,1:T(8,128)(2,1)}, bf16[1024,1024]{0,1:T(8,128)(2,1)}, u32[]{:S(2)}, u32[]{:S(2)}) collective-permute-start(bf16[1024,1024]{0,1:T(8,128)(2,1)} %all-gather.5.cloned.1.call-done), channel_id=1, source_target_pairs={{0,1},{1,0},{2,3},{3,2},{4,5},{5,4},{6,7},{7,6},{8,9},{9,8},{10,11... | collective-permute-start | bytes 6291464 | tf_op jit(solution)/shard_map/ppermute | solution.py:32
  145.6 7.0 %copy-start.6 = (bf16[512,512]{1,0:T(8,128)(2,1)S(1)}, bf16[512,512]{1,0:T(8,128)(2,1)}, u32[]{:S(2)}) copy-start(bf16[512,512]{1,0:T(8,128)(2,1)} %copy-done.5) | copy-start | bytes 1572868
  145.6 7.0 %copy-start.8 = (bf16[512,512]{1,0:T(8,128)(2,1)S(1)}, bf16[512,512]{1,0:T(8,128)(2,1)}, u32[]{:S(2)}) copy-start(bf16[512,512]{1,0:T(8,128)(2,1)} %copy-done.7) | copy-start | bytes 1572868
  147.3 7.5 %copy-start.1 = (bf16[512,1024]{1,0:T(8,128)(2,1)}, bf16[512,1024]{1,0:T(8,128)(2,1)S(1)}, u32[]{:S(2)}) copy-start(bf16[512,1024]{1,0:T(8,128)(2,1)S(1)} %get-tuple-element.27) | copy-start | bytes 3145732
  147.3 7.5 %copy-start.3 = (bf16[512,1024]{1,0:T(8,128)(2,1)}, bf16[512,1024]{1,0:T(8,128)(2,1)S(1)}, u32[]{:S(2)}) copy-start(bf16[512,1024]{1,0:T(8,128)(2,1)S(1)} %get-tuple-element.28) | copy-start | bytes 3145732
  147.4 7.4 %collective-permute-start.10 = (bf16[32,256]{1,0:T(8,128)(2,1)S(1)}, bf16[32,256]{1,0:T(8,128)(2,1)S(1)}, u32[]{:S(2)}, u32[]{:S(2)}) collective-permute-start(bf16[32,256]{1,0:T(8,128)(2,1)S(1)} %get-tuple-element.39), channel_id=1, source_target_pairs={{0,0},{16,32},{32,64},{48,96},{64,128},{80,160},{96,192},{112,224}... | collective-permute-start | bytes 49160 | tf_op jit(solution)/shard_map/ppermute | solution.py:32
  148.0 6.8 %collective-permute-start.11 = (bf16[32,256]{1,0:T(8,128)(2,1)S(1)}, bf16[32,256]{1,0:T(8,128)(2,1)S(1)}, u32[]{:S(2)}, u32[]{:S(2)}) collective-permute-start(bf16[32,256]{1,0:T(8,128)(2,1)S(1)} %get-tuple-element.40), channel_id=1, source_target_pairs={{0,16},{16,48},{32,80},{48,112},{64,144},{80,176},{96,208},{112,24... | collective-permute-start | bytes 49160 | tf_op jit(solution)/shard_map/ppermute | solution.py:32
  158.0 37.6 %all-to-all-start.5 = ((bf16[16,64,384]{2,1,0:T(8,128)(2,1)}), bf16[16,64,384]{2,1,0:T(8,128)(2,1)}, u32[]{:S(2)}, u32[]{:S(2)}) async-start(bf16[16,64,384]{2,1,0:T(8,128)(2,1)} %pad_maximum_fusion.8), calls=%async_computation.5 | async-start | bytes 1572864 | tf_op jit(solution)/shard_map/all_to_all | solution.py:50
  167.7 26.6 %collective-permute-start.12 = (bf16[512,512]{1,0:T(8,128)(2,1)S(1)}, bf16[512,512]{1,0:T(8,128)(2,1)S(1)}, u32[]{:S(2)}, u32[]{:S(2)}) collective-permute-start(bf16[512,512]{1,0:T(8,128)(2,1)S(1)} %fusion.13), channel_id=1, source_target_pairs={{0,128},{128,0},{1,129},{129,1},{2,130},{130,2},{3,131},{131,3},{4... | collective-permute-start | bytes 1572872 | tf_op jit(solution)/shard_map/ppermute | solution.py:32
  169.2 25.2 %collective-permute-start.13 = (bf16[512,512]{1,0:T(8,128)(2,1)S(1)}, bf16[512,512]{1,0:T(8,128)(2,1)S(1)}, u32[]{:S(2)}, u32[]{:S(2)}) collective-permute-start(bf16[512,512]{1,0:T(8,128)(2,1)S(1)} %fusion.10), channel_id=1, source_target_pairs={{0,128},{128,0},{1,129},{129,1},{2,130},{130,2},{3,131},{131,3},{4... | collective-permute-start | bytes 1572872 | tf_op jit(solution)/shard_map/ppermute | solution.py:32
  169.3 2.9 %copy-start.2 = (bf16[512,1024]{1,0:T(8,128)(2,1)S(1)}, bf16[512,1024]{1,0:T(8,128)(2,1)}, u32[]{:S(2)}) copy-start(bf16[512,1024]{1,0:T(8,128)(2,1)} %copy-done.1) | copy-start | bytes 3145732
  169.3 2.9 %copy-start.4 = (bf16[512,1024]{1,0:T(8,128)(2,1)S(1)}, bf16[512,1024]{1,0:T(8,128)(2,1)}, u32[]{:S(2)}) copy-start(bf16[512,1024]{1,0:T(8,128)(2,1)} %copy-done.3) | copy-start | bytes 3145732
  170.7 22.9 %collective-permute-start.9 = (bf16[32,1024]{1,0:T(8,128)(2,1)S(1)}, bf16[32,1024]{1,0:T(8,128)(2,1)S(1)}, u32[]{:S(2)}, u32[]{:S(2)}) collective-permute-start(bf16[32,1024]{1,0:T(8,128)(2,1)S(1)} %constant_dynamic-slice_fusion), channel_id=1, source_target_pairs={{0,128},{128,0},{1,129},{129,1},{2,130},{130,2},{3,131},{131,3},{4... | collective-permute-start | bytes 196616 | tf_op jit(solution)/shard_map/ppermute | solution.py:32
Sparse Core Ops, SparseCore 0:
  10.4 38.1 all-gather.2
  69.6 51.6 all-gather.4

commit v3 on v2

--- a/solution.py
+++ b/solution.py
@@ -53,8 +53,9 @@
         got = exchange(x, axis).reshape(size, -1, x.shape[1])
         return got.astype(F32).sum(0).astype(BF)
 
-    def gather(x, axis, size):
-        return exchange(jnp.broadcast_to(x, (size,) + x.shape).reshape(-1, x.shape[1]), axis)
+    def gather(x, axis, size, groups=None):
+        copies = jnp.broadcast_to(x, (size,) + x.shape).reshape(-1, x.shape[1])
+        return exchange(copies, axis, groups)
 
     def assemble(pieces, first):
         n = pieces[0].shape[0]
@@ -70,8 +71,7 @@
     def z_gather(x):
         return lax.all_gather(x, "col", axis=0, tiled=True, axis_index_groups=z_rings)
 
-    def both_cores(own):
-        other = core(own)
+    def by_core(own, other):
         low = jnp.where(core_id == 0, own, other)
         high = jnp.where(core_id == 0, other, own)
         return jnp.concatenate([low, high], 0)
@@ -89,14 +89,19 @@
 
     n_w = small_w.shape[0] // 2
     w_half = rows(small_w, d * n_w, n_w)
-    w_own = z_gather(w_half)
-    q_mine = scatter_sum(dot(cotangent, grow_a, 1, 0).astype(BF), "row", n_row)
-    q = gather(q_mine, "row", n_row)
-    x_other, c_other = x_pair(inputs), other_dp(cotangent)
-    w_own, q, x_other, c_other = lax.optimization_barrier(
-        (w_own, q, x_other, c_other)
-    )
-    w_all = both_cores(w_own)
+    w_own = gather(w_half, "col", n_z, z_rings)
+    q_part = dot(cotangent, grow_a, 1, 0).astype(BF)
+    q = q_part.astype(F32)
+    for k in range(1, n_row // 2):
+        q = q + from_y(q_part, k).astype(F32)
+    q = q.astype(BF)
+    q = total(q, x_far(q))
+    n_c = cotangent.shape[0] // 2
+    c_piece = other_dp(rows(cotangent, core_id * n_c, n_c))
+    w_own, q, x_other, c_piece = lax.optimization_barrier(
+        (w_own, q, x_pair(inputs), c_piece)
+    )
+    w_all = by_core(w_own, core(w_own))
 
     tok = inputs.shape[0] // n_col
     x_all = by_dp(inputs, x_other)
@@ -107,13 +112,15 @@
     a_half, _ = lax.optimization_barrier((a_half, w_own))
     a_own = z_gather(a_half)
     m_slice = scatter_sum(part, "row", n_row)
+    c_all = by_dp(cotangent, by_core(c_piece, core(c_piece)))
+    m_slice, c_all = lax.optimization_barrier((m_slice, c_all))
+    grad_weight = dot(c_all, x_all, 0, 0).astype(BF)
     x_hi = lax.axis_index("row") % 2
     m_other = x_far(m_slice)
     m_pair = jnp.concatenate(
         [jnp.where(x_hi == 0, m_slice, m_other), jnp.where(x_hi == 0, m_other, m_slice)], 0
     )
     m_pieces = [m_pair] + [from_y(m_pair, k) for k in range(1, n_row // 2)]
-    m_all = assemble(m_pieces, lax.axis_index("row") // 2)
 
     r_part = dot(q, small_w, 1, 0).astype(BF)
     n_k = r_part.shape[1] // 2
@@ -131,25 +138,39 @@
     send = jnp.where(core_id == 0, both[:, 1], both[:, 0])
     both = total(keep, core(send)).reshape(-1, n_s)
     both = exchange(both, "col", z_rings).reshape(n_z, -1, n_s)
+    both, a_own, grad_weight, *m_pieces = lax.optimization_barrier(
+        (both, a_own, grad_weight, *m_pieces)
+    )
+    n_y = n_row // 2
+    m_all = assemble(m_pieces, lax.axis_index("row") // 2 + core_id * (n_y // 2))
     both = both.astype(F32).sum(0).astype(BF)
     low, high, v_mine = both[:tok], both[tok : 2 * tok], both[2 * tok :]
 
-    def move(x, parity):
-        def target(i):
-            a, b = divmod(i, n_row)
-            return 2 * b + (a ^ parity)
-
-        return permute(x, ("dp", "row"), n_dp * n_row, target)
-
-    same = move(jnp.where(d == 0, low, high), 0)
-    swap = move(jnp.where(d == 0, high, low), 1)
-    r_piece = jnp.concatenate(
-        [jnp.where(x_hi == 0, same, swap), jnp.where(x_hi == 0, swap, same)], 0
-    )
-    v_both = gather(v_mine, ("dp", "row"), n_dp * n_row)
-    v_both, m_all, a_own = lax.optimization_barrier((v_both, m_all, a_own))
-    c_all = by_dp(cotangent, c_other)
-    v_both = v_both.reshape(n_dp, n_row, n_dp * tok, n_s)
+    places = n_dp * n_row
+    r_low_high = jnp.stack([low, high])
+    sent = jnp.concatenate(
+        [
+            jnp.broadcast_to(v_mine, (places,) + v_mine.shape),
+            jnp.broadcast_to(r_low_high, (places // 2,) + r_low_high.shape).reshape(
+                places, tok, n_k
+            ),
+        ],
+        1,
+    )
+    got = exchange(sent.reshape(-1, n_s), ("dp", "row"))
+    a_other = core(a_own)
+    depth = a_own.shape[0]
+    parts = []
+    for cut in (slice(0, a_own.shape[1] // 4), slice(a_own.shape[1] // 4, None)):
+        part = dot(a_own[:, cut], m_all[:depth], 0, 0)
+        part = part + dot(a_other[:, cut], m_all[depth:], 0, 0)
+        parts.append(part.astype(BF))
+    got, first, *parts = lax.optimization_barrier((got, other_dp(parts[0]), *parts))
+    got = got.reshape(n_dp, n_row, (n_dp + 1) * tok, n_s)
+    v_both = got[:, :, : n_dp * tok]
+    source = d * (n_row // 2) + lax.axis_index("row") // 2
+    r_piece = lax.dynamic_slice(got, (0, source, n_dp * tok, 0), (n_dp, 1, tok, n_k))
+    r_piece = r_piece.reshape(n_dp * tok, n_k)
     v = lax.dynamic_index_in_dim(v_both, d, 0, keepdims=False)
     v = v.transpose(1, 0, 2).reshape(n_dp * tok, n_row * n_s)
 
@@ -159,22 +180,20 @@
     r_rep = jnp.broadcast_to(r_piece, (n_col,) + r_piece.shape)
     sent = jnp.concatenate([r_rep, v_cols], 2).reshape(-1, n_k + n_w)
     got = exchange(sent, "col")
-    a_all = both_cores(a_own)
-    n = grow_a.shape[0] // 2
-    parts = [
-        dot(a_all[:, i * n : (i + 1) * n], m_all, 0, 0).astype(BF) for i in range(2)
-    ]
-    big_weight = jnp.concatenate([total(p, other_dp(p)) for p in parts], 0)
+    second = other_dp(parts[1])
+    big_weight = jnp.concatenate([total(parts[0], first), total(parts[1], second)], 0)
     got, big_weight = lax.optimization_barrier((got, big_weight))
     grad_b = dot(x_all, got[:, :n_k], 0, 0)
     grad_a = dot(c_all, got[:, n_k:], 0, 0)
 
-    y_part = dot(v, a_all, 1, 0).astype(BF)
+    low, high = v[:, :depth], v[:, depth:]
+    v_own = jnp.where(core_id == 0, low, high)
+    v_rest = jnp.where(core_id == 0, high, low)
+    y_part = (dot(v_own, a_own, 1, 0) + dot(v_rest, a_other, 1, 0)).astype(BF)
     outputs = total(
         rows(y_part, d * tok, tok), other_dp(rows(y_part, (1 - d) * tok, tok))
     )
 
-    grad_weight = dot(c_all, x_all, 0, 0).astype(BF)
     return outputs, big_weight, grad_weight, grad_a, grad_b
 
 

time: 209 us -> 204 us (0.976)
  blocking collectives: 36.8 us -> 0 us
  waiting for transfers between devices: 69.6 us -> 85.8 us
  starting transfers between devices: 44.4 us -> 50.9 us
  matrix products: 17.7 us -> 23.7 us
  other arithmetic: 15.7 us -> 18 us
    all_to_all x2 -> x0, blocking collectives: 36.8 us -> none  [exchange(): return lax.all_to_all(x, axis, 0, 0, tiled=True, axis_index_groups=groups)]
    ppermute x14 -> x17, waiting for transfers between devices: 25.9 us -> 50 us  [permute(): return lax.ppermute(x, axis, [(i, target(i)) for i in range(size)])]
    all_to_all x4 -> x5, starting transfers between devices: 22.5 us -> 31.2 us  [exchange(): return lax.all_to_all(x, axis, 0, 0, tiled=True, axis_index_groups=groups)]
    all_to_all x4 -> x5, waiting for transfers between devices: 43.6 us -> 35.8 us  [exchange(): return lax.all_to_all(x, axis, 0, 0, tiled=True, axis_index_groups=groups)]
    dot_general x10 -> x13, matrix products: 17.7 us -> 23.7 us  [dot(): lax.dot_general(a, b, (((da,), (db,)), ((), ())), preferred_element_type=...]
    convert_element_type x4 -> x5, other arithmetic: 1.94 us -> 4.17 us  [total(): return (a.astype(F32) + b.astype(F32)).astype(BF)]
    ppermute x14 -> x17, starting transfers between devices: 21.9 us -> 19.7 us  [permute(): return lax.ppermute(x, axis, [(i, target(i)) for i in range(size)])]
  transfers between devices with their start and end apart: 20 -> 23, of which waited for: 7 -> 15; matrix products, arithmetic and copies ran while one was open for 15% -> 19% of each run, Pallas kernels for 0% -> 0%
where the time goes in v3:
time: 204 us; the launch traced here: 203 us
  waiting for transfers between devices  85.8 us (42%)
  starting transfers between devices  50.9 us (25%)
  matrix products  23.7 us (12%)
  other arithmetic  18 us (9%)
  between operations  14.4 us (7%)
  local copies, waits for them, and re-layouts  9.71 us (5%)
    ppermute x17, waiting for transfers between devices, permute(): return lax.ppermute(x, axis, [(i, target(i)) for i in range(size)])  50 us
    all_to_all x5, waiting for transfers between devices, exchange(): return lax.all_to_all(x, axis, 0, 0, tiled=True, axis_index_groups=groups)  35.8 us
    all_to_all x5, starting transfers between devices, exchange(): return lax.all_to_all(x, axis, 0, 0, tiled=True, axis_index_groups=groups)  31.2 us
    dot_general x13, matrix products, dot(): lax.dot_general(a, b, (((da,), (db,)), ((), ())), preferred_element_type=...  23.7 us
    ppermute x17, starting transfers between devices, permute(): return lax.ppermute(x, axis, [(i, target(i)) for i in range(size)])  19.7 us
    convert_element_type x5, other arithmetic, total(): return (a.astype(F32) + b.astype(F32)).astype(BF)  4.17 us
  transfers between devices with their start and end apart: 23, of which 15 were waited for; matrix products, arithmetic and copies ran while one was open for 19% of the time, Pallas kernels for 0%

profile of v3, /device:TPU:1, one launch (start us, length us, event | category | flops | bytes accessed | tf_op | source)
XLA Modules:
  0.0 202.6 jit_solution(15183635375238814712)
XLA Ops:
  9.3 9.1 %all-to-all-start = ((bf16[8,128,512]{2,1,0:T(8,128)(2,1)}), bf16[8,128,512]{2,1,0:T(8,128)(2,1)S(1)}, u32[]{:S(2)}, u32[]{:S(2)}) async-start(bf16[8,128,512]{2,1,0:T(8,128)(2,1)} %broadcast_in_dim.15), calls=%async_computation | async-start | bytes 2097152 | tf_op jit(solution)/shard_map/all_to_all | solution.py:50
  18.4 1.5 convolution_convert_fusion.4
  19.9 2.8 %collective-permute-start = (bf16[512,256]{1,0:T(8,128)(2,1)S(1)}, bf16[512,256]{1,0:T(8,128)(2,1)}, u32[]{:S(2)}, u32[]{:S(2)}) collective-permute-start(bf16[512,256]{1,0:T(8,128)(2,1)S(1)} %convolution_convert_fusion.4), channel_id=1, source_target_pairs={{0,96},{16,112},{32,0},{48,16},{64,32},{80,48},{96,64},{112,80},{1... | collective-permute-start | bytes 786440 | tf_op jit(solution)/shard_map/ppermute | solution.py:32
  23.8 1.3 collective-permute-start.5
  25.1 1.8 collective-permute-start.4
  26.9 1.5 collective-permute-done
  28.5 2.5 %collective-permute-done.1 = bf16[512,256]{1,0:T(8,128)(2,1)} collective-permute-done((bf16[512,256]{1,0:T(8,128)(2,1)S(1)}, bf16[512,256]{1,0:T(8,128)(2,1)}, u32[]{:S(2)}, u32[]{:S(2)}) %collective-permute-start.1) | collective-permute-done | bytes 262176 | tf_op jit(solution)/shard_map/ppermute | solution.py:32
  31.0 7.2 %collective-permute-done.2 = bf16[512,256]{1,0:T(8,128)(2,1)} collective-permute-done((bf16[512,256]{1,0:T(8,128)(2,1)S(1)}, bf16[512,256]{1,0:T(8,128)(2,1)}, u32[]{:S(2)}, u32[]{:S(2)}) %collective-permute-start.2) | collective-permute-done | bytes 262176 | tf_op jit(solution)/shard_map/ppermute | solution.py:32
  38.2 1.2 add_convert_fusion.4
  39.4 2.8 %collective-permute-start.3 = (bf16[512,256]{1,0:T(8,128)(2,1)S(1)}, bf16[512,256]{1,0:T(8,128)(2,1)S(1)}, u32[]{:S(2)}, u32[]{:S(2)}) collective-permute-start(bf16[512,256]{1,0:T(8,128)(2,1)S(1)} %add_convert_fusion.4), channel_id=1, source_target_pairs={{0,16},{16,0},{32,48},{48,32},{64,80},{80,64},{96,112},{112,96},{1... | collective-permute-start | bytes 786440 | tf_op jit(solution)/shard_map/ppermute | solution.py:32
  42.3 6.1 %collective-permute-done.3 = bf16[512,256]{1,0:T(8,128)(2,1)S(1)} collective-permute-done((bf16[512,256]{1,0:T(8,128)(2,1)S(1)}, bf16[512,256]{1,0:T(8,128)(2,1)S(1)}, u32[]{:S(2)}, u32[]{:S(2)}) %collective-permute-start.3) | collective-permute-done | bytes 262176 | tf_op jit(solution)/shard_map/ppermute | solution.py:32
  48.5 1.4 collective-permute-start.6
  49.9 2.4 %collective-permute-done.6 = bf16[1024,512]{1,0:T(8,128)(2,1)} collective-permute-done((bf16[1024,512]{1,0:T(8,128)(2,1)S(1)}, bf16[1024,512]{1,0:T(8,128)(2,1)}, u32[]{:S(2)}, u32[]{:S(2)}) %collective-permute-start.6) | collective-permute-done | bytes 1048608 | tf_op jit(solution)/shard_map/ppermute | solution.py:32
  52.4 1.4 broadcast_select_fusion.3
  53.7 2.7 %convolution_convert_fusion = bf16[2048,512]{1,0:T(8,128)(2,1)} fusion(bf16[512,512]{1,0:T(8,128)(2,1)S(1)} %copy-done, bf16[1024,512]{1,0:T(8,128)(2,1)S(1)} %get-tuple-element.48, bf16[1024,512]{1,0:T(8,128)(2,1)S(1)} %get-tuple-element.47), kind=kOutput, calls=%fused_computation | convolution fusion | flops 1078984704 | bytes 4718592 | tf_op jit(solution)/shard_map/dot_general | solution.py:11
  56.4 5.0 %all-to-all-start.1 = ((bf16[8,256,512]{2,1,0:T(8,128)(2,1)}), bf16[8,256,512]{2,1,0:T(8,128)(2,1)}, u32[]{:S(2)}, u32[]{:S(2)}) async-start(bf16[8,256,512]{2,1,0:T(8,128)(2,1)} %bitcast.78), calls=%async_computation.1 | async-start | bytes 4194304 | tf_op jit(solution)/shard_map/all_to_all | solution.py:50
  62.9 1.2 broadcast_select_fusion.7
  64.0 1.1 pad_maximum_fusion.1
  65.5 1.3 broadcast_select_fusion.5
  67.5 21.8 %all-to-all-done.1 = bf16[8,256,512]{2,1,0:T(8,128)(2,1)} async-done(((bf16[8,256,512]{2,1,0:T(8,128)(2,1)}), bf16[8,256,512]{2,1,0:T(8,128)(2,1)}, u32[]{:S(2)}, u32[]{:S(2)}) %all-to-all-start.1) | async-done | bytes 2097184 | tf_op jit(solution)/shard_map/all_to_all | solution.py:50
  89.4 2.0 reduce_sum.24
  91.4 1.7 convolution_convert_fusion.2
  93.2 1.6 collective-permute-start.8
  97.4 6.1 %all-to-all-start.2 = ((bf16[8,128,256]{2,1,0:T(8,128)(2,1)}), bf16[8,128,256]{2,1,0:T(8,128)(2,1)S(1)}, u32[]{:S(2)}, u32[]{:S(2)}) async-start(bf16[8,128,256]{2,1,0:T(8,128)(2,1)} %fusion.11), calls=%async_computation.2 | async-start | bytes 1048576 | tf_op jit(solution)/shard_map/all_to_all | solution.py:50
  105.4 1.2 collective-permute-start.10
  107.5 2.3 %convolution_convert_fusion.1 = bf16[1024,512]{1,0:T(8,128)(2,1)} fusion(bf16[1024,1024]{1,0:T(8,128)(2,1)S(1)} %bitcast.67, bf16[1024,512]{1,0:T(8,128)(2,1)S(1)} %bitcast.73), kind=kOutput, calls=%fused_computation.11 | convolution fusion | flops 1074266112 | bytes 4194304 | tf_op jit(solution)/shard_map/dot_general | solution.py:11
  109.8 8.4 %collective-permute-done.10 = bf16[512,512]{1,0:T(8,128)(2,1)S(1)} collective-permute-done((bf16[512,512]{1,0:T(8,128)(2,1)S(1)}, bf16[512,512]{1,0:T(8,128)(2,1)S(1)}, u32[]{:S(2)}, u32[]{:S(2)}) %collective-permute-start.10) | collective-permute-done | bytes 524320 | tf_op jit(solution)/shard_map/ppermute | solution.py:32
  118.1 2.3 %collective-permute-done.11 = bf16[512,512]{1,0:T(8,128)(2,1)S(1)} collective-permute-done((bf16[512,512]{1,0:T(8,128)(2,1)S(1)}, bf16[512,512]{1,0:T(8,128)(2,1)S(1)}, u32[]{:S(2)}, u32[]{:S(2)}) %collective-permute-start.11) | collective-permute-done | bytes 524320 | tf_op jit(solution)/shard_map/ppermute | solution.py:32
  121.2 12.1 %collective-permute-done.12 = bf16[512,512]{1,0:T(8,128)(2,1)} collective-permute-done((bf16[512,512]{1,0:T(8,128)(2,1)S(1)}, bf16[512,512]{1,0:T(8,128)(2,1)}, u32[]{:S(2)}, u32[]{:S(2)}) %collective-permute-start.12) | collective-permute-done | bytes 524320 | tf_op jit(solution)/shard_map/ppermute | solution.py:32
  135.0 3.6 %all-to-all-start.3 = ((bf16[16,96,256]{2,1,0:T(8,128)(2,1)}), bf16[16,96,256]{2,1,0:T(8,128)(2,1)S(1)}, u32[]{:S(2)}, u32[]{:S(2)}) async-start(bf16[16,96,256]{2,1,0:T(8,128)(2,1)} %pad_maximum_fusion.5), calls=%async_computation.3 | async-start | bytes 1572864 | tf_op jit(solution)/shard_map/all_to_all | solution.py:50
  140.0 1.2 constant_dynamic-update-slice_fusion
  141.2 1.5 fusion.13
  142.7 1.1 fusion.9
  143.9 1.3 collective-permute-start.14
  145.2 2.4 %fusion.3 = f32[768,512]{1,0:T(8,128)S(1)} fusion(bf16[1024,1024]{0,1:T(8,128)(2,1)} %collective-permute-done.13, bf16[2048,512]{1,0:T(8,128)(2,1)S(1)} %constant_dynamic-update-slice_fusion), kind=kOutput, calls=%fused_computation.5 | convolution fusion | flops 805306368 | bytes 4194304 | tf_op jit(solution)/shard_map/dot_general | solution.py:11
  147.6 1.9 add_convert_fusion.1
  149.4 2.0 all-to-all-done.3
  151.4 3.5 %collective-permute-done.14 = bf16[256,512]{1,0:T(8,128)(2,1)} collective-permute-done((bf16[256,512]{1,0:T(8,128)(2,1)}, bf16[256,512]{1,0:T(8,128)(2,1)}, u32[]{:S(2)}, u32[]{:S(2)}) %collective-permute-start.14) | collective-permute-done | bytes 262176 | tf_op jit(solution)/shard_map/ppermute | solution.py:32
  157.5 1.1 constant_dynamic-slice_fusion
  160.5 7.4 %all-to-all-start.4 = ((bf16[16,64,384]{2,1,0:T(8,128)(2,1)}), bf16[16,64,384]{2,1,0:T(8,128)(2,1)}, u32[]{:S(2)}, u32[]{:S(2)}) async-start(bf16[16,64,384]{2,1,0:T(8,128)(2,1)} %pad_maximum_fusion.6), calls=%async_computation.4 | async-start | bytes 1572864 | tf_op jit(solution)/shard_map/all_to_all | solution.py:50
  168.0 2.5 %fusion.25 = f32[64,1024]{1,0:T(8,128)S(1)} fusion(bf16[1024,1024]{0,1:T(8,128)(2,1)} %collective-permute-done.13, pred[]{:T(512)S(6)} %eq.13, bf16[64,2048]{1,0:T(8,128)(2,1)S(1)} %bitcast.84), kind=kOutput, calls=%fused_computation.59 | convolution fusion | flops 134283264 | bytes 2621441 | tf_op jit(solution)/shard_map/dot_general | solution.py:11
  171.3 1.3 collective-permute-start.15
  172.5 1.1 add_convert_fusion.2
  173.6 2.0 collective-permute-done.15
  176.3 1.4 add_convert_fusion
  178.7 12.0 %all-to-all-done.4 = bf16[16,64,384]{2,1,0:T(8,128)(2,1)} async-done(((bf16[16,64,384]{2,1,0:T(8,128)(2,1)}), bf16[16,64,384]{2,1,0:T(8,128)(2,1)}, u32[]{:S(2)}, u32[]{:S(2)}) %all-to-all-start.4) | async-done | bytes 786464 | tf_op jit(solution)/shard_map/all_to_all | solution.py:50
  190.7 2.6 %fusion.20 = f32[512,256]{1,0:T(8,128)} fusion(bf16[1024,512]{1,0:T(8,128)(2,1)} %bitcast.72, bf16[1024,384]{1,0:T(8,128)(2,1)} %bitcast.27), kind=kOutput, calls=%fused_computation.42 | convolution fusion | flops 268435456 | bytes 2097152 | tf_op jit(solution)/shard_map/dot_general | solution.py:11
  193.3 2.5 %fusion.23 = f32[1024,128]{1,0:T(8,128)} fusion(bf16[1024,1024]{1,0:T(8,128)(2,1)S(1)} %bitcast.68, bf16[1024,384]{1,0:T(8,128)(2,1)} %bitcast.27), kind=kOutput, calls=%fused_computation.52 | convolution fusion | flops 268435456 | bytes 2883584 | tf_op jit(solution)/shard_map/dot_general | solution.py:11
  (89 shorter events, 21.9 us)
Async XLA Ops:
  7.2 46.6 %copy-start = (bf16[512,512]{1,0:T(8,128)(2,1)S(1)}, bf16[512,512]{1,0:T(8,128)(2,1)}, u32[]{:S(2)}) copy-start(bf16[512,512]{1,0:T(8,128)(2,1)} %param.7) | copy-start | bytes 1572868
  7.2 11.3 %copy-start.2 = (bf16[512,1024]{1,0:T(8,128)(2,1)S(1)}, bf16[512,1024]{1,0:T(8,128)(2,1)}, u32[]{:S(2)}) copy-start(bf16[512,1024]{1,0:T(8,128)(2,1)} %param.9) | copy-start | bytes 3145732
  9.3 15.8 %copy-start.10 = (bf16[512,512]{1,0:T(8,128)(2,1)S(1)}, bf16[512,512]{1,0:T(8,128)(2,1)}, u32[]{:S(2)}) copy-start(bf16[512,512]{1,0:T(8,128)(2,1)} %param.8) | copy-start | bytes 1572868
  9.3 39.2 %all-to-all-start = ((bf16[8,128,512]{2,1,0:T(8,128)(2,1)}), bf16[8,128,512]{2,1,0:T(8,128)(2,1)S(1)}, u32[]{:S(2)}, u32[]{:S(2)}) async-start(bf16[8,128,512]{2,1,0:T(8,128)(2,1)} %broadcast_in_dim.15), calls=%async_computation | async-start | bytes 2097152 | tf_op jit(solution)/shard_map/all_to_all | solution.py:50
  19.9 8.5 %collective-permute-start = (bf16[512,256]{1,0:T(8,128)(2,1)S(1)}, bf16[512,256]{1,0:T(8,128)(2,1)}, u32[]{:S(2)}, u32[]{:S(2)}) collective-permute-start(bf16[512,256]{1,0:T(8,128)(2,1)S(1)} %convolution_convert_fusion.4), channel_id=1, source_target_pairs={{0,96},{16,112},{32,0},{48,16},{64,32},{80,48},{96,64},{112,80},{1... | collective-permute-start | bytes 786440 | tf_op jit(solution)/shard_map/ppermute | solution.py:32
  22.7 8.2 %collective-permute-start.1 = (bf16[512,256]{1,0:T(8,128)(2,1)S(1)}, bf16[512,256]{1,0:T(8,128)(2,1)}, u32[]{:S(2)}, u32[]{:S(2)}) collective-permute-start(bf16[512,256]{1,0:T(8,128)(2,1)S(1)} %convolution_convert_fusion.4), channel_id=1, source_target_pairs={{0,64},{16,80},{32,96},{48,112},{64,0},{80,16},{96,32},{112,48},{1... | collective-permute-start | bytes 786440 | tf_op jit(solution)/shard_map/ppermute | solution.py:32
  23.1 15.1 %collective-permute-start.2 = (bf16[512,256]{1,0:T(8,128)(2,1)S(1)}, bf16[512,256]{1,0:T(8,128)(2,1)}, u32[]{:S(2)}, u32[]{:S(2)}) collective-permute-start(bf16[512,256]{1,0:T(8,128)(2,1)S(1)} %convolution_convert_fusion.4), channel_id=1, source_target_pairs={{0,32},{16,48},{32,64},{48,80},{64,96},{80,112},{96,0},{112,16},{1... | collective-permute-start | bytes 786440 | tf_op jit(solution)/shard_map/ppermute | solution.py:32
  23.8 24.7 %collective-permute-start.5 = (bf16[256,1024]{1,0:T(8,128)(2,1)S(1)}, bf16[256,1024]{1,0:T(8,128)(2,1)}, u32[]{:S(2)}, u32[]{:S(2)}) collective-permute-start(bf16[256,1024]{1,0:T(8,128)(2,1)S(1)} %constant_dynamic-slice_fusion.3), channel_id=1, source_target_pairs={{0,128},{128,0},{1,129},{129,1},{2,130},{130,2},{3,131},{131,3},{4... | collective-permute-start | bytes 1572872 | tf_op jit(solution)/shard_map/ppermute | solution.py:32
  25.1 23.4 %collective-permute-start.4 = (bf16[512,512]{1,0:T(8,128)(2,1)S(1)}, bf16[512,512]{1,0:T(8,128)(2,1)}, u32[]{:S(2)}, u32[]{:S(2)}) collective-permute-start(bf16[512,512]{1,0:T(8,128)(2,1)S(1)} %copy-done.10), channel_id=1, source_target_pairs={{0,144},{16,128},{32,176},{48,160},{64,208},{80,192},{96,240},{112... | collective-permute-start | bytes 1572872 | tf_op jit(solution)/shard_map/ppermute | solution.py:32
  39.4 9.0 %collective-permute-start.3 = (bf16[512,256]{1,0:T(8,128)(2,1)S(1)}, bf16[512,256]{1,0:T(8,128)(2,1)S(1)}, u32[]{:S(2)}, u32[]{:S(2)}) collective-permute-start(bf16[512,256]{1,0:T(8,128)(2,1)S(1)} %add_convert_fusion.4), channel_id=1, source_target_pairs={{0,16},{16,0},{32,48},{48,32},{64,80},{80,64},{96,112},{112,96},{1... | collective-permute-start | bytes 786440 | tf_op jit(solution)/shard_map/ppermute | solution.py:32
  48.5 3.8 %collective-permute-start.6 = (bf16[1024,512]{1,0:T(8,128)(2,1)S(1)}, bf16[1024,512]{1,0:T(8,128)(2,1)}, u32[]{:S(2)}, u32[]{:S(2)}) collective-permute-start(bf16[1024,512]{1,0:T(8,128)(2,1)S(1)} %bitcast.69), channel_id=1, source_target_pairs={{0,1},{1,0},{2,3},{3,2},{4,5},{5,4},{6,7},{7,6},{8,9},{9,8},{10,11... | collective-permute-start | bytes 3145736 | tf_op jit(solution)/shard_map/ppermute | solution.py:32
  56.4 5.0 %copy-start.11 = (bf16[1024,256]{1,0:T(8,128)(2,1)S(1)}, bf16[1024,256]{1,0:T(8,128)(2,1)}, u32[]{:S(2)}) copy-start(bf16[1024,256]{1,0:T(8,128)(2,1)} %param.6) | copy-start | bytes 1572868
  56.4 32.9 %all-to-all-start.1 = ((bf16[8,256,512]{2,1,0:T(8,128)(2,1)}), bf16[8,256,512]{2,1,0:T(8,128)(2,1)}, u32[]{:S(2)}, u32[]{:S(2)}) async-start(bf16[8,256,512]{2,1,0:T(8,128)(2,1)} %bitcast.78), calls=%async_computation.1 | async-start | bytes 4194304 | tf_op jit(solution)/shard_map/all_to_all | solution.py:50
  61.4 71.9 %all-gather.2.cloned.1.call-start = ((), (), s32[]{:S(2)}) async-start(), calls=%async_computation.5 | async-start | bytes 2359296 | tf_op jit(solution)/shard_map/all_gather | solution.py:72
  62.2 3.3 %collective-permute-start.7 = (bf16[256,1024]{1,0:T(8,128)(2,1)}, bf16[256,1024]{1,0:T(8,128)(2,1)}, u32[]{:S(2)}, u32[]{:S(2)}) collective-permute-start(bf16[256,1024]{1,0:T(8,128)(2,1)} %collective-permute-done.5), channel_id=1, source_target_pairs={{0,1},{1,0},{2,3},{3,2},{4,5},{5,4},{6,7},{7,6},{8,9},{9,8},{10,11... | collective-permute-start | bytes 1572872 | tf_op jit(solution)/shard_map/ppermute | solution.py:32
  62.9 2.3 %copy-start.9 = (bf16[256,512]{1,0:T(8,128)(2,1)S(1)}, bf16[256,512]{1,0:T(8,128)(2,1)}, u32[]{:S(2)}) copy-start(bf16[256,512]{1,0:T(8,128)(2,1)} %param.5) | copy-start | bytes 786436
  93.2 3.2 %collective-permute-start.8 = (bf16[8,128,256]{2,1,0:T(8,128)(2,1)S(1)}, bf16[8,128,256]{2,1,0:T(8,128)(2,1)S(1)}, u32[]{:S(2)}, u32[]{:S(2)}) collective-permute-start(bf16[8,128,256]{2,1,0:T(8,128)(2,1)S(1)} %fusion.17), channel_id=1, source_target_pairs={{0,1},{1,0},{2,3},{3,2},{4,5},{5,4},{6,7},{7,6},{8,9},{9,8},{10,11... | collective-permute-start | bytes 1572872 | tf_op jit(solution)/shard_map/ppermute | solution.py:32
  94.9 9.5 %collective-permute-start.9 = (bf16[256,512]{1,0:T(8,128)(2,1)S(1)}, bf16[256,512]{1,0:T(8,128)(2,1)}, u32[]{:S(2)}, u32[]{:S(2)}) collective-permute-start(bf16[256,512]{1,0:T(8,128)(2,1)S(1)} %reduce_sum.24), channel_id=1, source_target_pairs={{0,16},{16,0},{32,48},{48,32},{64,80},{80,64},{96,112},{112,96},{1... | collective-permute-start | bytes 786440 | tf_op jit(solution)/shard_map/ppermute | solution.py:32
  97.4 35.9 %all-to-all-start.2 = ((bf16[8,128,256]{2,1,0:T(8,128)(2,1)}), bf16[8,128,256]{2,1,0:T(8,128)(2,1)S(1)}, u32[]{:S(2)}, u32[]{:S(2)}) async-start(bf16[8,128,256]{2,1,0:T(8,128)(2,1)} %fusion.11), calls=%async_computation.2 | async-start | bytes 1048576 | tf_op jit(solution)/shard_map/all_to_all | solution.py:50
  103.5 4.0 %copy-start.1 = (bf16[16,2,32,512]{3,2,1,0:T(8,128)(2,1)S(1)}, bf16[16,2,32,512]{3,2,1,0:T(8,128)(2,1)}, u32[]{:S(2)}) copy-start(bf16[16,2,32,512]{3,2,1,0:T(8,128)(2,1)} %pad_maximum_fusion.1) | copy-start | bytes 3145732
  105.4 4.4 %copy-start.6 = (bf16[512,512]{1,0:T(8,128)(2,1)}, bf16[512,512]{1,0:T(8,128)(2,1)S(1)}, u32[]{:S(2)}) copy-start(bf16[512,512]{1,0:T(8,128)(2,1)S(1)} %pad_maximum_fusion.7) | copy-start | bytes 1572868
  105.4 12.7 %collective-permute-start.10 = (bf16[512,512]{1,0:T(8,128)(2,1)S(1)}, bf16[512,512]{1,0:T(8,128)(2,1)S(1)}, u32[]{:S(2)}, u32[]{:S(2)}) collective-permute-start(bf16[512,512]{1,0:T(8,128)(2,1)S(1)} %pad_maximum_fusion.7), channel_id=1, source_target_pairs={{0,96},{16,112},{32,0},{48,16},{64,32},{80,48},{96,64},{112,80},{1... | collective-permute-start | bytes 1572872 | tf_op jit(solution)/shard_map/ppermute | solution.py:32
  106.6 13.8 %collective-permute-start.11 = (bf16[512,512]{1,0:T(8,128)(2,1)S(1)}, bf16[512,512]{1,0:T(8,128)(2,1)S(1)}, u32[]{:S(2)}, u32[]{:S(2)}) collective-permute-start(bf16[512,512]{1,0:T(8,128)(2,1)S(1)} %pad_maximum_fusion.7), channel_id=1, source_target_pairs={{0,64},{16,80},{32,96},{48,112},{64,0},{80,16},{96,32},{112,48},{1... | collective-permute-start | bytes 1572872 | tf_op jit(solution)/shard_map/ppermute | solution.py:32
  107.2 26.1 %collective-permute-start.12 = (bf16[512,512]{1,0:T(8,128)(2,1)S(1)}, bf16[512,512]{1,0:T(8,128)(2,1)}, u32[]{:S(2)}, u32[]{:S(2)}) collective-permute-start(bf16[512,512]{1,0:T(8,128)(2,1)S(1)} %pad_maximum_fusion.7), channel_id=1, source_target_pairs={{0,32},{16,48},{32,64},{48,80},{64,96},{80,112},{96,0},{112,16},{1... | collective-permute-start | bytes 1572872 | tf_op jit(solution)/shard_map/ppermute | solution.py:32
  118.1 2.3 %copy-start.12 = (bf16[512,512]{1,0:T(8,128)(2,1)}, bf16[512,512]{1,0:T(8,128)(2,1)S(1)}, u32[]{:S(2)}) copy-start(bf16[512,512]{1,0:T(8,128)(2,1)S(1)} %collective-permute-done.10) | copy-start | bytes 1572868
  120.5 0.8 copy-start.14
  133.3 7.9 %collective-permute-start.13 = (bf16[1024,1024]{0,1:T(8,128)(2,1)}, bf16[1024,1024]{0,1:T(8,128)(2,1)}, u32[]{:S(2)}, u32[]{:S(2)}) collective-permute-start(bf16[1024,1024]{0,1:T(8,128)(2,1)} %all-gather.2.cloned.1.call-done), channel_id=1, source_target_pairs={{0,1},{1,0},{2,3},{3,2},{4,5},{5,4},{6,7},{7,6},{8,9},{9,8},{10,11... | collective-permute-start | bytes 6291464 | tf_op jit(solution)/shard_map/ppermute | solution.py:32
  135.0 16.4 %all-to-all-start.3 = ((bf16[16,96,256]{2,1,0:T(8,128)(2,1)}), bf16[16,96,256]{2,1,0:T(8,128)(2,1)S(1)}, u32[]{:S(2)}, u32[]{:S(2)}) async-start(bf16[16,96,256]{2,1,0:T(8,128)(2,1)} %pad_maximum_fusion.5), calls=%async_computation.3 | async-start | bytes 1572864 | tf_op jit(solution)/shard_map/all_to_all | solution.py:50
  138.6 1.0 copy-start.7
  138.6 1.2 copy-start.13
  138.6 1.3 copy-start.15
  140.0 2.8 %copy-start.4 = (bf16[1024,1024]{0,1:T(8,128)(2,1)S(1)}, bf16[1024,1024]{0,1:T(8,128)(2,1)}, u32[]{:S(2)}) copy-start(bf16[1024,1024]{0,1:T(8,128)(2,1)} %all-gather.2.cloned.1.call-done) | copy-start | bytes 6291460
  143.9 11.0 %collective-permute-start.14 = (bf16[256,512]{1,0:T(8,128)(2,1)}, bf16[256,512]{1,0:T(8,128)(2,1)}, u32[]{:S(2)}, u32[]{:S(2)}) collective-permute-start(bf16[256,512]{1,0:T(8,128)(2,1)} %fusion.9), channel_id=1, source_target_pairs={{0,128},{128,0},{1,129},{129,1},{2,130},{130,2},{3,131},{131,3},{4... | collective-permute-start | bytes 786440 | tf_op jit(solution)/shard_map/ppermute | solution.py:32
  151.4 4.1 %copy-start.3 = (bf16[16,96,256]{2,1,0:T(8,128)(2,1)}, bf16[16,96,256]{2,1,0:T(8,128)(2,1)S(1)}, u32[]{:S(2)}) copy-start(bf16[16,96,256]{2,1,0:T(8,128)(2,1)S(1)} %all-to-all-done.3) | copy-start | bytes 2359300
  154.9 21.4 %collective-permute-start.16 = (bf16[768,512]{1,0:T(8,128)(2,1)}, bf16[768,512]{1,0:T(8,128)(2,1)}, u32[]{:S(2)}, u32[]{:S(2)}) collective-permute-start(bf16[768,512]{1,0:T(8,128)(2,1)} %add_convert_fusion.1), channel_id=1, source_target_pairs={{0,128},{128,0},{1,129},{129,1},{2,130},{130,2},{3,131},{131,3},{4... | collective-permute-start | bytes 2359304 | tf_op jit(solution)/shard_map/ppermute | solution.py:32
  160.5 30.2 %all-to-all-start.4 = ((bf16[16,64,384]{2,1,0:T(8,128)(2,1)}), bf16[16,64,384]{2,1,0:T(8,128)(2,1)}, u32[]{:S(2)}, u32[]{:S(2)}) async-start(bf16[16,64,384]{2,1,0:T(8,128)(2,1)} %pad_maximum_fusion.6), calls=%async_computation.4 | async-start | bytes 1572864 | tf_op jit(solution)/shard_map/all_to_all | solution.py:50
  167.9 2.6 %copy-start.5 = (bf16[1024,1024]{0,1:T(8,128)(2,1)S(1)}, bf16[1024,1024]{0,1:T(8,128)(2,1)}, u32[]{:S(2)}) copy-start(bf16[1024,1024]{0,1:T(8,128)(2,1)} %all-gather.2.cloned.1.call-done) | copy-start | bytes 6291460
  170.5 5.8 %copy-start.8 = (bf16[768,512]{1,0:T(8,128)(2,1)S(1)}, bf16[768,512]{1,0:T(8,128)(2,1)}, u32[]{:S(2)}) copy-start(bf16[768,512]{1,0:T(8,128)(2,1)} %add_convert_fusion.1) | copy-start | bytes 2359300
  171.3 4.4 %collective-permute-start.15 = (bf16[32,1024]{1,0:T(8,128)(2,1)S(1)}, bf16[32,1024]{1,0:T(8,128)(2,1)S(1)}, u32[]{:S(2)}, u32[]{:S(2)}) collective-permute-start(bf16[32,1024]{1,0:T(8,128)(2,1)S(1)} %constant_dynamic-slice_fusion.2), channel_id=1, source_target_pairs={{0,128},{128,0},{1,129},{129,1},{2,130},{130,2},{3,131},{131,3},{4... | collective-permute-start | bytes 196616 | tf_op jit(solution)/shard_map/ppermute | solution.py:32
Sparse Core Ops, SparseCore 0:
  64.5 50.1 all-gather.1

commit v4 on v3

--- a/solution.py
+++ b/solution.py
@@ -42,9 +42,6 @@
 
     def x_far(x):
         return permute(x, "row", n_row, lambda i: i ^ 1)
-
-    def from_z(x, k):
-        return permute(x, "col", n_col, lambda i: (i - 2 * k) % n_col) if k else x
 
     def exchange(x, axis, groups=None):
         return lax.all_to_all(x, axis, 0, 0, tiled=True, axis_index_groups=groups)
@@ -64,9 +61,6 @@
             at = (first + k) % len(pieces) * n
             out = lax.dynamic_update_slice_in_dim(out, piece, at, 0)
         return out
-
-    def z_assemble(x):
-        return assemble([from_z(x, k) for k in range(n_z)], c // 2)
 
     def z_gather(x):
         return lax.all_gather(x, "col", axis=0, tiled=True, axis_index_groups=z_rings)
@@ -161,21 +155,24 @@
     a_other = core(a_own)
     depth = a_own.shape[0]
     parts = []
-    for cut in (slice(0, a_own.shape[1] // 4), slice(a_own.shape[1] // 4, None)):
+    for cut in (slice(0, a_own.shape[1] // 8), slice(a_own.shape[1] // 8, None)):
         part = dot(a_own[:, cut], m_all[:depth], 0, 0)
         part = part + dot(a_other[:, cut], m_all[depth:], 0, 0)
         parts.append(part.astype(BF))
     got, first, *parts = lax.optimization_barrier((got, other_dp(parts[0]), *parts))
     got = got.reshape(n_dp, n_row, (n_dp + 1) * tok, n_s)
-    v_both = got[:, :, : n_dp * tok]
     source = d * (n_row // 2) + lax.axis_index("row") // 2
     r_piece = lax.dynamic_slice(got, (0, source, n_dp * tok, 0), (n_dp, 1, tok, n_k))
     r_piece = r_piece.reshape(n_dp * tok, n_k)
-    v = lax.dynamic_index_in_dim(v_both, d, 0, keepdims=False)
-    v = v.transpose(1, 0, 2).reshape(n_dp * tok, n_row * n_s)
-
-    v_cols = v_both.reshape(n_dp, 2, n_z // 2, n_dp * tok, 2, n_w)
-    v_cols = lax.dynamic_slice_in_dim(v_cols, d * (n_z // 4), n_z // 4, 2)
+    v = lax.dynamic_slice(got, (d, 0, 0, 0), (1, n_row, n_dp * tok, n_s))
+    v = v[0].transpose(1, 0, 2).reshape(n_dp * tok, n_row * n_s)
+
+    v_cols = got.reshape(n_dp, 2, n_z // 2, (n_dp + 1) * tok, 2, n_w)
+    v_cols = lax.dynamic_slice(
+        v_cols,
+        (0, 0, d * (n_z // 4), 0, 0, 0),
+        (n_dp, 2, n_z // 4, n_dp * tok, 2, n_w),
+    )
     v_cols = v_cols.transpose(2, 4, 1, 0, 3, 5).reshape(n_col, n_dp * tok, n_w)
     r_rep = jnp.broadcast_to(r_piece, (n_col,) + r_piece.shape)
     sent = jnp.concatenate([r_rep, v_cols], 2).reshape(-1, n_k + n_w)

time: 204 us -> 199 us (0.975)
  waiting for transfers between devices: 85.8 us -> 83.5 us
    all_to_all x5, waiting for transfers between devices: 35.8 us -> 32.7 us  [exchange(): return lax.all_to_all(x, axis, 0, 0, tiled=True, axis_index_groups=groups)]
  transfers between devices with their start and end apart: 23 -> 23, of which waited for: 15 -> 15; matrix products, arithmetic and copies ran while one was open for 19% -> 18% of each run, Pallas kernels for 0% -> 0%
where the time goes in v4:
time: 199 us; the launch traced here: 198 us
  waiting for transfers between devices  83.5 us (42%)
  starting transfers between devices  51.2 us (26%)
  matrix products  23 us (12%)
  other arithmetic  18 us (9%)
  between operations  14.5 us (7%)
  local copies, waits for them, and re-layouts  8.04 us (4%)
    ppermute x17, waiting for transfers between devices, permute(): return lax.ppermute(x, axis, [(i, target(i)) for i in range(size)])  50.8 us
    all_to_all x5, waiting for transfers between devices, exchange(): return lax.all_to_all(x, axis, 0, 0, tiled=True, axis_index_groups=groups)  32.7 us
    all_to_all x5, starting transfers between devices, exchange(): return lax.all_to_all(x, axis, 0, 0, tiled=True, axis_index_groups=groups)  31.2 us
    dot_general x13, matrix products, dot(): lax.dot_general(a, b, (((da,), (db,)), ((), ())), preferred_element_type=...  23 us
    ppermute x17, starting transfers between devices, permute(): return lax.ppermute(x, axis, [(i, target(i)) for i in range(size)])  20 us
    convert_element_type x5, other arithmetic, total(): return (a.astype(F32) + b.astype(F32)).astype(BF)  4.1 us
  transfers between devices with their start and end apart: 23, of which 15 were waited for; matrix products, arithmetic and copies ran while one was open for 18% of the time, Pallas kernels for 0%

profile of v4, /device:TPU:1, one launch (start us, length us, event | category | flops | bytes accessed | tf_op | source)
XLA Modules:
  0.0 198.2 jit_solution(6896987691579038051)
XLA Ops:
  8.2 1.1 broadcast_in_dim.15
  9.3 9.1 %all-to-all-start = ((bf16[8,128,512]{2,1,0:T(8,128)(2,1)}), bf16[8,128,512]{2,1,0:T(8,128)(2,1)S(1)}, u32[]{:S(2)}, u32[]{:S(2)}) async-start(bf16[8,128,512]{2,1,0:T(8,128)(2,1)} %broadcast_in_dim.15), calls=%async_computation | async-start | bytes 2097152 | tf_op jit(solution)/shard_map/all_to_all | solution.py:47
  18.4 1.5 convolution_convert_fusion.4
  19.9 2.8 %collective-permute-start = (bf16[512,256]{1,0:T(8,128)(2,1)S(1)}, bf16[512,256]{1,0:T(8,128)(2,1)}, u32[]{:S(2)}, u32[]{:S(2)}) collective-permute-start(bf16[512,256]{1,0:T(8,128)(2,1)S(1)} %convolution_convert_fusion.4), channel_id=1, source_target_pairs={{0,96},{16,112},{32,0},{48,16},{64,32},{80,48},{96,64},{112,80},{1... | collective-permute-start | bytes 786440 | tf_op jit(solution)/shard_map/ppermute | solution.py:32
  23.8 1.3 collective-permute-start.5
  25.1 1.8 collective-permute-start.4
  26.9 1.5 collective-permute-done
  28.5 2.5 %collective-permute-done.1 = bf16[512,256]{1,0:T(8,128)(2,1)} collective-permute-done((bf16[512,256]{1,0:T(8,128)(2,1)S(1)}, bf16[512,256]{1,0:T(8,128)(2,1)}, u32[]{:S(2)}, u32[]{:S(2)}) %collective-permute-start.1) | collective-permute-done | bytes 262176 | tf_op jit(solution)/shard_map/ppermute | solution.py:32
  31.0 7.2 %collective-permute-done.2 = bf16[512,256]{1,0:T(8,128)(2,1)} collective-permute-done((bf16[512,256]{1,0:T(8,128)(2,1)S(1)}, bf16[512,256]{1,0:T(8,128)(2,1)}, u32[]{:S(2)}, u32[]{:S(2)}) %collective-permute-start.2) | collective-permute-done | bytes 262176 | tf_op jit(solution)/shard_map/ppermute | solution.py:32
  38.2 1.2 add_convert_fusion.3
  39.4 2.8 %collective-permute-start.3 = (bf16[512,256]{1,0:T(8,128)(2,1)S(1)}, bf16[512,256]{1,0:T(8,128)(2,1)S(1)}, u32[]{:S(2)}, u32[]{:S(2)}) collective-permute-start(bf16[512,256]{1,0:T(8,128)(2,1)S(1)} %add_convert_fusion.3), channel_id=1, source_target_pairs={{0,16},{16,0},{32,48},{48,32},{64,80},{80,64},{96,112},{112,96},{1... | collective-permute-start | bytes 786440 | tf_op jit(solution)/shard_map/ppermute | solution.py:32
  42.3 6.1 %collective-permute-done.3 = bf16[512,256]{1,0:T(8,128)(2,1)S(1)} collective-permute-done((bf16[512,256]{1,0:T(8,128)(2,1)S(1)}, bf16[512,256]{1,0:T(8,128)(2,1)S(1)}, u32[]{:S(2)}, u32[]{:S(2)}) %collective-permute-start.3) | collective-permute-done | bytes 262176 | tf_op jit(solution)/shard_map/ppermute | solution.py:32
  48.5 1.4 collective-permute-start.6
  49.9 2.4 %collective-permute-done.6 = bf16[1024,512]{1,0:T(8,128)(2,1)} collective-permute-done((bf16[1024,512]{1,0:T(8,128)(2,1)S(1)}, bf16[1024,512]{1,0:T(8,128)(2,1)}, u32[]{:S(2)}, u32[]{:S(2)}) %collective-permute-start.6) | collective-permute-done | bytes 1048608 | tf_op jit(solution)/shard_map/ppermute | solution.py:32
  52.4 1.4 broadcast_select_fusion.3
  53.7 2.7 %convolution_convert_fusion = bf16[2048,512]{1,0:T(8,128)(2,1)} fusion(bf16[512,512]{1,0:T(8,128)(2,1)S(1)} %copy-done, bf16[1024,512]{1,0:T(8,128)(2,1)S(1)} %get-tuple-element.48, bf16[1024,512]{1,0:T(8,128)(2,1)S(1)} %get-tuple-element.47), kind=kOutput, calls=%fused_computation | convolution fusion | flops 1078984704 | bytes 4718592 | tf_op jit(solution)/shard_map/dot_general | solution.py:11
  56.5 5.0 %all-to-all-start.1 = ((bf16[8,256,512]{2,1,0:T(8,128)(2,1)}), bf16[8,256,512]{2,1,0:T(8,128)(2,1)}, u32[]{:S(2)}, u32[]{:S(2)}) async-start(bf16[8,256,512]{2,1,0:T(8,128)(2,1)} %bitcast.77), calls=%async_computation.1 | async-start | bytes 4194304 | tf_op jit(solution)/shard_map/all_to_all | solution.py:47
  62.9 1.2 broadcast_select_fusion.7
  64.1 1.1 pad_maximum_fusion.1
  65.5 1.3 broadcast_select_fusion.5
  67.5 21.9 %all-to-all-done.1 = bf16[8,256,512]{2,1,0:T(8,128)(2,1)} async-done(((bf16[8,256,512]{2,1,0:T(8,128)(2,1)}), bf16[8,256,512]{2,1,0:T(8,128)(2,1)}, u32[]{:S(2)}, u32[]{:S(2)}) %all-to-all-start.1) | async-done | bytes 2097184 | tf_op jit(solution)/shard_map/all_to_all | solution.py:47
  89.4 2.0 %reduce_sum.24 = bf16[256,512]{1,0:T(8,128)(2,1)S(1)} reduce(bf16[8,256,512]{2,1,0:T(8,128)(2,1)} %all-to-all-done.1, bf16[]{:T(256)} %constant.79.clone.1), dimensions={0}, to_apply=%region_0.1 | reduce | flops 917504 | bytes 2359298 | tf_op jit(solution)/shard_map/reduce_sum | solution.py:51
  91.4 1.7 convolution_convert_fusion.2
  93.2 1.6 collective-permute-start.8
  97.4 6.1 %all-to-all-start.2 = ((bf16[8,128,256]{2,1,0:T(8,128)(2,1)}), bf16[8,128,256]{2,1,0:T(8,128)(2,1)S(1)}, u32[]{:S(2)}, u32[]{:S(2)}) async-start(bf16[8,128,256]{2,1,0:T(8,128)(2,1)} %fusion.11), calls=%async_computation.2 | async-start | bytes 1048576 | tf_op jit(solution)/shard_map/all_to_all | solution.py:47
  105.4 1.3 collective-permute-start.10
  107.6 2.3 %convolution_convert_fusion.1 = bf16[1024,512]{1,0:T(8,128)(2,1)} fusion(bf16[1024,1024]{1,0:T(8,128)(2,1)S(1)} %bitcast.65, bf16[1024,512]{1,0:T(8,128)(2,1)S(1)} %bitcast.74), kind=kOutput, calls=%fused_computation.11 | convolution fusion | flops 1074266112 | bytes 4194304 | tf_op jit(solution)/shard_map/dot_general | solution.py:11
  109.8 8.3 %collective-permute-done.10 = bf16[512,512]{1,0:T(8,128)(2,1)S(1)} collective-permute-done((bf16[512,512]{1,0:T(8,128)(2,1)S(1)}, bf16[512,512]{1,0:T(8,128)(2,1)S(1)}, u32[]{:S(2)}, u32[]{:S(2)}) %collective-permute-start.10) | collective-permute-done | bytes 524320 | tf_op jit(solution)/shard_map/ppermute | solution.py:32
  118.2 2.4 %collective-permute-done.11 = bf16[512,512]{1,0:T(8,128)(2,1)S(1)} collective-permute-done((bf16[512,512]{1,0:T(8,128)(2,1)S(1)}, bf16[512,512]{1,0:T(8,128)(2,1)S(1)}, u32[]{:S(2)}, u32[]{:S(2)}) %collective-permute-start.11) | collective-permute-done | bytes 524320 | tf_op jit(solution)/shard_map/ppermute | solution.py:32
  121.3 12.1 %collective-permute-done.12 = bf16[512,512]{1,0:T(8,128)(2,1)} collective-permute-done((bf16[512,512]{1,0:T(8,128)(2,1)S(1)}, bf16[512,512]{1,0:T(8,128)(2,1)}, u32[]{:S(2)}, u32[]{:S(2)}) %collective-permute-start.12) | collective-permute-done | bytes 524320 | tf_op jit(solution)/shard_map/ppermute | solution.py:32
  135.1 3.6 %all-to-all-start.3 = ((bf16[16,96,256]{2,1,0:T(8,128)(2,1)}), bf16[16,96,256]{2,1,0:T(8,128)(2,1)S(1)}, u32[]{:S(2)}, u32[]{:S(2)}) async-start(bf16[16,96,256]{2,1,0:T(8,128)(2,1)} %pad_maximum_fusion.5), calls=%async_computation.3 | async-start | bytes 1572864 | tf_op jit(solution)/shard_map/all_to_all | solution.py:47
  140.1 1.2 constant_dynamic-update-slice_fusion
  141.3 1.3 fusion.13
  142.9 1.4 collective-permute-start.14
  144.3 2.6 %fusion.3 = f32[896,512]{1,0:T(8,128)S(1)} fusion(bf16[1024,1024]{0,1:T(8,128)(2,1)} %collective-permute-done.13, bf16[2048,512]{1,0:T(8,128)(2,1)S(1)} %constant_dynamic-update-slice_fusion), kind=kOutput, calls=%fused_computation.5 | convolution fusion | flops 939524096 | bytes 4718592 | tf_op jit(solution)/shard_map/dot_general | solution.py:11
  146.9 2.0 %add_convert_fusion.1 = bf16[896,512]{1,0:T(8,128)(2,1)} fusion(f32[896,512]{1,0:T(8,128)S(1)} %fusion.3, bf16[1024,1024]{0,1:T(8,128)(2,1)S(1)} %copy-done.3, bf16[2048,512]{1,0:T(8,128)(2,1)S(1)} %constant_dynamic-update-slice_fusion), kind=kOutput, calls=%fused_computation.8 | convolution fusion | flops 940441600 | bytes 5636096 | tf_op jit(solution)/shard_map/dot_general | solution.py:11
  148.9 2.5 %all-to-all-done.3 = bf16[16,96,256]{2,1,0:T(8,128)(2,1)S(1)} async-done(((bf16[16,96,256]{2,1,0:T(8,128)(2,1)}), bf16[16,96,256]{2,1,0:T(8,128)(2,1)S(1)}, u32[]{:S(2)}, u32[]{:S(2)}) %all-to-all-start.3) | async-done | bytes 786464 | tf_op jit(solution)/shard_map/all_to_all | solution.py:47
  152.8 1.1 reshape_reshape.3
  153.9 1.1 constant_dynamic-slice_fusion
  155.1 1.1 pad_maximum_fusion.6
  156.2 7.3 %all-to-all-start.4 = ((bf16[16,64,384]{2,1,0:T(8,128)(2,1)}), bf16[16,64,384]{2,1,0:T(8,128)(2,1)}, u32[]{:S(2)}, u32[]{:S(2)}) async-start(bf16[16,64,384]{2,1,0:T(8,128)(2,1)} %pad_maximum_fusion.6), calls=%async_computation.4 | async-start | bytes 1572864 | tf_op jit(solution)/shard_map/all_to_all | solution.py:47
  163.6 2.5 %fusion.25 = f32[64,1024]{1,0:T(8,128)S(1)} fusion(bf16[1024,1024]{0,1:T(8,128)(2,1)} %collective-permute-done.13, pred[]{:T(512)S(6)} %eq.13, bf16[64,2048]{1,0:T(8,128)(2,1)S(1)} %bitcast.83), kind=kOutput, calls=%fused_computation.59 | convolution fusion | flops 134283264 | bytes 2621441 | tf_op jit(solution)/shard_map/dot_general | solution.py:11
  166.9 1.3 collective-permute-start.15
  169.1 5.7 %collective-permute-done.15 = bf16[32,1024]{1,0:T(8,128)(2,1)S(1)} collective-permute-done((bf16[32,1024]{1,0:T(8,128)(2,1)S(1)}, bf16[32,1024]{1,0:T(8,128)(2,1)S(1)}, u32[]{:S(2)}, u32[]{:S(2)}) %collective-permute-start.15) | collective-permute-done | bytes 65568 | tf_op jit(solution)/shard_map/ppermute | solution.py:32
  175.5 1.4 add_convert_fusion
  178.0 8.3 %all-to-all-done.4 = bf16[16,64,384]{2,1,0:T(8,128)(2,1)} async-done(((bf16[16,64,384]{2,1,0:T(8,128)(2,1)}), bf16[16,64,384]{2,1,0:T(8,128)(2,1)}, u32[]{:S(2)}, u32[]{:S(2)}) %all-to-all-start.4) | async-done | bytes 786464 | tf_op jit(solution)/shard_map/all_to_all | solution.py:47
  186.3 2.6 %fusion.19 = f32[512,256]{1,0:T(8,128)} fusion(bf16[1024,512]{1,0:T(8,128)(2,1)} %bitcast.73, bf16[1024,384]{1,0:T(8,128)(2,1)} %bitcast.27), kind=kOutput, calls=%fused_computation.41 | convolution fusion | flops 268435456 | bytes 2097152 | tf_op jit(solution)/shard_map/dot_general | solution.py:11
  188.9 2.5 %fusion.22 = f32[1024,128]{1,0:T(8,128)} fusion(bf16[1024,1024]{1,0:T(8,128)(2,1)S(1)} %bitcast.66, bf16[1024,384]{1,0:T(8,128)(2,1)} %bitcast.27), kind=kOutput, calls=%fused_computation.50 | convolution fusion | flops 268435456 | bytes 2883584 | tf_op jit(solution)/shard_map/dot_general | solution.py:11
  (86 shorter events, 19.1 us)
Async XLA Ops:
  7.2 46.6 %copy-start = (bf16[512,512]{1,0:T(8,128)(2,1)S(1)}, bf16[512,512]{1,0:T(8,128)(2,1)}, u32[]{:S(2)}) copy-start(bf16[512,512]{1,0:T(8,128)(2,1)} %param.7) | copy-start | bytes 1572868
  7.2 11.3 %copy-start.2 = (bf16[512,1024]{1,0:T(8,128)(2,1)S(1)}, bf16[512,1024]{1,0:T(8,128)(2,1)}, u32[]{:S(2)}) copy-start(bf16[512,1024]{1,0:T(8,128)(2,1)} %param.9) | copy-start | bytes 3145732
  9.3 15.8 %copy-start.9 = (bf16[512,512]{1,0:T(8,128)(2,1)S(1)}, bf16[512,512]{1,0:T(8,128)(2,1)}, u32[]{:S(2)}) copy-start(bf16[512,512]{1,0:T(8,128)(2,1)} %param.8) | copy-start | bytes 1572868
  9.3 39.2 %all-to-all-start = ((bf16[8,128,512]{2,1,0:T(8,128)(2,1)}), bf16[8,128,512]{2,1,0:T(8,128)(2,1)S(1)}, u32[]{:S(2)}, u32[]{:S(2)}) async-start(bf16[8,128,512]{2,1,0:T(8,128)(2,1)} %broadcast_in_dim.15), calls=%async_computation | async-start | bytes 2097152 | tf_op jit(solution)/shard_map/all_to_all | solution.py:47
  19.9 8.5 %collective-permute-start = (bf16[512,256]{1,0:T(8,128)(2,1)S(1)}, bf16[512,256]{1,0:T(8,128)(2,1)}, u32[]{:S(2)}, u32[]{:S(2)}) collective-permute-start(bf16[512,256]{1,0:T(8,128)(2,1)S(1)} %convolution_convert_fusion.4), channel_id=1, source_target_pairs={{0,96},{16,112},{32,0},{48,16},{64,32},{80,48},{96,64},{112,80},{1... | collective-permute-start | bytes 786440 | tf_op jit(solution)/shard_map/ppermute | solution.py:32
  22.7 8.2 %collective-permute-start.1 = (bf16[512,256]{1,0:T(8,128)(2,1)S(1)}, bf16[512,256]{1,0:T(8,128)(2,1)}, u32[]{:S(2)}, u32[]{:S(2)}) collective-permute-start(bf16[512,256]{1,0:T(8,128)(2,1)S(1)} %convolution_convert_fusion.4), channel_id=1, source_target_pairs={{0,64},{16,80},{32,96},{48,112},{64,0},{80,16},{96,32},{112,48},{1... | collective-permute-start | bytes 786440 | tf_op jit(solution)/shard_map/ppermute | solution.py:32
  23.1 15.1 %collective-permute-start.2 = (bf16[512,256]{1,0:T(8,128)(2,1)S(1)}, bf16[512,256]{1,0:T(8,128)(2,1)}, u32[]{:S(2)}, u32[]{:S(2)}) collective-permute-start(bf16[512,256]{1,0:T(8,128)(2,1)S(1)} %convolution_convert_fusion.4), channel_id=1, source_target_pairs={{0,32},{16,48},{32,64},{48,80},{64,96},{80,112},{96,0},{112,16},{1... | collective-permute-start | bytes 786440 | tf_op jit(solution)/shard_map/ppermute | solution.py:32
  23.8 24.7 %collective-permute-start.5 = (bf16[256,1024]{1,0:T(8,128)(2,1)S(1)}, bf16[256,1024]{1,0:T(8,128)(2,1)}, u32[]{:S(2)}, u32[]{:S(2)}) collective-permute-start(bf16[256,1024]{1,0:T(8,128)(2,1)S(1)} %constant_dynamic-slice_fusion.3), channel_id=1, source_target_pairs={{0,128},{128,0},{1,129},{129,1},{2,130},{130,2},{3,131},{131,3},{4... | collective-permute-start | bytes 1572872 | tf_op jit(solution)/shard_map/ppermute | solution.py:32
  25.1 23.4 %collective-permute-start.4 = (bf16[512,512]{1,0:T(8,128)(2,1)S(1)}, bf16[512,512]{1,0:T(8,128)(2,1)}, u32[]{:S(2)}, u32[]{:S(2)}) collective-permute-start(bf16[512,512]{1,0:T(8,128)(2,1)S(1)} %copy-done.9), channel_id=1, source_target_pairs={{0,144},{16,128},{32,176},{48,160},{64,208},{80,192},{96,240},{112... | collective-permute-start | bytes 1572872 | tf_op jit(solution)/shard_map/ppermute | solution.py:32
  39.4 9.0 %collective-permute-start.3 = (bf16[512,256]{1,0:T(8,128)(2,1)S(1)}, bf16[512,256]{1,0:T(8,128)(2,1)S(1)}, u32[]{:S(2)}, u32[]{:S(2)}) collective-permute-start(bf16[512,256]{1,0:T(8,128)(2,1)S(1)} %add_convert_fusion.3), channel_id=1, source_target_pairs={{0,16},{16,0},{32,48},{48,32},{64,80},{80,64},{96,112},{112,96},{1... | collective-permute-start | bytes 786440 | tf_op jit(solution)/shard_map/ppermute | solution.py:32
  48.5 3.8 %collective-permute-start.6 = (bf16[1024,512]{1,0:T(8,128)(2,1)S(1)}, bf16[1024,512]{1,0:T(8,128)(2,1)}, u32[]{:S(2)}, u32[]{:S(2)}) collective-permute-start(bf16[1024,512]{1,0:T(8,128)(2,1)S(1)} %bitcast.70), channel_id=1, source_target_pairs={{0,1},{1,0},{2,3},{3,2},{4,5},{5,4},{6,7},{7,6},{8,9},{9,8},{10,11... | collective-permute-start | bytes 3145736 | tf_op jit(solution)/shard_map/ppermute | solution.py:32
  56.5 5.0 %copy-start.10 = (bf16[1024,256]{1,0:T(8,128)(2,1)S(1)}, bf16[1024,256]{1,0:T(8,128)(2,1)}, u32[]{:S(2)}) copy-start(bf16[1024,256]{1,0:T(8,128)(2,1)} %param.6) | copy-start | bytes 1572868
  56.5 32.9 %all-to-all-start.1 = ((bf16[8,256,512]{2,1,0:T(8,128)(2,1)}), bf16[8,256,512]{2,1,0:T(8,128)(2,1)}, u32[]{:S(2)}, u32[]{:S(2)}) async-start(bf16[8,256,512]{2,1,0:T(8,128)(2,1)} %bitcast.77), calls=%async_computation.1 | async-start | bytes 4194304 | tf_op jit(solution)/shard_map/all_to_all | solution.py:47
  61.4 72.0 %all-gather.2.cloned.1.call-start = ((), (), s32[]{:S(2)}) async-start(), calls=%async_computation.5 | async-start | bytes 2359296 | tf_op jit(solution)/shard_map/all_gather | solution.py:66
  62.3 3.3 %collective-permute-start.7 = (bf16[256,1024]{1,0:T(8,128)(2,1)}, bf16[256,1024]{1,0:T(8,128)(2,1)}, u32[]{:S(2)}, u32[]{:S(2)}) collective-permute-start(bf16[256,1024]{1,0:T(8,128)(2,1)} %collective-permute-done.5), channel_id=1, source_target_pairs={{0,1},{1,0},{2,3},{3,2},{4,5},{5,4},{6,7},{7,6},{8,9},{9,8},{10,11... | collective-permute-start | bytes 1572872 | tf_op jit(solution)/shard_map/ppermute | solution.py:32
  62.9 2.2 %copy-start.8 = (bf16[256,512]{1,0:T(8,128)(2,1)S(1)}, bf16[256,512]{1,0:T(8,128)(2,1)}, u32[]{:S(2)}) copy-start(bf16[256,512]{1,0:T(8,128)(2,1)} %param.5) | copy-start | bytes 786436
  93.2 3.2 %collective-permute-start.8 = (bf16[8,128,256]{2,1,0:T(8,128)(2,1)S(1)}, bf16[8,128,256]{2,1,0:T(8,128)(2,1)S(1)}, u32[]{:S(2)}, u32[]{:S(2)}) collective-permute-start(bf16[8,128,256]{2,1,0:T(8,128)(2,1)S(1)} %fusion.17), channel_id=1, source_target_pairs={{0,1},{1,0},{2,3},{3,2},{4,5},{5,4},{6,7},{7,6},{8,9},{9,8},{10,11... | collective-permute-start | bytes 1572872 | tf_op jit(solution)/shard_map/ppermute | solution.py:32
  94.9 9.5 %collective-permute-start.9 = (bf16[256,512]{1,0:T(8,128)(2,1)S(1)}, bf16[256,512]{1,0:T(8,128)(2,1)}, u32[]{:S(2)}, u32[]{:S(2)}) collective-permute-start(bf16[256,512]{1,0:T(8,128)(2,1)S(1)} %reduce_sum.24), channel_id=1, source_target_pairs={{0,16},{16,0},{32,48},{48,32},{64,80},{80,64},{96,112},{112,96},{1... | collective-permute-start | bytes 786440 | tf_op jit(solution)/shard_map/ppermute | solution.py:32
  97.4 36.0 %all-to-all-start.2 = ((bf16[8,128,256]{2,1,0:T(8,128)(2,1)}), bf16[8,128,256]{2,1,0:T(8,128)(2,1)S(1)}, u32[]{:S(2)}, u32[]{:S(2)}) async-start(bf16[8,128,256]{2,1,0:T(8,128)(2,1)} %fusion.11), calls=%async_computation.2 | async-start | bytes 1048576 | tf_op jit(solution)/shard_map/all_to_all | solution.py:47
  103.5 4.0 %copy-start.1 = (bf16[16,2,32,512]{3,2,1,0:T(8,128)(2,1)S(1)}, bf16[16,2,32,512]{3,2,1,0:T(8,128)(2,1)}, u32[]{:S(2)}) copy-start(bf16[16,2,32,512]{3,2,1,0:T(8,128)(2,1)} %pad_maximum_fusion.1) | copy-start | bytes 3145732
  105.4 4.5 %copy-start.5 = (bf16[512,512]{1,0:T(8,128)(2,1)}, bf16[512,512]{1,0:T(8,128)(2,1)S(1)}, u32[]{:S(2)}) copy-start(bf16[512,512]{1,0:T(8,128)(2,1)S(1)} %pad_maximum_fusion.7) | copy-start | bytes 1572868
  105.4 12.7 %collective-permute-start.10 = (bf16[512,512]{1,0:T(8,128)(2,1)S(1)}, bf16[512,512]{1,0:T(8,128)(2,1)S(1)}, u32[]{:S(2)}, u32[]{:S(2)}) collective-permute-start(bf16[512,512]{1,0:T(8,128)(2,1)S(1)} %pad_maximum_fusion.7), channel_id=1, source_target_pairs={{0,96},{16,112},{32,0},{48,16},{64,32},{80,48},{96,64},{112,80},{1... | collective-permute-start | bytes 1572872 | tf_op jit(solution)/shard_map/ppermute | solution.py:32
  106.7 13.8 %collective-permute-start.11 = (bf16[512,512]{1,0:T(8,128)(2,1)S(1)}, bf16[512,512]{1,0:T(8,128)(2,1)S(1)}, u32[]{:S(2)}, u32[]{:S(2)}) collective-permute-start(bf16[512,512]{1,0:T(8,128)(2,1)S(1)} %pad_maximum_fusion.7), channel_id=1, source_target_pairs={{0,64},{16,80},{32,96},{48,112},{64,0},{80,16},{96,32},{112,48},{1... | collective-permute-start | bytes 1572872 | tf_op jit(solution)/shard_map/ppermute | solution.py:32
  107.3 26.1 %collective-permute-start.12 = (bf16[512,512]{1,0:T(8,128)(2,1)S(1)}, bf16[512,512]{1,0:T(8,128)(2,1)}, u32[]{:S(2)}, u32[]{:S(2)}) collective-permute-start(bf16[512,512]{1,0:T(8,128)(2,1)S(1)} %pad_maximum_fusion.7), channel_id=1, source_target_pairs={{0,32},{16,48},{32,64},{48,80},{64,96},{80,112},{96,0},{112,16},{1... | collective-permute-start | bytes 1572872 | tf_op jit(solution)/shard_map/ppermute | solution.py:32
  118.1 2.4 %copy-start.11 = (bf16[512,512]{1,0:T(8,128)(2,1)}, bf16[512,512]{1,0:T(8,128)(2,1)S(1)}, u32[]{:S(2)}) copy-start(bf16[512,512]{1,0:T(8,128)(2,1)S(1)} %collective-permute-done.10) | copy-start | bytes 1572868
  120.5 0.8 copy-start.13
  133.4 7.9 %collective-permute-start.13 = (bf16[1024,1024]{0,1:T(8,128)(2,1)}, bf16[1024,1024]{0,1:T(8,128)(2,1)}, u32[]{:S(2)}, u32[]{:S(2)}) collective-permute-start(bf16[1024,1024]{0,1:T(8,128)(2,1)} %all-gather.2.cloned.1.call-done), channel_id=1, source_target_pairs={{0,1},{1,0},{2,3},{3,2},{4,5},{5,4},{6,7},{7,6},{8,9},{9,8},{10,11... | collective-permute-start | bytes 6291464 | tf_op jit(solution)/shard_map/ppermute | solution.py:32
  135.1 16.4 %all-to-all-start.3 = ((bf16[16,96,256]{2,1,0:T(8,128)(2,1)}), bf16[16,96,256]{2,1,0:T(8,128)(2,1)S(1)}, u32[]{:S(2)}, u32[]{:S(2)}) async-start(bf16[16,96,256]{2,1,0:T(8,128)(2,1)} %pad_maximum_fusion.5), calls=%async_computation.3 | async-start | bytes 1572864 | tf_op jit(solution)/shard_map/all_to_all | solution.py:47
  138.7 1.0 copy-start.6
  138.7 1.2 copy-start.12
  138.7 1.3 copy-start.14
  140.0 2.5 %copy-start.3 = (bf16[1024,1024]{0,1:T(8,128)(2,1)S(1)}, bf16[1024,1024]{0,1:T(8,128)(2,1)}, u32[]{:S(2)}) copy-start(bf16[1024,1024]{0,1:T(8,128)(2,1)} %all-gather.2.cloned.1.call-done) | copy-start | bytes 6291460
  142.9 9.3 %collective-permute-start.14 = (bf16[128,512]{1,0:T(8,128)(2,1)S(1)}, bf16[128,512]{1,0:T(8,128)(2,1)}, u32[]{:S(2)}, u32[]{:S(2)}) collective-permute-start(bf16[128,512]{1,0:T(8,128)(2,1)S(1)} %fusion.10), channel_id=1, source_target_pairs={{0,128},{128,0},{1,129},{129,1},{2,130},{130,2},{3,131},{131,3},{4... | collective-permute-start | bytes 393224 | tf_op jit(solution)/shard_map/ppermute | solution.py:32
  152.2 23.3 %collective-permute-start.16 = (bf16[896,512]{1,0:T(8,128)(2,1)}, bf16[896,512]{1,0:T(8,128)(2,1)}, u32[]{:S(2)}, u32[]{:S(2)}) collective-permute-start(bf16[896,512]{1,0:T(8,128)(2,1)} %add_convert_fusion.1), channel_id=1, source_target_pairs={{0,128},{128,0},{1,129},{129,1},{2,130},{130,2},{3,131},{131,3},{4... | collective-permute-start | bytes 2752520 | tf_op jit(solution)/shard_map/ppermute | solution.py:32
  156.2 30.1 %all-to-all-start.4 = ((bf16[16,64,384]{2,1,0:T(8,128)(2,1)}), bf16[16,64,384]{2,1,0:T(8,128)(2,1)}, u32[]{:S(2)}, u32[]{:S(2)}) async-start(bf16[16,64,384]{2,1,0:T(8,128)(2,1)} %pad_maximum_fusion.6), calls=%async_computation.4 | async-start | bytes 1572864 | tf_op jit(solution)/shard_map/all_to_all | solution.py:47
  163.5 2.6 %copy-start.4 = (bf16[1024,1024]{0,1:T(8,128)(2,1)S(1)}, bf16[1024,1024]{0,1:T(8,128)(2,1)}, u32[]{:S(2)}) copy-start(bf16[1024,1024]{0,1:T(8,128)(2,1)} %all-gather.2.cloned.1.call-done) | copy-start | bytes 6291460
  166.1 9.4 %copy-start.7 = (bf16[896,512]{1,0:T(8,128)(2,1)S(1)}, bf16[896,512]{1,0:T(8,128)(2,1)}, u32[]{:S(2)}) copy-start(bf16[896,512]{1,0:T(8,128)(2,1)} %add_convert_fusion.1) | copy-start | bytes 2752516
  166.9 8.0 %collective-permute-start.15 = (bf16[32,1024]{1,0:T(8,128)(2,1)S(1)}, bf16[32,1024]{1,0:T(8,128)(2,1)S(1)}, u32[]{:S(2)}, u32[]{:S(2)}) collective-permute-start(bf16[32,1024]{1,0:T(8,128)(2,1)S(1)} %constant_dynamic-slice_fusion.2), channel_id=1, source_target_pairs={{0,128},{128,0},{1,129},{129,1},{2,130},{130,2},{3,131},{131,3},{4... | collective-permute-start | bytes 196616 | tf_op jit(solution)/shard_map/ppermute | solution.py:32
Sparse Core Ops, SparseCore 0:
  64.0 52.2 all-gather.1

commit v5 on v4

--- a/solution.py
+++ b/solution.py
@@ -132,8 +132,8 @@
     send = jnp.where(core_id == 0, both[:, 1], both[:, 0])
     both = total(keep, core(send)).reshape(-1, n_s)
     both = exchange(both, "col", z_rings).reshape(n_z, -1, n_s)
-    both, a_own, grad_weight, *m_pieces = lax.optimization_barrier(
-        (both, a_own, grad_weight, *m_pieces)
+    both, a_own, grad_weight, x_t, c_t, *m_pieces = lax.optimization_barrier(
+        (both, a_own, grad_weight, x_all.T, c_all.T, *m_pieces)
     )
     n_y = n_row // 2
     m_all = assemble(m_pieces, lax.axis_index("row") // 2 + core_id * (n_y // 2))
@@ -180,8 +180,8 @@
     second = other_dp(parts[1])
     big_weight = jnp.concatenate([total(parts[0], first), total(parts[1], second)], 0)
     got, big_weight = lax.optimization_barrier((got, big_weight))
-    grad_b = dot(x_all, got[:, :n_k], 0, 0)
-    grad_a = dot(c_all, got[:, n_k:], 0, 0)
+    grad_b = dot(x_t, got[:, :n_k], 1, 0)
+    grad_a = dot(c_t, got[:, n_k:], 1, 0)
 
     low, high = v[:, :depth], v[:, depth:]
     v_own = jnp.where(core_id == 0, low, high)

time: 199 us -> 199 us (level)
  no operation moved by 1% of the time
where the time goes in v5:
time: 199 us; the launch traced here: 198 us
  waiting for transfers between devices  83.5 us (42%)
  starting transfers between devices  51.2 us (26%)
  matrix products  23 us (12%)
  other arithmetic  18 us (9%)
  between operations  14.5 us (7%)
  local copies, waits for them, and re-layouts  8.04 us (4%)
    ppermute x17, waiting for transfers between devices, permute(): return lax.ppermute(x, axis, [(i, target(i)) for i in range(size)])  50.8 us
    all_to_all x5, waiting for transfers between devices, exchange(): return lax.all_to_all(x, axis, 0, 0, tiled=True, axis_index_groups=groups)  32.7 us
    all_to_all x5, starting transfers between devices, exchange(): return lax.all_to_all(x, axis, 0, 0, tiled=True, axis_index_groups=groups)  31.2 us
    dot_general x13, matrix products, dot(): lax.dot_general(a, b, (((da,), (db,)), ((), ())), preferred_element_type=...  23 us
    ppermute x17, starting transfers between devices, permute(): return lax.ppermute(x, axis, [(i, target(i)) for i in range(size)])  20 us
    convert_element_type x5, other arithmetic, total(): return (a.astype(F32) + b.astype(F32)).astype(BF)  4.1 us
  transfers between devices with their start and end apart: 23, of which 15 were waited for; matrix products, arithmetic and copies ran while one was open for 18% of the time, Pallas kernels for 0%

profile of v5, /device:TPU:1, one launch (start us, length us, event | category | flops | bytes accessed | tf_op | source)
XLA Modules:
  0.0 198.2 jit_solution(6896987691579038051)
XLA Ops:
  8.2 1.1 broadcast_in_dim.15
  9.3 9.1 %all-to-all-start = ((bf16[8,128,512]{2,1,0:T(8,128)(2,1)}), bf16[8,128,512]{2,1,0:T(8,128)(2,1)S(1)}, u32[]{:S(2)}, u32[]{:S(2)}) async-start(bf16[8,128,512]{2,1,0:T(8,128)(2,1)} %broadcast_in_dim.15), calls=%async_computation | async-start | bytes 2097152 | tf_op jit(solution)/shard_map/all_to_all | solution.py:47
  18.4 1.5 convolution_convert_fusion.4
  19.9 2.8 %collective-permute-start = (bf16[512,256]{1,0:T(8,128)(2,1)S(1)}, bf16[512,256]{1,0:T(8,128)(2,1)}, u32[]{:S(2)}, u32[]{:S(2)}) collective-permute-start(bf16[512,256]{1,0:T(8,128)(2,1)S(1)} %convolution_convert_fusion.4), channel_id=1, source_target_pairs={{0,96},{16,112},{32,0},{48,16},{64,32},{80,48},{96,64},{112,80},{1... | collective-permute-start | bytes 786440 | tf_op jit(solution)/shard_map/ppermute | solution.py:32
  23.8 1.3 collective-permute-start.5
  25.1 1.8 collective-permute-start.4
  26.9 1.5 collective-permute-done
  28.5 2.5 %collective-permute-done.1 = bf16[512,256]{1,0:T(8,128)(2,1)} collective-permute-done((bf16[512,256]{1,0:T(8,128)(2,1)S(1)}, bf16[512,256]{1,0:T(8,128)(2,1)}, u32[]{:S(2)}, u32[]{:S(2)}) %collective-permute-start.1) | collective-permute-done | bytes 262176 | tf_op jit(solution)/shard_map/ppermute | solution.py:32
  31.0 7.2 %collective-permute-done.2 = bf16[512,256]{1,0:T(8,128)(2,1)} collective-permute-done((bf16[512,256]{1,0:T(8,128)(2,1)S(1)}, bf16[512,256]{1,0:T(8,128)(2,1)}, u32[]{:S(2)}, u32[]{:S(2)}) %collective-permute-start.2) | collective-permute-done | bytes 262176 | tf_op jit(solution)/shard_map/ppermute | solution.py:32
  38.2 1.2 add_convert_fusion.3
  39.4 2.8 %collective-permute-start.3 = (bf16[512,256]{1,0:T(8,128)(2,1)S(1)}, bf16[512,256]{1,0:T(8,128)(2,1)S(1)}, u32[]{:S(2)}, u32[]{:S(2)}) collective-permute-start(bf16[512,256]{1,0:T(8,128)(2,1)S(1)} %add_convert_fusion.3), channel_id=1, source_target_pairs={{0,16},{16,0},{32,48},{48,32},{64,80},{80,64},{96,112},{112,96},{1... | collective-permute-start | bytes 786440 | tf_op jit(solution)/shard_map/ppermute | solution.py:32
  42.3 6.1 %collective-permute-done.3 = bf16[512,256]{1,0:T(8,128)(2,1)S(1)} collective-permute-done((bf16[512,256]{1,0:T(8,128)(2,1)S(1)}, bf16[512,256]{1,0:T(8,128)(2,1)S(1)}, u32[]{:S(2)}, u32[]{:S(2)}) %collective-permute-start.3) | collective-permute-done | bytes 262176 | tf_op jit(solution)/shard_map/ppermute | solution.py:32
  48.5 1.4 collective-permute-start.6
  49.9 2.4 %collective-permute-done.6 = bf16[1024,512]{1,0:T(8,128)(2,1)} collective-permute-done((bf16[1024,512]{1,0:T(8,128)(2,1)S(1)}, bf16[1024,512]{1,0:T(8,128)(2,1)}, u32[]{:S(2)}, u32[]{:S(2)}) %collective-permute-start.6) | collective-permute-done | bytes 1048608 | tf_op jit(solution)/shard_map/ppermute | solution.py:32
  52.4 1.4 broadcast_select_fusion.3
  53.7 2.7 %convolution_convert_fusion = bf16[2048,512]{1,0:T(8,128)(2,1)} fusion(bf16[512,512]{1,0:T(8,128)(2,1)S(1)} %copy-done, bf16[1024,512]{1,0:T(8,128)(2,1)S(1)} %get-tuple-element.52, bf16[1024,512]{1,0:T(8,128)(2,1)S(1)} %get-tuple-element.51), kind=kOutput, calls=%fused_computation | convolution fusion | flops 1078984704 | bytes 4718592 | tf_op jit(solution)/shard_map/dot_general | solution.py:11
  56.5 5.0 %all-to-all-start.1 = ((bf16[8,256,512]{2,1,0:T(8,128)(2,1)}), bf16[8,256,512]{2,1,0:T(8,128)(2,1)}, u32[]{:S(2)}, u32[]{:S(2)}) async-start(bf16[8,256,512]{2,1,0:T(8,128)(2,1)} %bitcast.80), calls=%async_computation.1 | async-start | bytes 4194304 | tf_op jit(solution)/shard_map/all_to_all | solution.py:47
  62.9 1.2 broadcast_select_fusion.7
  64.1 1.1 pad_maximum_fusion.1
  65.5 1.3 broadcast_select_fusion.5
  67.5 21.9 %all-to-all-done.1 = bf16[8,256,512]{2,1,0:T(8,128)(2,1)} async-done(((bf16[8,256,512]{2,1,0:T(8,128)(2,1)}), bf16[8,256,512]{2,1,0:T(8,128)(2,1)}, u32[]{:S(2)}, u32[]{:S(2)}) %all-to-all-start.1) | async-done | bytes 2097184 | tf_op jit(solution)/shard_map/all_to_all | solution.py:47
  89.4 2.0 %reduce_sum.24 = bf16[256,512]{1,0:T(8,128)(2,1)S(1)} reduce(bf16[8,256,512]{2,1,0:T(8,128)(2,1)} %all-to-all-done.1, bf16[]{:T(256)} %constant.79.clone.1), dimensions={0}, to_apply=%region_0.1 | reduce | flops 917504 | bytes 2359298 | tf_op jit(solution)/shard_map/reduce_sum | solution.py:51
  91.4 1.7 convolution_convert_fusion.2
  93.2 1.6 collective-permute-start.8
  97.4 6.1 %all-to-all-start.2 = ((bf16[8,128,256]{2,1,0:T(8,128)(2,1)}), bf16[8,128,256]{2,1,0:T(8,128)(2,1)S(1)}, u32[]{:S(2)}, u32[]{:S(2)}) async-start(bf16[8,128,256]{2,1,0:T(8,128)(2,1)} %fusion.11), calls=%async_computation.2 | async-start | bytes 1048576 | tf_op jit(solution)/shard_map/all_to_all | solution.py:47
  105.4 1.3 collective-permute-start.10
  107.6 2.3 %convolution_convert_fusion.1 = bf16[1024,512]{1,0:T(8,128)(2,1)} fusion(bf16[1024,1024]{1,0:T(8,128)(2,1)S(1)} %bitcast.68, bf16[1024,512]{1,0:T(8,128)(2,1)S(1)} %bitcast.77), kind=kOutput, calls=%fused_computation.11 | convolution fusion | flops 1074266112 | bytes 4194304 | tf_op jit(solution)/shard_map/dot_general | solution.py:11
  109.8 8.3 %collective-permute-done.10 = bf16[512,512]{1,0:T(8,128)(2,1)S(1)} collective-permute-done((bf16[512,512]{1,0:T(8,128)(2,1)S(1)}, bf16[512,512]{1,0:T(8,128)(2,1)S(1)}, u32[]{:S(2)}, u32[]{:S(2)}) %collective-permute-start.10) | collective-permute-done | bytes 524320 | tf_op jit(solution)/shard_map/ppermute | solution.py:32
  118.2 2.4 %collective-permute-done.11 = bf16[512,512]{1,0:T(8,128)(2,1)S(1)} collective-permute-done((bf16[512,512]{1,0:T(8,128)(2,1)S(1)}, bf16[512,512]{1,0:T(8,128)(2,1)S(1)}, u32[]{:S(2)}, u32[]{:S(2)}) %collective-permute-start.11) | collective-permute-done | bytes 524320 | tf_op jit(solution)/shard_map/ppermute | solution.py:32
  121.3 12.1 %collective-permute-done.12 = bf16[512,512]{1,0:T(8,128)(2,1)} collective-permute-done((bf16[512,512]{1,0:T(8,128)(2,1)S(1)}, bf16[512,512]{1,0:T(8,128)(2,1)}, u32[]{:S(2)}, u32[]{:S(2)}) %collective-permute-start.12) | collective-permute-done | bytes 524320 | tf_op jit(solution)/shard_map/ppermute | solution.py:32
  135.1 3.6 %all-to-all-start.3 = ((bf16[16,96,256]{2,1,0:T(8,128)(2,1)}), bf16[16,96,256]{2,1,0:T(8,128)(2,1)S(1)}, u32[]{:S(2)}, u32[]{:S(2)}) async-start(bf16[16,96,256]{2,1,0:T(8,128)(2,1)} %pad_maximum_fusion.5), calls=%async_computation.3 | async-start | bytes 1572864 | tf_op jit(solution)/shard_map/all_to_all | solution.py:47
  140.1 1.2 constant_dynamic-update-slice_fusion
  141.3 1.3 fusion.13
  142.9 1.4 collective-permute-start.14
  144.3 2.6 %fusion.3 = f32[896,512]{1,0:T(8,128)S(1)} fusion(bf16[1024,1024]{0,1:T(8,128)(2,1)} %collective-permute-done.13, bf16[2048,512]{1,0:T(8,128)(2,1)S(1)} %constant_dynamic-update-slice_fusion), kind=kOutput, calls=%fused_computation.5 | convolution fusion | flops 939524096 | bytes 4718592 | tf_op jit(solution)/shard_map/dot_general | solution.py:11
  146.9 2.0 %add_convert_fusion.1 = bf16[896,512]{1,0:T(8,128)(2,1)} fusion(f32[896,512]{1,0:T(8,128)S(1)} %fusion.3, bf16[1024,1024]{0,1:T(8,128)(2,1)S(1)} %copy-done.3, bf16[2048,512]{1,0:T(8,128)(2,1)S(1)} %constant_dynamic-update-slice_fusion), kind=kOutput, calls=%fused_computation.8 | convolution fusion | flops 940441600 | bytes 5636096 | tf_op jit(solution)/shard_map/dot_general | solution.py:11
  148.9 2.5 %all-to-all-done.3 = bf16[16,96,256]{2,1,0:T(8,128)(2,1)S(1)} async-done(((bf16[16,96,256]{2,1,0:T(8,128)(2,1)}), bf16[16,96,256]{2,1,0:T(8,128)(2,1)S(1)}, u32[]{:S(2)}, u32[]{:S(2)}) %all-to-all-start.3) | async-done | bytes 786464 | tf_op jit(solution)/shard_map/all_to_all | solution.py:47
  152.8 1.1 reshape_reshape.3
  153.9 1.1 constant_dynamic-slice_fusion
  155.1 1.1 pad_maximum_fusion.6
  156.2 7.3 %all-to-all-start.4 = ((bf16[16,64,384]{2,1,0:T(8,128)(2,1)}), bf16[16,64,384]{2,1,0:T(8,128)(2,1)}, u32[]{:S(2)}, u32[]{:S(2)}) async-start(bf16[16,64,384]{2,1,0:T(8,128)(2,1)} %pad_maximum_fusion.6), calls=%async_computation.4 | async-start | bytes 1572864 | tf_op jit(solution)/shard_map/all_to_all | solution.py:47
  163.6 2.5 %fusion.25 = f32[64,1024]{1,0:T(8,128)S(1)} fusion(bf16[1024,1024]{0,1:T(8,128)(2,1)} %collective-permute-done.13, pred[]{:T(512)S(6)} %eq.13, bf16[64,2048]{1,0:T(8,128)(2,1)S(1)} %bitcast.86), kind=kOutput, calls=%fused_computation.59 | convolution fusion | flops 134283264 | bytes 2621441 | tf_op jit(solution)/shard_map/dot_general | solution.py:11
  166.9 1.3 collective-permute-start.15
  169.1 5.7 %collective-permute-done.15 = bf16[32,1024]{1,0:T(8,128)(2,1)S(1)} collective-permute-done((bf16[32,1024]{1,0:T(8,128)(2,1)S(1)}, bf16[32,1024]{1,0:T(8,128)(2,1)S(1)}, u32[]{:S(2)}, u32[]{:S(2)}) %collective-permute-start.15) | collective-permute-done | bytes 65568 | tf_op jit(solution)/shard_map/ppermute | solution.py:32
  175.5 1.4 add_convert_fusion
  178.0 8.3 %all-to-all-done.4 = bf16[16,64,384]{2,1,0:T(8,128)(2,1)} async-done(((bf16[16,64,384]{2,1,0:T(8,128)(2,1)}), bf16[16,64,384]{2,1,0:T(8,128)(2,1)}, u32[]{:S(2)}, u32[]{:S(2)}) %all-to-all-start.4) | async-done | bytes 786464 | tf_op jit(solution)/shard_map/all_to_all | solution.py:47
  186.3 2.6 %fusion.19 = f32[512,256]{1,0:T(8,128)} fusion(bf16[512,1024]{0,1:T(8,128)(2,1)} %bitcast.76, bf16[1024,384]{1,0:T(8,128)(2,1)} %bitcast.29), kind=kOutput, calls=%fused_computation.41 | convolution fusion | flops 268435456 | bytes 2097152 | tf_op jit(solution)/shard_map/dot_general | solution.py:11
  188.9 2.5 %fusion.22 = f32[1024,128]{1,0:T(8,128)} fusion(bf16[1024,1024]{0,1:T(8,128)(2,1)S(1)} %bitcast.69, bf16[1024,384]{1,0:T(8,128)(2,1)} %bitcast.29), kind=kOutput, calls=%fused_computation.50 | convolution fusion | flops 268435456 | bytes 2883584 | tf_op jit(solution)/shard_map/dot_general | solution.py:11
  (86 shorter events, 19.1 us)
Async XLA Ops:
  7.2 46.6 %copy-start = (bf16[512,512]{1,0:T(8,128)(2,1)S(1)}, bf16[512,512]{1,0:T(8,128)(2,1)}, u32[]{:S(2)}) copy-start(bf16[512,512]{1,0:T(8,128)(2,1)} %param.7) | copy-start | bytes 1572868
  7.2 11.3 %copy-start.2 = (bf16[512,1024]{1,0:T(8,128)(2,1)S(1)}, bf16[512,1024]{1,0:T(8,128)(2,1)}, u32[]{:S(2)}) copy-start(bf16[512,1024]{1,0:T(8,128)(2,1)} %param.9) | copy-start | bytes 3145732
  9.3 15.8 %copy-start.9 = (bf16[512,512]{1,0:T(8,128)(2,1)S(1)}, bf16[512,512]{1,0:T(8,128)(2,1)}, u32[]{:S(2)}) copy-start(bf16[512,512]{1,0:T(8,128)(2,1)} %param.8) | copy-start | bytes 1572868
  9.3 39.2 %all-to-all-start = ((bf16[8,128,512]{2,1,0:T(8,128)(2,1)}), bf16[8,128,512]{2,1,0:T(8,128)(2,1)S(1)}, u32[]{:S(2)}, u32[]{:S(2)}) async-start(bf16[8,128,512]{2,1,0:T(8,128)(2,1)} %broadcast_in_dim.15), calls=%async_computation | async-start | bytes 2097152 | tf_op jit(solution)/shard_map/all_to_all | solution.py:47
  19.9 8.5 %collective-permute-start = (bf16[512,256]{1,0:T(8,128)(2,1)S(1)}, bf16[512,256]{1,0:T(8,128)(2,1)}, u32[]{:S(2)}, u32[]{:S(2)}) collective-permute-start(bf16[512,256]{1,0:T(8,128)(2,1)S(1)} %convolution_convert_fusion.4), channel_id=1, source_target_pairs={{0,96},{16,112},{32,0},{48,16},{64,32},{80,48},{96,64},{112,80},{1... | collective-permute-start | bytes 786440 | tf_op jit(solution)/shard_map/ppermute | solution.py:32
  22.7 8.2 %collective-permute-start.1 = (bf16[512,256]{1,0:T(8,128)(2,1)S(1)}, bf16[512,256]{1,0:T(8,128)(2,1)}, u32[]{:S(2)}, u32[]{:S(2)}) collective-permute-start(bf16[512,256]{1,0:T(8,128)(2,1)S(1)} %convolution_convert_fusion.4), channel_id=1, source_target_pairs={{0,64},{16,80},{32,96},{48,112},{64,0},{80,16},{96,32},{112,48},{1... | collective-permute-start | bytes 786440 | tf_op jit(solution)/shard_map/ppermute | solution.py:32
  23.1 15.1 %collective-permute-start.2 = (bf16[512,256]{1,0:T(8,128)(2,1)S(1)}, bf16[512,256]{1,0:T(8,128)(2,1)}, u32[]{:S(2)}, u32[]{:S(2)}) collective-permute-start(bf16[512,256]{1,0:T(8,128)(2,1)S(1)} %convolution_convert_fusion.4), channel_id=1, source_target_pairs={{0,32},{16,48},{32,64},{48,80},{64,96},{80,112},{96,0},{112,16},{1... | collective-permute-start | bytes 786440 | tf_op jit(solution)/shard_map/ppermute | solution.py:32
  23.8 24.7 %collective-permute-start.5 = (bf16[256,1024]{1,0:T(8,128)(2,1)S(1)}, bf16[256,1024]{1,0:T(8,128)(2,1)}, u32[]{:S(2)}, u32[]{:S(2)}) collective-permute-start(bf16[256,1024]{1,0:T(8,128)(2,1)S(1)} %constant_dynamic-slice_fusion.3), channel_id=1, source_target_pairs={{0,128},{128,0},{1,129},{129,1},{2,130},{130,2},{3,131},{131,3},{4... | collective-permute-start | bytes 1572872 | tf_op jit(solution)/shard_map/ppermute | solution.py:32
  25.1 23.4 %collective-permute-start.4 = (bf16[512,512]{1,0:T(8,128)(2,1)S(1)}, bf16[512,512]{1,0:T(8,128)(2,1)}, u32[]{:S(2)}, u32[]{:S(2)}) collective-permute-start(bf16[512,512]{1,0:T(8,128)(2,1)S(1)} %copy-done.9), channel_id=1, source_target_pairs={{0,144},{16,128},{32,176},{48,160},{64,208},{80,192},{96,240},{112... | collective-permute-start | bytes 1572872 | tf_op jit(solution)/shard_map/ppermute | solution.py:32
  39.4 9.0 %collective-permute-start.3 = (bf16[512,256]{1,0:T(8,128)(2,1)S(1)}, bf16[512,256]{1,0:T(8,128)(2,1)S(1)}, u32[]{:S(2)}, u32[]{:S(2)}) collective-permute-start(bf16[512,256]{1,0:T(8,128)(2,1)S(1)} %add_convert_fusion.3), channel_id=1, source_target_pairs={{0,16},{16,0},{32,48},{48,32},{64,80},{80,64},{96,112},{112,96},{1... | collective-permute-start | bytes 786440 | tf_op jit(solution)/shard_map/ppermute | solution.py:32
  48.5 3.8 %collective-permute-start.6 = (bf16[1024,512]{1,0:T(8,128)(2,1)S(1)}, bf16[1024,512]{1,0:T(8,128)(2,1)}, u32[]{:S(2)}, u32[]{:S(2)}) collective-permute-start(bf16[1024,512]{1,0:T(8,128)(2,1)S(1)} %bitcast.73), channel_id=1, source_target_pairs={{0,1},{1,0},{2,3},{3,2},{4,5},{5,4},{6,7},{7,6},{8,9},{9,8},{10,11... | collective-permute-start | bytes 3145736 | tf_op jit(solution)/shard_map/ppermute | solution.py:32
  56.5 5.0 %copy-start.10 = (bf16[1024,256]{1,0:T(8,128)(2,1)S(1)}, bf16[1024,256]{1,0:T(8,128)(2,1)}, u32[]{:S(2)}) copy-start(bf16[1024,256]{1,0:T(8,128)(2,1)} %param.6) | copy-start | bytes 1572868
  56.5 32.9 %all-to-all-start.1 = ((bf16[8,256,512]{2,1,0:T(8,128)(2,1)}), bf16[8,256,512]{2,1,0:T(8,128)(2,1)}, u32[]{:S(2)}, u32[]{:S(2)}) async-start(bf16[8,256,512]{2,1,0:T(8,128)(2,1)} %bitcast.80), calls=%async_computation.1 | async-start | bytes 4194304 | tf_op jit(solution)/shard_map/all_to_all | solution.py:47
  61.4 72.0 %all-gather.2.cloned.1.call-start = ((), (), s32[]{:S(2)}) async-start(), calls=%async_computation.5 | async-start | bytes 2359296 | tf_op jit(solution)/shard_map/all_gather | solution.py:66
  62.3 3.3 %collective-permute-start.7 = (bf16[256,1024]{1,0:T(8,128)(2,1)}, bf16[256,1024]{1,0:T(8,128)(2,1)}, u32[]{:S(2)}, u32[]{:S(2)}) collective-permute-start(bf16[256,1024]{1,0:T(8,128)(2,1)} %collective-permute-done.5), channel_id=1, source_target_pairs={{0,1},{1,0},{2,3},{3,2},{4,5},{5,4},{6,7},{7,6},{8,9},{9,8},{10,11... | collective-permute-start | bytes 1572872 | tf_op jit(solution)/shard_map/ppermute | solution.py:32
  62.9 2.2 %copy-start.8 = (bf16[256,512]{1,0:T(8,128)(2,1)S(1)}, bf16[256,512]{1,0:T(8,128)(2,1)}, u32[]{:S(2)}) copy-start(bf16[256,512]{1,0:T(8,128)(2,1)} %param.5) | copy-start | bytes 786436
  93.2 3.2 %collective-permute-start.8 = (bf16[8,128,256]{2,1,0:T(8,128)(2,1)S(1)}, bf16[8,128,256]{2,1,0:T(8,128)(2,1)S(1)}, u32[]{:S(2)}, u32[]{:S(2)}) collective-permute-start(bf16[8,128,256]{2,1,0:T(8,128)(2,1)S(1)} %fusion.17), channel_id=1, source_target_pairs={{0,1},{1,0},{2,3},{3,2},{4,5},{5,4},{6,7},{7,6},{8,9},{9,8},{10,11... | collective-permute-start | bytes 1572872 | tf_op jit(solution)/shard_map/ppermute | solution.py:32
  94.9 9.5 %collective-permute-start.9 = (bf16[256,512]{1,0:T(8,128)(2,1)S(1)}, bf16[256,512]{1,0:T(8,128)(2,1)}, u32[]{:S(2)}, u32[]{:S(2)}) collective-permute-start(bf16[256,512]{1,0:T(8,128)(2,1)S(1)} %reduce_sum.24), channel_id=1, source_target_pairs={{0,16},{16,0},{32,48},{48,32},{64,80},{80,64},{96,112},{112,96},{1... | collective-permute-start | bytes 786440 | tf_op jit(solution)/shard_map/ppermute | solution.py:32
  97.4 36.0 %all-to-all-start.2 = ((bf16[8,128,256]{2,1,0:T(8,128)(2,1)}), bf16[8,128,256]{2,1,0:T(8,128)(2,1)S(1)}, u32[]{:S(2)}, u32[]{:S(2)}) async-start(bf16[8,128,256]{2,1,0:T(8,128)(2,1)} %fusion.11), calls=%async_computation.2 | async-start | bytes 1048576 | tf_op jit(solution)/shard_map/all_to_all | solution.py:47
  103.5 4.0 %copy-start.1 = (bf16[16,2,32,512]{3,2,1,0:T(8,128)(2,1)S(1)}, bf16[16,2,32,512]{3,2,1,0:T(8,128)(2,1)}, u32[]{:S(2)}) copy-start(bf16[16,2,32,512]{3,2,1,0:T(8,128)(2,1)} %pad_maximum_fusion.1) | copy-start | bytes 3145732
  105.4 4.5 %copy-start.5 = (bf16[512,512]{1,0:T(8,128)(2,1)}, bf16[512,512]{1,0:T(8,128)(2,1)S(1)}, u32[]{:S(2)}) copy-start(bf16[512,512]{1,0:T(8,128)(2,1)S(1)} %pad_maximum_fusion.7) | copy-start | bytes 1572868
  105.4 12.7 %collective-permute-start.10 = (bf16[512,512]{1,0:T(8,128)(2,1)S(1)}, bf16[512,512]{1,0:T(8,128)(2,1)S(1)}, u32[]{:S(2)}, u32[]{:S(2)}) collective-permute-start(bf16[512,512]{1,0:T(8,128)(2,1)S(1)} %pad_maximum_fusion.7), channel_id=1, source_target_pairs={{0,96},{16,112},{32,0},{48,16},{64,32},{80,48},{96,64},{112,80},{1... | collective-permute-start | bytes 1572872 | tf_op jit(solution)/shard_map/ppermute | solution.py:32
  106.7 13.8 %collective-permute-start.11 = (bf16[512,512]{1,0:T(8,128)(2,1)S(1)}, bf16[512,512]{1,0:T(8,128)(2,1)S(1)}, u32[]{:S(2)}, u32[]{:S(2)}) collective-permute-start(bf16[512,512]{1,0:T(8,128)(2,1)S(1)} %pad_maximum_fusion.7), channel_id=1, source_target_pairs={{0,64},{16,80},{32,96},{48,112},{64,0},{80,16},{96,32},{112,48},{1... | collective-permute-start | bytes 1572872 | tf_op jit(solution)/shard_map/ppermute | solution.py:32
  107.3 26.1 %collective-permute-start.12 = (bf16[512,512]{1,0:T(8,128)(2,1)S(1)}, bf16[512,512]{1,0:T(8,128)(2,1)}, u32[]{:S(2)}, u32[]{:S(2)}) collective-permute-start(bf16[512,512]{1,0:T(8,128)(2,1)S(1)} %pad_maximum_fusion.7), channel_id=1, source_target_pairs={{0,32},{16,48},{32,64},{48,80},{64,96},{80,112},{96,0},{112,16},{1... | collective-permute-start | bytes 1572872 | tf_op jit(solution)/shard_map/ppermute | solution.py:32
  118.1 2.4 %copy-start.11 = (bf16[512,512]{1,0:T(8,128)(2,1)}, bf16[512,512]{1,0:T(8,128)(2,1)S(1)}, u32[]{:S(2)}) copy-start(bf16[512,512]{1,0:T(8,128)(2,1)S(1)} %collective-permute-done.10) | copy-start | bytes 1572868
  120.5 0.8 copy-start.13
  133.4 7.9 %collective-permute-start.13 = (bf16[1024,1024]{0,1:T(8,128)(2,1)}, bf16[1024,1024]{0,1:T(8,128)(2,1)}, u32[]{:S(2)}, u32[]{:S(2)}) collective-permute-start(bf16[1024,1024]{0,1:T(8,128)(2,1)} %all-gather.2.cloned.1.call-done), channel_id=1, source_target_pairs={{0,1},{1,0},{2,3},{3,2},{4,5},{5,4},{6,7},{7,6},{8,9},{9,8},{10,11... | collective-permute-start | bytes 6291464 | tf_op jit(solution)/shard_map/ppermute | solution.py:32
  135.1 16.4 %all-to-all-start.3 = ((bf16[16,96,256]{2,1,0:T(8,128)(2,1)}), bf16[16,96,256]{2,1,0:T(8,128)(2,1)S(1)}, u32[]{:S(2)}, u32[]{:S(2)}) async-start(bf16[16,96,256]{2,1,0:T(8,128)(2,1)} %pad_maximum_fusion.5), calls=%async_computation.3 | async-start | bytes 1572864 | tf_op jit(solution)/shard_map/all_to_all | solution.py:47
  138.7 1.0 copy-start.6
  138.7 1.2 copy-start.12
  138.7 1.3 copy-start.14
  140.0 2.5 %copy-start.3 = (bf16[1024,1024]{0,1:T(8,128)(2,1)S(1)}, bf16[1024,1024]{0,1:T(8,128)(2,1)}, u32[]{:S(2)}) copy-start(bf16[1024,1024]{0,1:T(8,128)(2,1)} %all-gather.2.cloned.1.call-done) | copy-start | bytes 6291460
  142.9 9.3 %collective-permute-start.14 = (bf16[128,512]{1,0:T(8,128)(2,1)S(1)}, bf16[128,512]{1,0:T(8,128)(2,1)}, u32[]{:S(2)}, u32[]{:S(2)}) collective-permute-start(bf16[128,512]{1,0:T(8,128)(2,1)S(1)} %fusion.10), channel_id=1, source_target_pairs={{0,128},{128,0},{1,129},{129,1},{2,130},{130,2},{3,131},{131,3},{4... | collective-permute-start | bytes 393224 | tf_op jit(solution)/shard_map/ppermute | solution.py:32
  152.2 23.3 %collective-permute-start.16 = (bf16[896,512]{1,0:T(8,128)(2,1)}, bf16[896,512]{1,0:T(8,128)(2,1)}, u32[]{:S(2)}, u32[]{:S(2)}) collective-permute-start(bf16[896,512]{1,0:T(8,128)(2,1)} %add_convert_fusion.1), channel_id=1, source_target_pairs={{0,128},{128,0},{1,129},{129,1},{2,130},{130,2},{3,131},{131,3},{4... | collective-permute-start | bytes 2752520 | tf_op jit(solution)/shard_map/ppermute | solution.py:32
  156.2 30.1 %all-to-all-start.4 = ((bf16[16,64,384]{2,1,0:T(8,128)(2,1)}), bf16[16,64,384]{2,1,0:T(8,128)(2,1)}, u32[]{:S(2)}, u32[]{:S(2)}) async-start(bf16[16,64,384]{2,1,0:T(8,128)(2,1)} %pad_maximum_fusion.6), calls=%async_computation.4 | async-start | bytes 1572864 | tf_op jit(solution)/shard_map/all_to_all | solution.py:47
  163.5 2.6 %copy-start.4 = (bf16[1024,1024]{0,1:T(8,128)(2,1)S(1)}, bf16[1024,1024]{0,1:T(8,128)(2,1)}, u32[]{:S(2)}) copy-start(bf16[1024,1024]{0,1:T(8,128)(2,1)} %all-gather.2.cloned.1.call-done) | copy-start | bytes 6291460
  166.1 9.4 %copy-start.7 = (bf16[896,512]{1,0:T(8,128)(2,1)S(1)}, bf16[896,512]{1,0:T(8,128)(2,1)}, u32[]{:S(2)}) copy-start(bf16[896,512]{1,0:T(8,128)(2,1)} %add_convert_fusion.1) | copy-start | bytes 2752516
  166.9 8.0 %collective-permute-start.15 = (bf16[32,1024]{1,0:T(8,128)(2,1)S(1)}, bf16[32,1024]{1,0:T(8,128)(2,1)S(1)}, u32[]{:S(2)}, u32[]{:S(2)}) collective-permute-start(bf16[32,1024]{1,0:T(8,128)(2,1)S(1)} %constant_dynamic-slice_fusion.2), channel_id=1, source_target_pairs={{0,128},{128,0},{1,129},{129,1},{2,130},{130,2},{3,131},{131,3},{4... | collective-permute-start | bytes 196616 | tf_op jit(solution)/shard_map/ppermute | solution.py:32
Sparse Core Ops, SparseCore 0:
  64.0 52.2 all-gather.1
